TPU v7x, 256 devices: a whole 4x4x8 slice. The times are simulated.
256 devices in a mesh: grp: 4 (over x), kv: 64 (over y, z, core).
Axes of the slice: x: 4, y: 4, z: 8, core: 2. Of those that a mesh axis runs over, the one named last changes fastest.
Arguments:
- query_lat: bfloat16 [32, 128, 512], P('grp', 'kv'), may hold values from -122.91343 to 122.91343
- query_rope: bfloat16 [32, 128, 64], P('grp', 'kv'), may hold values from -6 to 6
- cache_lat: bfloat16 [32, 16384, 512], P('grp', 'kv'), may hold values from -6 to 6
- cache_rope: bfloat16 [32, 64, 16384], P('grp', None, 'kv'), may hold values from -6 to 6
- lengths: int32 [32], P('grp'), may hold values from 2048 to 16384, as said below
- w_value: bfloat16 [128, 512, 128], P('kv'), may hold values from -12 to 12
- w_out: bfloat16 [16384, 7168], P('kv'), may hold values from -0.125 to 0.125
- moe_tokens: bfloat16 [32, 7168], P('grp', 'kv'), may hold values from -6 to 6
- expert_ids: int32 [32, 8], P('grp'), may hold values from 0 to 31, all different within a row; in each aligned block of 8 rows (0 to 7, 8 to 15, ...) at most 4 rows name the same one
- route_weights: float32 [32, 8], P('grp'), may hold values from 0.1 to 1
- w_gate: bfloat16 [7168, 32768], P(None, ('grp', 'kv')), may hold values from -0.0625 to 0.0625
- w_up: bfloat16 [7168, 32768], P(None, ('grp', 'kv')), may hold values from -0.0625 to 0.0625
- w_down: bfloat16 [32768, 7168], P(('grp', 'kv')), may hold values from -0.75 to 0.75
Outputs:
- attn_out: bfloat16 [32, 7168], P('grp', 'kv')
- moe_out: bfloat16 [32, 7168], P('grp', 'kv')
Inputs may be any that keep to these rules, and one draw needn't show every extreme that they name: `lengths`: in every group of 8 consecutive requests one has length 16384. `expert_ids`: each row names 8 different experts; among the 8 rows of one group no expert is named by more than 4 rows, and some expert of some group is named by exactly 4.
All inputs are finite; a program needn't handle non-finite values.
Results may differ from a plain program's by a relative error of at most 0.015.
Values may be sent and summed in bfloat16 or wider, within the bound.
No kernel may reach another device: no remote copies, remote signals or barrier semaphores. Data moves between devices by JAX's collectives and lax.ppermute only.
A program may use at most 64 MiB of HBM per device.

v0:
```python
import jax
import jax.numpy as jnp
from jax import lax
from jax.sharding import PartitionSpec as P

FF = 1024
CAP = 4


def shards(
    query_lat,
    query_rope,
    cache_lat,
    cache_rope,
    lengths,
    w_value,
    w_out,
    moe_tokens,
    expert_ids,
    route_weights,
    w_gate,
    w_up,
    w_down,
):
    shard_count = lax.axis_size("kv")
    shard_index = lax.axis_index("kv")
    group_count = lax.axis_size("grp")
    full_lat, full_rope = (
        lax.all_gather(query_lat, "kv", axis=1, tiled=True),
        lax.all_gather(query_rope, "kv", axis=1, tiled=True),
    )
    request_count = cache_lat.shape[0]
    positions = cache_lat.shape[1]
    head_total = full_lat.shape[1]
    head_share = head_total // shard_count
    latent_width = cache_lat.shape[2]
    score_scale = (w_value.shape[2] + full_rope.shape[2]) ** (-0.5)
    scores = (
        jnp.einsum("rhl,rtl->rht", full_lat, cache_lat, preferred_element_type=jnp.float32)
        + jnp.einsum("rhe,ret->rht", full_rope, cache_rope, preferred_element_type=jnp.float32)
    ) * score_scale
    position = shard_index * positions + lax.iota(jnp.int32, positions)
    usable = position[None, None, :] < lengths[:, None, None]
    scores = jnp.where(usable, scores, -1e30)
    maxima = jnp.max(scores, axis=2)
    weights = jnp.where(usable, jnp.exp(scores - maxima[:, :, None]), 0.0)
    totals = jnp.sum(weights, axis=2)
    weighted = jnp.einsum(
        "rht,rtl->rhl", weights.astype(jnp.bfloat16), cache_lat, preferred_element_type=jnp.float32
    )
    partial_value = (weighted / jnp.maximum(totals, 1.0)[:, :, None]).astype(jnp.bfloat16)
    split_part = partial_value.reshape(request_count, shard_count, head_share, latent_width)
    split_max = maxima.reshape(request_count, shard_count, head_share)
    split_tot = totals.reshape(request_count, shard_count, head_share)
    got_part = lax.all_to_all(split_part, "kv", split_axis=1, concat_axis=1, tiled=True)
    got_max, got_tot = (
        lax.all_to_all(split_max, "kv", split_axis=1, concat_axis=1, tiled=True),
        lax.all_to_all(split_tot, "kv", split_axis=1, concat_axis=1, tiled=True),
    )
    global_max = jnp.max(got_max, axis=1, keepdims=True)
    scale_b = got_tot * jnp.exp(got_max - global_max)
    numerator = jnp.sum(got_part.astype(jnp.float32) * scale_b[:, :, :, None], axis=1)
    denominator = jnp.sum(scale_b, axis=1)
    merged = (numerator / denominator[:, :, None]).astype(jnp.bfloat16)
    head_values = jnp.einsum(
        "rhl,hlv->rhv", merged, w_value, preferred_element_type=jnp.float32
    ).astype(jnp.bfloat16)
    partial_out = jnp.dot(
        head_values.reshape(request_count, -1), w_out, preferred_element_type=jnp.float32
    )
    attn_out = lax.psum_scatter(partial_out, "kv", scatter_dimension=1, tiled=True).astype(
        jnp.bfloat16
    )
    token_rows = lax.all_gather(moe_tokens, "kv", axis=1, tiled=True)
    units_here = w_gate.shape[1]
    shard_span = FF // units_here
    expert_count = group_count * shard_count * units_here // FF
    numbers = lax.iota(jnp.int32, expert_count)
    picked = expert_ids[:, :, None] == numbers[None, None, :]
    chosen_now = jnp.sum(picked.astype(jnp.int32), axis=1)
    slot_rank = jnp.cumsum(chosen_now, axis=0) - chosen_now
    coefficient = jnp.sum(jnp.where(picked, route_weights[:, :, None], 0.0), axis=1)
    dest_expert = (lax.iota(jnp.int32, group_count) * shard_count + shard_index) // shard_span
    selector = dest_expert[:, None] == numbers[None, :]
    chosen_dest = jnp.sum(jnp.where(selector[:, None, :], chosen_now[None, :, :], 0), axis=2)
    rank_dest = jnp.sum(jnp.where(selector[:, None, :], slot_rank[None, :, :], 0), axis=2)
    weight_dest = jnp.sum(jnp.where(selector[:, None, :], coefficient[None, :, :], 0.0), axis=2)
    slot_ids = lax.iota(jnp.int32, CAP)
    placing = (chosen_dest[:, None, :] == 1) & (rank_dest[:, None, :] == slot_ids[None, :, None])
    send_rows = jnp.einsum(
        "gct,td->gcd", placing.astype(jnp.bfloat16), token_rows, preferred_element_type=jnp.float32
    ).astype(jnp.bfloat16)
    arrived = lax.all_to_all(send_rows, "grp", split_axis=0, concat_axis=0, tiled=True)
    gate_proj = jnp.einsum("gcd,du->gcu", arrived, w_gate, preferred_element_type=jnp.float32)
    up_proj = jnp.einsum("gcd,du->gcu", arrived, w_up, preferred_element_type=jnp.float32)
    hidden = (jax.nn.silu(gate_proj) * up_proj).astype(jnp.bfloat16)
    expert_out = jnp.einsum("gcu,ud->gcd", hidden, w_down, preferred_element_type=jnp.float32)
    returned = lax.all_to_all(
        expert_out.astype(jnp.bfloat16), "grp", split_axis=0, concat_axis=0, tiled=True
    ).astype(expert_out.dtype)
    mixing = jnp.where(placing, weight_dest[:, None, :], 0.0)
    combined = jnp.einsum("gct,gcd->td", mixing, returned, preferred_element_type=jnp.float32)
    moe_out = lax.psum_scatter(combined, "kv", scatter_dimension=1, tiled=True).astype(jnp.bfloat16)
    return (attn_out, moe_out)


def solution(mesh):
    return jax.shard_map(
        shards,
        mesh=mesh,
        in_specs=(
            P("grp", "kv", None),
            P("grp", "kv", None),
            P("grp", "kv", None),
            P("grp", None, "kv"),
            P("grp"),
            P("kv", None, None),
            P("kv", None),
            P("grp", "kv"),
            P("grp", None),
            P("grp", None),
            P(None, ("grp", "kv")),
            P(None, ("grp", "kv")),
            P(("grp", "kv"), None),
        ),
        out_specs=(P("grp", "kv"), P("grp", "kv")),
        check_vma=False,
    )
```

profile of v0, /device:TPU:1, one launch (start us, length us, event | category | flops | bytes accessed | tf_op | source)
XLA Modules:
  0.0 464.5 jit_solution(3405354478071212989)
XLA Ops:
  7.2 1.5 copy.69
  9.6 54.3 %all-gather = bf16[64,112,8]{1,2,0:T(8,128)(2,1)S(1)} all-gather(bf16[1,112,8]{1,2,0:T(8,128)(2,1)} %bitcast.46), channel_id=1, replica_groups=mesh['grp'=4,'kv'=64] {'kv'}, dimensions={0}, use_global_device_ids=true | all-gather | bytes 116480 | tf_op jit(solution)/shard_map/all_gather | solution.py:74
  65.3 4.0 all-to-all-start.3
  70.0 43.4 %all_gather.10 = bf16[8,128,64]{2,0,1:T(8,128)(2,1)S(1)} all-gather(bf16[8,2,64]{2,0,1:T(8,128)(2,1)S(1)} %copy.71), channel_id=1, replica_groups=mesh['grp'=4,'kv'=64] {'kv'}, dimensions={1}, use_global_device_ids=true | all-gather | bytes 133120 | tf_op jit(solution)/shard_map/all_gather | solution.py:30
  113.4 2.3 fusion.21
  115.7 2.0 fusion.3
  117.8 1.9 fusion.10
  120.9 4.5 all-to-all-start.4
  125.4 2.5 fusion.38
  129.0 2.1 all-to-all-done.4
  131.1 7.4 %all-to-all-start.1 = ((f32[8,64,2]{0,2,1:T(2,128)}), f32[8,64,2]{0,2,1:T(2,128)S(1)}, u32[]{:S(2)}, u32[]{:S(2)}) async-start(f32[8,64,2]{0,2,1:T(2,128)} %bitcast), calls=%async_computation.1 | async-start | bytes 131072 | tf_op jit(solution)/shard_map/all_to_all | solution.py:58
  139.2 9.1 %all-to-all-done.1 = f32[8,64,2]{0,2,1:T(2,128)S(1)} async-done(((f32[8,64,2]{0,2,1:T(2,128)}), f32[8,64,2]{0,2,1:T(2,128)S(1)}, u32[]{:S(2)}, u32[]{:S(2)}) %all-to-all-start.1) | async-done | bytes 4128 | tf_op jit(solution)/shard_map/all_to_all | solution.py:58
  148.3 4.4 all-to-all-start.2
  152.7 1.6 divide_convert_fusion
  154.3 1.5 reshape.112
  155.8 2.1 copy.73
  157.9 4.7 %all-to-all-done.2 = f32[8,64,2]{0,2,1:T(2,128)S(1)} async-done(((f32[8,64,2]{0,2,1:T(2,128)}), f32[8,64,2]{0,2,1:T(2,128)S(1)}, u32[]{:S(2)}, u32[]{:S(2)}) %all-to-all-start.2) | async-done | bytes 4128 | tf_op jit(solution)/shard_map/all_to_all | solution.py:57
  162.6 5.7 %all-to-all-start = ((bf16[8,64,2,512]{3,2,0,1:T(2,128)(2,1)}), bf16[8,64,2,512]{3,2,0,1:T(2,128)(2,1)S(1)}, u32[]{:S(2)}, u32[]{:S(2)}) async-start(bf16[8,64,2,512]{3,2,0,1:T(2,128)(2,1)} %copy.73), calls=%async_computation | async-start | bytes 2097152 | tf_op jit(solution)/shard_map/all_to_all | solution.py:55
  168.6 2.7 convolution_bitcast_fusion
  171.8 25.1 %all-to-all-done = bf16[8,64,2,512]{3,2,0,1:T(2,128)(2,1)S(1)} async-done(((bf16[8,64,2,512]{3,2,0,1:T(2,128)(2,1)}), bf16[8,64,2,512]{3,2,0,1:T(2,128)(2,1)S(1)}, u32[]{:S(2)}, u32[]{:S(2)}) %all-to-all-start) | async-done | bytes 1048608 | tf_op jit(solution)/shard_map/all_to_all | solution.py:55
  198.3 5.6 %convolution_bitcast_fusion.1 = f32[7168,8]{1,0:T(8,128)} fusion(bf16[256,7168]{1,0:T(8,128)(2,1)} %param.19, bf16[2,512,128]{2,1,0:T(8,128)(2,1)} %param.18, f32[8,2,512]{2,1,0:T(2,128)S(1)} %multiply_reduce_fusion, f32[8,2]{0,1:T(2,128)S(1)} %get-tuple-element.4), kind=kOutput, calls=%fused_computation.1 | convolution fusion | flops 31475712 | bytes 4194368
  203.9 106.7 %reduce-scatter.9.cloned.1.call-done = f32[112,8]{1,0:T(8,128)} async-done(((f32[7168,8]{1,0:T(8,128)}), f32[112,8]{1,0:T(8,128)}) %reduce-scatter.9.cloned.1.call-update) | async-done | bytes 3600
  310.6 1.5 copy.88
  312.0 144.4 %reduce-scatter.7.cloned.1.call-done = f32[112,8]{1,0:T(8,128)} async-done(((f32[7168,8]{1,0:T(8,128)}), f32[112,8]{1,0:T(8,128)}) %reduce-scatter.7.cloned.1.call-update) | async-done | bytes 3600
  (45 shorter events, 9.6 us)
Async XLA Ops:
  7.2 118.2 %copy-start = (bf16[8,256,512]{2,1,0:T(8,128)(2,1)S(1)}, bf16[8,256,512]{2,1,0:T(8,128)(2,1)}, u32[]{:S(2)}) copy-start(bf16[8,256,512]{2,1,0:T(8,128)(2,1)} %param.15) | copy-start | bytes 6291460
  7.2 108.5 %copy-start.4 = (s32[8]{0:T(128)S(1)}, s32[8]{0:T(128)}, u32[]{:S(2)}) copy-start(s32[8]{0:T(128)} %param.17) | copy-start | bytes 100
  7.2 118.2 %all-gather.3.cloned.1.call-start = ((), (), s32[]{:S(2)}) async-start(), calls=%async_computation.7 | async-start | bytes 1064960 | tf_op jit(solution)/shard_map/all_gather | solution.py:29
  65.3 50.4 %all-to-all-start.3 = ((bf16[4,4,7168]{2,1,0:T(4,128)(2,1)}), bf16[4,4,7168]{2,1,0:T(4,128)(2,1)S(1)}, u32[]{:S(2)}, u32[]{:S(2)}) async-start(bf16[4,4,7168]{2,1,0:T(4,128)(2,1)} %convolution_convert_fusion.1), calls=%async_computation.3 | async-start | bytes 458752 | tf_op jit(solution)/shard_map/all_to_all | solution.py:93
  115.7 4.0 copy-start.1
  120.9 10.2 %all-to-all-start.4 = ((bf16[4,4,7168]{2,1,0:T(4,128)(2,1)}), bf16[4,4,7168]{2,1,0:T(4,128)(2,1)S(1)}, u32[]{:S(2)}, u32[]{:S(2)}) async-start(bf16[4,4,7168]{2,1,0:T(4,128)(2,1)} %copy.83), calls=%async_computation.4 | async-start | bytes 458752 | tf_op jit(solution)/shard_map/all_to_all | solution.py:98
  131.1 17.2 %all-to-all-start.1 = ((f32[8,64,2]{0,2,1:T(2,128)}), f32[8,64,2]{0,2,1:T(2,128)S(1)}, u32[]{:S(2)}, u32[]{:S(2)}) async-start(f32[8,64,2]{0,2,1:T(2,128)} %bitcast), calls=%async_computation.1 | async-start | bytes 131072 | tf_op jit(solution)/shard_map/all_to_all | solution.py:58
  148.3 14.3 %all-to-all-start.2 = ((f32[8,64,2]{0,2,1:T(2,128)}), f32[8,64,2]{0,2,1:T(2,128)S(1)}, u32[]{:S(2)}, u32[]{:S(2)}) async-start(f32[8,64,2]{0,2,1:T(2,128)} %bitcast.43), calls=%async_computation.2 | async-start | bytes 131072 | tf_op jit(solution)/shard_map/all_to_all | solution.py:57
  155.8 12.6 %copy-start.2 = (s32[8,8]{1,0:T(8,128)S(1)}, s32[8,8]{1,0:T(8,128)}, u32[]{:S(2)}) copy-start(s32[8,8]{1,0:T(8,128)} %param.21) | copy-start | bytes 772
  155.8 12.6 %copy-start.3 = (f32[8,8]{1,0:T(8,128)S(1)}, f32[8,8]{1,0:T(8,128)}, u32[]{:S(2)}) copy-start(f32[8,8]{1,0:T(8,128)} %param.22) | copy-start | bytes 772
  162.6 34.3 %all-to-all-start = ((bf16[8,64,2,512]{3,2,0,1:T(2,128)(2,1)}), bf16[8,64,2,512]{3,2,0,1:T(2,128)(2,1)S(1)}, u32[]{:S(2)}, u32[]{:S(2)}) async-start(bf16[8,64,2,512]{3,2,0,1:T(2,128)(2,1)} %copy.73), calls=%async_computation | async-start | bytes 2097152 | tf_op jit(solution)/shard_map/all_to_all | solution.py:55
  168.4 142.2 %reduce-scatter.9.cloned.1.call-start = ((), (), s32[]{:S(2)}) async-start(), calls=%async_computation.9 | async-start | bytes 3727360
  171.4 285.1 %reduce-scatter.7.cloned.1.call-start = ((), (), s32[]{:S(2)}) async-start(), calls=%async_computation.8 | async-start | bytes 3727360
Sparse Core Ops, SparseCore 0:
  10.8 80.6 all-gather.2
  173.4 137.1 reduce-scatter.8
  315.3 141.1 reduce-scatter.6
where the time goes:
time: 470 us; the launch traced here: 464 us
  waiting for transfers between devices  292 us (62%)
  blocking collectives  97.7 us (21%)
  starting transfers between devices  26.4 us (6%)
  matrix products  19.8 us (4%)
  between operations  13.9 us (3%)
  local copies, waits for them, and re-layouts  11.3 us (2%)
    unnamed x5, waiting for transfers between devices  251 us
    all_gather x1, blocking collectives, shards(): token_rows = lax.all_gather(moe_tokens, 'kv', axis=1, tiled=True)  54.3 us
    all_gather x1, blocking collectives, shards(): lax.all_gather(query_rope, 'kv', axis=1, tiled=True)  43.4 us
    all_to_all x1, waiting for transfers between devices, shards(): lax.all_to_all(split_part, 'kv', split_axis=1, concat_axis=1, tiled=True)  25.1 us
  transfers between devices with their start and end apart: 8, of which 6 were waited for; matrix products, arithmetic and copies ran while one was open for 7% of the time, Pallas kernels for 0%

commit v1 on v0

v1 whole, which is shorter than its diff:
```python
import jax
import jax.numpy as jnp
from jax import lax
from jax.experimental import pallas as pl
from jax.experimental.pallas import tpu as pltpu
from jax.sharding import Mesh
from jax.sharding import PartitionSpec as P

FF = 1024
F32 = jnp.float32
BF16 = jnp.bfloat16
LANES = 128


def three_terms(value):
    high = value.astype(BF16).astype(F32)
    rest = value - high
    middle = rest.astype(BF16).astype(F32)
    return high, middle, rest - middle


def attention_kernel(
    info, query, lat_own, lat_far, rope_own, rope_far, out, query_rows, out_rows, *, scale
):
    request = pl.program_id(0)
    peers, chunk, width = query.shape
    latent = lat_own.shape[2]
    rope = rope_own.shape[1]
    requests = pl.num_programs(0)
    rows = peers * chunk // 8

    @pl.when(request == 0)
    def _():
        for tile in range(width // LANES):
            piece = query[:, :, tile * LANES : (tile + 1) * LANES].astype(F32)
            query_rows[tile] = piece.reshape(peers * chunk, LANES)

    mine = jnp.concatenate(
        [query_rows[tile, pl.ds(request, rows, stride=8), :] for tile in range(width // LANES)],
        axis=1,
    ).astype(BF16)
    length = info[request]
    parts = []
    for lat, rot, base in (
        (lat_own, rope_own, info[requests]),
        (lat_far, rope_far, info[requests + 1]),
    ):
        score = (
            lax.dot_general(
                mine[:, :latent],
                lat[0],
                (((1,), (1,)), ((), ())),
                preferred_element_type=F32,
            )
            + jnp.dot(mine[:, latent : latent + rope], rot[0], preferred_element_type=F32)
        ) * scale
        usable = base + lax.broadcasted_iota(jnp.int32, score.shape, 1) < length
        parts.append((jnp.where(usable, score, -1e30), usable, lat))
    top = jnp.maximum(
        jnp.max(parts[0][0], axis=1, keepdims=True), jnp.max(parts[1][0], axis=1, keepdims=True)
    )
    total = jnp.zeros_like(top)
    weighted = jnp.zeros((rows, latent), F32)
    for score, usable, lat in parts:
        weight = jnp.where(usable, jnp.exp(score - top), 0.0)
        total += jnp.sum(weight, axis=1, keepdims=True)
        weighted += jnp.dot(weight.astype(BF16), lat[0], preferred_element_type=F32)
    partial = weighted / jnp.maximum(total, 1.0)
    lane = lax.broadcasted_iota(jnp.int32, (rows, LANES), 1)
    stats = jnp.zeros((rows, LANES), F32)
    for place, term in enumerate(three_terms(top) + three_terms(total)):
        stats = jnp.where(lane == place, term, stats)
    tiles = latent // LANES
    for tile in range(tiles):
        out_rows[tile, pl.ds(request, rows, stride=8), :] = partial[
            :, tile * LANES : (tile + 1) * LANES
        ]
    out_rows[tiles, pl.ds(request, rows, stride=8), :] = stats

    @pl.when(request == requests - 1)
    def _():
        for tile in range(tiles + 1):
            out[:, tile * chunk : (tile + 1) * chunk, :] = (
                out_rows[tile].reshape(peers, chunk, LANES).astype(BF16)
            )


def attention(info, query, lat_own, lat_far, rope_own, rope_far, scale):
    peers, chunk, width = query.shape
    requests, positions, latent = lat_own.shape
    rope = rope_own.shape[1]
    lat_spec = pl.BlockSpec((1, positions, latent), lambda r: (r, 0, 0))
    rope_spec = pl.BlockSpec((1, rope, positions), lambda r: (r, 0, 0))
    out_shape = (peers, (latent // LANES + 1) * chunk, LANES)
    return pl.pallas_call(
        lambda *refs: attention_kernel(*refs, scale=scale),
        out_shape=jax.ShapeDtypeStruct(out_shape, BF16),
        grid=(requests,),
        in_specs=[
            pl.BlockSpec(memory_space=pltpu.SMEM),
            pl.BlockSpec((peers, chunk, width), lambda r: (0, 0, 0)),
            lat_spec,
            lat_spec,
            rope_spec,
            rope_spec,
        ],
        out_specs=pl.BlockSpec(out_shape, lambda r: (0, 0, 0)),
        scratch_shapes=[
            pltpu.VMEM((width // LANES, peers * chunk, LANES), F32),
            pltpu.VMEM((latent // LANES + 1, peers * chunk, LANES), F32),
        ],
        compiler_params=pltpu.CompilerParams(vmem_limit_bytes=20 * 2**20),
        cost_estimate=pl.CostEstimate(
            flops=2 * peers * chunk * 2 * positions * (2 * latent + rope),
            bytes_accessed=6 * 2**20,
            transcendentals=peers * chunk * 2 * positions,
        ),
        name="attention",
    )(info, query, lat_own, lat_far, rope_own, rope_far)


def experts_kernel(own, one, two, three, swapped, weight, gate, up, down, out, rows_ref):
    peers, chunk, _ = own.shape
    span = gate.shape[0] // (2 * peers)
    half = span // 2
    first = LANES - 64
    core = weight[0:1, LANES - 1 :] > 0.0
    near = (own, one, two, three)
    for peer in range(peers):
        for block in range(4):
            mine = near[block][peer].astype(F32)
            theirs = swapped[block, peer].astype(F32)
            pieces = []
            for side in (mine, theirs):
                pieces.append(
                    jnp.concatenate(
                        [side[:8, first : first + half], side[8:, first : first + half]], axis=1
                    )
                )
            even = jnp.where(core, pieces[1], pieces[0])
            odd = jnp.where(core, pieces[0], pieces[1])
            begin = 2 * peer * span
            rows_ref[8 * block : 8 * block + 8, begin : begin + 2 * span] = jnp.concatenate(
                [even, odd], axis=1
            )
    tokens = rows_ref[...].astype(BF16)
    gate_proj = jnp.dot(tokens, gate[...], preferred_element_type=F32)
    up_proj = jnp.dot(tokens, up[...], preferred_element_type=F32)
    hidden = (gate_proj * jax.nn.sigmoid(gate_proj) * up_proj).astype(BF16)
    share = weight[:, 0:1]
    width = down.shape[1]
    step = 1024
    for start in range(0, width, step):
        result = jnp.dot(hidden, down[:, start : start + step], preferred_element_type=F32) * share
        for block in range(4):
            out[block, :, start : start + step] = result[8 * block : 8 * block + 8].astype(BF16)


def experts(near, swapped, weight, gate, up, down):
    depth, units = gate.shape
    width = down.shape[1]
    return pl.pallas_call(
        experts_kernel,
        out_shape=jax.ShapeDtypeStruct((4, 8, width), BF16),
        in_specs=[pl.BlockSpec(memory_space=pltpu.VMEM)] * 9,
        out_specs=pl.BlockSpec(memory_space=pltpu.VMEM),
        scratch_shapes=[pltpu.VMEM((32, depth), F32)],
        compiler_params=pltpu.CompilerParams(vmem_limit_bytes=20 * 2**20),
        cost_estimate=pl.CostEstimate(
            flops=2 * 32 * 3 * depth * units, bytes_accessed=8 * 2**20, transcendentals=0
        ),
        name="experts",
    )(*near, swapped, weight, gate, up, down)


def merge_kernel(got, value, project, moe_own, moe_one, moe_two, moe_three, out):
    peers, height, _ = got.shape
    chunk = 16
    tiles = height // chunk - 1
    stats = got[:, tiles * chunk :, :].astype(F32)
    top = stats[:, :, 0:1] + stats[:, :, 1:2] + stats[:, :, 2:3]
    total = stats[:, :, 3:4] + stats[:, :, 4:5] + stats[:, :, 5:6]
    peak = jnp.max(top, axis=0, keepdims=True)
    share = total * jnp.exp(top - peak)
    denominator = jnp.sum(share, axis=0)
    columns = []
    for tile in range(tiles):
        piece = got[:, tile * chunk : (tile + 1) * chunk, :].astype(F32)
        columns.append(jnp.sum(piece * share, axis=0) / denominator)
    merged = jnp.concatenate(columns, axis=1)
    heads = []
    for head in range(2):
        rows = merged[8 * head : 8 * head + 8].astype(BF16)
        heads.append(jnp.dot(rows, value[head], preferred_element_type=F32))
    head_values = jnp.concatenate(heads, axis=1).astype(BF16)
    attended = jnp.dot(head_values, project[...], preferred_element_type=F32)
    routed = (
        moe_own[...].astype(F32)
        + moe_one[...].astype(F32)
        + moe_two[...].astype(F32)
        + moe_three[...].astype(F32)
    )
    both = jnp.concatenate([attended, routed], axis=0)
    count, _, span = out.shape
    for place in range(count):
        out[place] = both[:, place * span : (place + 1) * span].astype(BF16)


def merge(got, value, project, moe, count):
    width = project.shape[1]
    return pl.pallas_call(
        merge_kernel,
        out_shape=jax.ShapeDtypeStruct((count, 16, width // count), BF16),
        in_specs=[pl.BlockSpec(memory_space=pltpu.VMEM)] * 7,
        out_specs=pl.BlockSpec(memory_space=pltpu.VMEM),
        compiler_params=pltpu.CompilerParams(vmem_limit_bytes=20 * 2**20),
        cost_estimate=pl.CostEstimate(
            flops=2 * 8 * project.shape[0] * width, bytes_accessed=6 * 2**20, transcendentals=0
        ),
        name="merge",
    )(got, value, project, *moe)


def shards(
    query_lat,
    query_rope,
    cache_lat,
    cache_rope,
    lengths,
    w_value,
    w_out,
    moe_tokens,
    expert_ids,
    route_weights,
    w_gate,
    w_up,
    w_down,
):
    plane = ("y", "z")
    kv = ("y", "z", "c")
    shard_count = lax.axis_size(kv)
    shard_index = lax.axis_index(kv)
    core = lax.axis_index("c")
    group_count = lax.axis_size("x")
    peers = lax.axis_size(plane)
    requests, positions, latent = cache_lat.shape
    head_share = query_lat.shape[1]
    rope = query_rope.shape[2]
    span = moe_tokens.shape[1]
    swap = [(0, 1), (1, 0)]

    def along_x(value, shift):
        return lax.ppermute(
            value, "x", [(i, (i + shift) % group_count) for i in range(group_count)]
        )

    halves = moe_tokens.reshape(requests, head_share, span // head_share)
    spare = -(latent + rope + span // head_share) % LANES
    payload = jnp.concatenate(
        [query_lat, query_rope, halves, jnp.zeros((requests, head_share, spare), BF16)], axis=2
    )
    payload = payload.transpose(1, 0, 2).reshape(1, head_share * requests, -1)
    payload = jnp.broadcast_to(payload, (peers,) + payload.shape[1:])
    query = lax.all_to_all(payload, plane, 0, 0, tiled=True)
    lat_far = lax.ppermute(cache_lat, "c", swap)
    rope_far = lax.ppermute(cache_rope, "c", swap)

    expert_count = group_count * shard_count * w_gate.shape[1] // FF
    numbers = lax.iota(jnp.int32, expert_count)
    picked = expert_ids[:, :, None] == numbers[None, None, :]
    coefficient = jnp.sum(jnp.where(picked, route_weights[:, :, None], 0.0), axis=1)
    coefficients = [coefficient] + [along_x(coefficient, d) for d in range(1, group_count)]
    here = (lax.axis_index("x") * shard_count + shard_index) * w_gate.shape[1] // FF
    weight = jnp.sum(
        jnp.where(numbers == here, jnp.concatenate(coefficients, axis=0), 0.0),
        axis=1,
        keepdims=True,
    )
    weight = jnp.broadcast_to(weight, (group_count * requests, LANES))
    weight = jnp.where(lax.iota(jnp.int32, LANES) == LANES - 1, core.astype(F32), weight)

    info = jnp.concatenate(
        [lengths, jnp.stack([shard_index * positions, (shard_index + 1 - 2 * core) * positions])]
    )
    scale = (w_value.shape[2] + rope) ** (-0.5)
    raw = query[:, :, latent:]
    near = [raw] + [along_x(raw, d) for d in range(1, group_count)]
    part = attention(info, query, cache_lat, lat_far, cache_rope, rope_far, scale)
    got = lax.all_to_all(part, plane, 0, 0, tiled=True)

    swapped = lax.ppermute(jnp.stack(near), "c", swap)
    routed = experts(near, swapped, weight, w_gate, w_up, w_down)
    moe = [routed[0]] + [along_x(routed[d], -d) for d in range(1, group_count)]

    terms = merge(got, w_value, w_out, moe, shard_count)
    arrived = lax.all_to_all(terms, kv, 0, 0, tiled=True)
    summed = jnp.sum(arrived.astype(F32), axis=0).astype(BF16)
    return (summed[:requests], summed[requests:])


def solution(mesh):
    groups = mesh.shape["grp"]
    split = Mesh(mesh.devices.reshape(groups, 4, 8, 2), ("x", "y", "z", "c"))
    kv = ("y", "z", "c")
    both = ("x",) + kv
    return jax.shard_map(
        shards,
        mesh=split,
        in_specs=(
            P("x", kv, None),
            P("x", kv, None),
            P("x", kv, None),
            P("x", None, kv),
            P("x"),
            P(kv, None, None),
            P(kv, None),
            P("x", kv),
            P("x", None),
            P("x", None),
            P(None, both),
            P(None, both),
            P(both, None),
        ),
        out_specs=(P("x", kv), P("x", kv)),
        check_vma=False,
    )
```

time: 470 us -> 114 us (0.24); the launches traced: 464 us -> 113 us
  waiting for transfers between devices: 292 us -> 29.8 us
  blocking collectives: 97.7 us -> 22.5 us
  matrix products: 19.8 us -> 0 us
  between operations: 13.9 us -> 0.82 us
  Pallas kernels: 0 us -> 10.7 us
  starting transfers between devices: 26.4 us -> 35.9 us
    unnamed x5 -> x0, waiting for transfers between devices: 251 us -> none
    all_gather x2 -> x0, blocking collectives: 97.7 us -> none  [the longest x1 54.3 us: shards(): token_rows = lax.all_gather(moe_tokens, 'kv', axis=1, tiled=True)]
    all_to_all x0 -> x1, blocking collectives: none -> 22.5 us  [shards(): arrived = lax.all_to_all(terms, kv, 0, 0, tiled=True)]
    all_to_all x5 -> x2, waiting for transfers between devices: 40.9 us -> 20.3 us  [the longest x1 15.3 us: shards(): query = lax.all_to_all(payload, plane, 0, 0, tiled=True)]
    ppermute x0 -> x12, starting transfers between devices: none -> 18.3 us  [the longest x9 10.5 us: along_x(): lax.ppermute(value, 'x', [(i, (i + shift) % group_count) for i in range(g...]
    dot_general x8 -> x0, matrix products: 14.3 us -> none  [the longest x1 2.7 us: shards(): jnp.einsum('gct,gcd->td', mixing, returned, preferred_element_type=jnp.fl...]
    pallas_call x0 -> x3, Pallas kernels: none -> 10.7 us  [the longest x1 7.07 us: attention(): pl.pallas_call(lambda *refs: attention_kernel(*refs, scale=scale), out_sh...]
    ppermute x0 -> x12, waiting for transfers between devices: none -> 9.44 us  [the longest x9 7.91 us: along_x(): lax.ppermute(value, 'x', [(i, (i + shift) % group_count) for i in range(g...]
  transfers between devices with their start and end apart: 8 -> 14, of which waited for: 6 -> 7; matrix products, arithmetic and copies ran while one was open for 7% -> 1% of each run, Pallas kernels for 0% -> 2%
where the time goes in v1:
time: 114 us; the launch traced here: 113 us
  starting transfers between devices  35.9 us (31%)
  waiting for transfers between devices  29.8 us (26%)
  blocking collectives  22.5 us (20%)
  local copies, waits for them, and re-layouts  12.2 us (11%)
  Pallas kernels  10.7 us (9%)
  other arithmetic  1.39 us (1%)
    all_to_all x1, blocking collectives, shards(): arrived = lax.all_to_all(terms, kv, 0, 0, tiled=True)  22.5 us
    all_to_all x1, waiting for transfers between devices, shards(): query = lax.all_to_all(payload, plane, 0, 0, tiled=True)  15.3 us
    all_to_all x1, starting transfers between devices, shards(): query = lax.all_to_all(payload, plane, 0, 0, tiled=True)  12 us
    ppermute x9, starting transfers between devices, along_x(): lax.ppermute(value, 'x', [(i, (i + shift) % group_count) for i in range(g...  10.5 us
    unnamed x28, local copies, waits for them, and re-layouts  9.78 us
    ppermute x9, waiting for transfers between devices, along_x(): lax.ppermute(value, 'x', [(i, (i + shift) % group_count) for i in range(g...  7.91 us
    pallas_call x1, Pallas kernels, attention(): pl.pallas_call(lambda *refs: attention_kernel(*refs, scale=scale), out_sh...  7.07 us
    ppermute x1, starting transfers between devices, shards(): swapped = lax.ppermute(jnp.stack(near), 'c', swap)  6.73 us
  transfers between devices with their start and end apart: 14, of which 7 were waited for; matrix products, arithmetic and copies ran while one was open for 1% of the time, Pallas kernels for 2%

profile of v1, /device:TPU:1, one launch (start us, length us, event | category | flops | bytes accessed | tf_op | source)
XLA Modules:
  0.0 113.3 jit_solution(4618947478106533370)
XLA Ops:
  3.0 0.9 broadcast_in_dim.49
  3.9 12.0 %all-to-all-start = ((bf16[32,16,640]{2,1,0:T(8,128)(2,1)}), bf16[32,16,640]{2,1,0:T(8,128)(2,1)S(1)}, u32[]{:S(2)}, u32[]{:S(2)}) async-start(bf16[32,16,640]{2,1,0:T(8,128)(2,1)} %broadcast_in_dim.49), calls=%async_computation | async-start | bytes 1310720 | tf_op jit(solution)/shard_map/all_to_all | solution.py:264
  16.0 1.0 collective-permute-start
  17.0 15.3 %all-to-all-done.refs_1_ = bf16[32,16,640]{2,1,0:T(8,128)(2,1)S(1)} async-done(((bf16[32,16,640]{2,1,0:T(8,128)(2,1)}), bf16[32,16,640]{2,1,0:T(8,128)(2,1)S(1)}, u32[]{:S(2)}, u32[]{:S(2)}) %all-to-all-start) | async-done | bytes 655392 | tf_op jit(solution)/shard_map/all_to_all | solution.py:264
  32.4 1.3 %collective-permute-start.2 = (bf16[32,16,128]{2,1,0:T(8,128)(2,1)S(1)}, bf16[32,16,128]{2,1,0:T(8,128)(2,1)S(1)}, u32[]{:S(2)}, u32[]{:S(2)}) collective-permute-start(bf16[32,16,128]{2,1,0:T(8,128)(2,1)S(1)} %get-tuple-element.3.own), channel_id=1, source_target_pairs={{0,64},{64,128},{128,192},{192,0},{1,65},{65,129},{129,193},{193,1... | collective-permute-start | bytes 393224 | tf_op jit(solution)/shard_map/ppermute | solution.py:253
  33.7 2.5 %collective-permute-start.3 = (bf16[32,16,128]{2,1,0:T(8,128)(2,1)S(1)}, bf16[32,16,128]{2,1,0:T(8,128)(2,1)S(1)}, u32[]{:S(2)}, u32[]{:S(2)}) collective-permute-start(bf16[32,16,128]{2,1,0:T(8,128)(2,1)S(1)} %get-tuple-element.3.own), channel_id=1, source_target_pairs={{0,128},{64,192},{128,0},{192,64},{1,129},{65,193},{129,1},{193,65... | collective-permute-start | bytes 393224 | tf_op jit(solution)/shard_map/ppermute | solution.py:253
  36.1 1.2 %collective-permute-start.4 = (bf16[32,16,128]{2,1,0:T(8,128)(2,1)S(1)}, bf16[32,16,128]{2,1,0:T(8,128)(2,1)S(1)}, u32[]{:S(2)}, u32[]{:S(2)}) collective-permute-start(bf16[32,16,128]{2,1,0:T(8,128)(2,1)S(1)} %get-tuple-element.3.own), channel_id=1, source_target_pairs={{0,192},{64,0},{128,64},{192,128},{1,193},{65,1},{129,65},{193,129... | collective-permute-start | bytes 393224 | tf_op jit(solution)/shard_map/ppermute | solution.py:253
  37.5 2.0 %collective-permute-start.7 = (f32[8,32]{1,0:T(8,128)S(1)}, f32[8,32]{1,0:T(8,128)S(1)}, u32[]{:S(2)}, u32[]{:S(2)}) collective-permute-start(f32[8,32]{1,0:T(8,128)S(1)} %select_reduce_fusion), channel_id=1, source_target_pairs={{0,128},{64,192},{128,0},{192,64},{1,129},{65,193},{129,1},{193,65... | collective-permute-start | bytes 3080 | tf_op jit(solution)/shard_map/ppermute | solution.py:253
  41.2 6.7 %collective-permute-start.5 = (bf16[4,32,16,128]{3,2,1,0:T(8,128)(2,1)}, bf16[4,32,16,128]{3,2,1,0:T(8,128)(2,1)}, u32[]{:S(2)}, u32[]{:S(2)}) collective-permute-start(bf16[4,32,16,128]{3,2,1,0:T(8,128)(2,1)} %pad_maximum_fusion), channel_id=1, source_target_pairs={{0,1},{1,0},{2,3},{3,2},{4,5},{5,4},{6,7},{7,6},{8,9},{9,8},{10,11... | collective-permute-start | bytes 1572872 | tf_op jit(solution)/shard_map/ppermute | solution.py:291
  48.3 1.5 %collective-permute-done.5.swapped = bf16[4,32,16,128]{3,2,1,0:T(8,128)(2,1)} collective-permute-done((bf16[4,32,16,128]{3,2,1,0:T(8,128)(2,1)}, bf16[4,32,16,128]{3,2,1,0:T(8,128)(2,1)}, u32[]{:S(2)}, u32[]{:S(2)}) %collective-permute-start.5) | collective-permute-done | bytes 524320 | tf_op jit(solution)/shard_map/ppermute | solution.py:291
  49.8 1.5 %copy-done.2 = bf16[7168,128]{1,0:T(8,128)(2,1)S(1)} copy-done((bf16[7168,128]{1,0:T(8,128)(2,1)S(1)}, bf16[7168,128]{1,0:T(8,128)(2,1)}, u32[]{:S(2)}) %copy-start.2) | copy-done | bytes 1835032
  51.3 1.5 %copy-done.3 = bf16[7168,128]{1,0:T(8,128)(2,1)S(1)} copy-done((bf16[7168,128]{1,0:T(8,128)(2,1)S(1)}, bf16[7168,128]{1,0:T(8,128)(2,1)}, u32[]{:S(2)}) %copy-start.3) | copy-done | bytes 1835032
  52.8 1.5 %copy-done.4 = bf16[128,7168]{1,0:T(8,128)(2,1)S(1)} copy-done((bf16[128,7168]{1,0:T(8,128)(2,1)S(1)}, bf16[128,7168]{1,0:T(8,128)(2,1)}, u32[]{:S(2)}) %copy-start.4) | copy-done | bytes 1835032
  56.1 2.5 %experts.1 = bf16[4,8,7168]{2,1,0:T(8,128)(2,1)S(1)} custom-call(bf16[32,16,128]{2,1,0:T(8,128)(2,1)S(1)} %get-tuple-element.3.own, bf16[32,16,128]{2,1,0:T(8,128)(2,1)S(1)} %collective-permute-done.2.one, bf16[32,16,128]{2,1,0:T(8,128)(2,1)S(1)} %copy-done.6, bf16[32,16,128]{2,1,0:T(8,128)(2,1)S(1)} %copy-done.8, ...), custom_call_target="tpu_custom_call" | custom-call | flops 176160768 | bytes 8388608 | tf_op jit(solution)/shard_map/experts/pallas_call | solution.py:162
  58.6 7.1 %attention.1 = bf16[32,80,128]{2,1,0:T(8,128)(2,1)} custom-call(s32[10]{0:T(128)S(1)} %pad_add_fusion.refs_0_, bf16[32,16,640]{2,1,0:T(8,128)(2,1)S(1)} %all-to-all-done.refs_1_, bf16[8,256,512]{2,1,0:T(8,128)(2,1)S(1)} %copy-done.1, bf16[8,256,512]{2,1,0:T(8,128)(2,1)S(1)} %collective-permute-done.refs_3_, bf16[8,64,256]{2,1,0:T(8,128)(2,1)} %refs_4_.1, ...), custom_call_target="tpu_custom_call" | custom-call | flops 570425344 | bytes 6291456 | tf_op jit(solution)/shard_map/attention/pallas_call | solution.py:95
  65.7 5.6 %all-to-all-start.1 = ((bf16[32,80,128]{2,1,0:T(8,128)(2,1)}), bf16[32,80,128]{2,1,0:T(8,128)(2,1)S(1)}, u32[]{:S(2)}, u32[]{:S(2)}) async-start(bf16[32,80,128]{2,1,0:T(8,128)(2,1)} %attention.1), calls=%async_computation.1 | async-start | bytes 1310720 | tf_op jit(solution)/shard_map/all_to_all | solution.py:289
  71.3 2.4 %collective-permute-start.9 = (bf16[8,7168]{1,0:T(8,128)(2,1)S(1)}, bf16[8,7168]{1,0:T(8,128)(2,1)S(1)}, u32[]{:S(2)}, u32[]{:S(2)}) collective-permute-start(bf16[8,7168]{1,0:T(8,128)(2,1)S(1)} %get-tuple-element.6), channel_id=1, source_target_pairs={{0,192},{64,0},{128,64},{192,128},{1,193},{65,1},{129,65},{193,129... | collective-permute-start | bytes 344072 | tf_op jit(solution)/shard_map/ppermute | solution.py:253
  74.4 2.9 %collective-permute-done.9.moe_one = bf16[8,7168]{1,0:T(8,128)(2,1)S(1)} collective-permute-done((bf16[8,7168]{1,0:T(8,128)(2,1)S(1)}, bf16[8,7168]{1,0:T(8,128)(2,1)S(1)}, u32[]{:S(2)}, u32[]{:S(2)}) %collective-permute-start.9) | collective-permute-done | bytes 114720 | tf_op jit(solution)/shard_map/ppermute | solution.py:253
  77.2 1.7 %collective-permute-done.10.moe_two = bf16[8,7168]{1,0:T(8,128)(2,1)S(1)} collective-permute-done((bf16[8,7168]{1,0:T(8,128)(2,1)S(1)}, bf16[8,7168]{1,0:T(8,128)(2,1)S(1)}, u32[]{:S(2)}, u32[]{:S(2)}) %collective-permute-start.10) | collective-permute-done | bytes 114720 | tf_op jit(solution)/shard_map/ppermute | solution.py:253
  78.9 3.0 %collective-permute-done.11.moe_three = bf16[8,7168]{1,0:T(8,128)(2,1)S(1)} collective-permute-done((bf16[8,7168]{1,0:T(8,128)(2,1)S(1)}, bf16[8,7168]{1,0:T(8,128)(2,1)S(1)}, u32[]{:S(2)}, u32[]{:S(2)}) %collective-permute-start.11) | collective-permute-done | bytes 114720 | tf_op jit(solution)/shard_map/ppermute | solution.py:253
  81.9 5.0 %all-to-all-done.1.got = bf16[32,80,128]{2,1,0:T(8,128)(2,1)S(1)} async-done(((bf16[32,80,128]{2,1,0:T(8,128)(2,1)}), bf16[32,80,128]{2,1,0:T(8,128)(2,1)S(1)}, u32[]{:S(2)}, u32[]{:S(2)}) %all-to-all-start.1) | async-done | bytes 655392 | tf_op jit(solution)/shard_map/all_to_all | solution.py:289
  87.0 2.0 %copy-done = bf16[256,7168]{1,0:T(8,128)(2,1)S(1)} copy-done((bf16[256,7168]{1,0:T(8,128)(2,1)S(1)}, bf16[256,7168]{1,0:T(8,128)(2,1)}, u32[]{:S(2)}) %copy-start) | copy-done | bytes 3670040
  89.0 1.1 merge.1
  90.1 22.5 %all_to_all.15 = bf16[64,16,112]{2,1,0:T(8,128)(2,1)S(1)} all-to-all(bf16[64,16,112]{2,1,0:T(8,128)(2,1)S(1)} %merge.1), channel_id=1, replica_groups=mesh['x'=4,'y'=4,'z'=8,'c'=2] {'y','z','c'}, dimensions={0} | all-to-all | bytes 458752 | tf_op jit(solution)/shard_map/all_to_all | solution.py:296
  (53 shorter events, 7.7 us)
Async XLA Ops:
  0.6 36.7 %copy-start.10 = (f32[8,8]{1,0:T(8,128)S(1)}, f32[8,8]{1,0:T(8,128)}, u32[]{:S(2)}) copy-start(f32[8,8]{1,0:T(8,128)} %param.22) | copy-start | bytes 772
  0.6 36.7 %copy-start.11 = (s32[8,8]{1,0:T(8,128)S(1)}, s32[8,8]{1,0:T(8,128)}, u32[]{:S(2)}) copy-start(s32[8,8]{1,0:T(8,128)} %param.21) | copy-start | bytes 772
  0.7 47.3 %copy-start.12 = (s32[8]{0:T(128)S(1)}, s32[8]{0:T(128)}, u32[]{:S(2)}) copy-start(s32[8]{0:T(128)} %param.17) | copy-start | bytes 100
  3.9 28.4 %all-to-all-start = ((bf16[32,16,640]{2,1,0:T(8,128)(2,1)}), bf16[32,16,640]{2,1,0:T(8,128)(2,1)S(1)}, u32[]{:S(2)}, u32[]{:S(2)}) async-start(bf16[32,16,640]{2,1,0:T(8,128)(2,1)} %broadcast_in_dim.49), calls=%async_computation | async-start | bytes 1310720 | tf_op jit(solution)/shard_map/all_to_all | solution.py:264
  16.0 42.6 %collective-permute-start = (bf16[8,256,512]{2,1,0:T(8,128)(2,1)}, bf16[8,256,512]{2,1,0:T(8,128)(2,1)S(1)}, u32[]{:S(2)}, u32[]{:S(2)}) collective-permute-start(bf16[8,256,512]{2,1,0:T(8,128)(2,1)} %refs_2_.1), channel_id=1, source_target_pairs={{0,1},{1,0},{2,3},{3,2},{4,5},{5,4},{6,7},{7,6},{8,9},{9,8},{10,11... | collective-permute-start | bytes 6291464 | tf_op jit(solution)/shard_map/ppermute | solution.py:265
  32.4 5.1 %collective-permute-start.2 = (bf16[32,16,128]{2,1,0:T(8,128)(2,1)S(1)}, bf16[32,16,128]{2,1,0:T(8,128)(2,1)S(1)}, u32[]{:S(2)}, u32[]{:S(2)}) collective-permute-start(bf16[32,16,128]{2,1,0:T(8,128)(2,1)S(1)} %get-tuple-element.3.own), channel_id=1, source_target_pairs={{0,64},{64,128},{128,192},{192,0},{1,65},{65,129},{129,193},{193,1... | collective-permute-start | bytes 393224 | tf_op jit(solution)/shard_map/ppermute | solution.py:253
  33.7 6.2 %collective-permute-start.3 = (bf16[32,16,128]{2,1,0:T(8,128)(2,1)S(1)}, bf16[32,16,128]{2,1,0:T(8,128)(2,1)S(1)}, u32[]{:S(2)}, u32[]{:S(2)}) collective-permute-start(bf16[32,16,128]{2,1,0:T(8,128)(2,1)S(1)} %get-tuple-element.3.own), channel_id=1, source_target_pairs={{0,128},{64,192},{128,0},{192,64},{1,129},{65,193},{129,1},{193,65... | collective-permute-start | bytes 393224 | tf_op jit(solution)/shard_map/ppermute | solution.py:253
  36.1 4.2 %collective-permute-start.4 = (bf16[32,16,128]{2,1,0:T(8,128)(2,1)S(1)}, bf16[32,16,128]{2,1,0:T(8,128)(2,1)S(1)}, u32[]{:S(2)}, u32[]{:S(2)}) collective-permute-start(bf16[32,16,128]{2,1,0:T(8,128)(2,1)S(1)} %get-tuple-element.3.own), channel_id=1, source_target_pairs={{0,192},{64,0},{128,64},{192,128},{1,193},{65,1},{129,65},{193,129... | collective-permute-start | bytes 393224 | tf_op jit(solution)/shard_map/ppermute | solution.py:253
  37.4 10.6 %collective-permute-start.8 = (f32[8,32]{1,0:T(8,128)S(1)}, f32[8,32]{1,0:T(8,128)S(1)}, u32[]{:S(2)}, u32[]{:S(2)}) collective-permute-start(f32[8,32]{1,0:T(8,128)S(1)} %select_reduce_fusion), channel_id=1, source_target_pairs={{0,192},{64,0},{128,64},{192,128},{1,193},{65,1},{129,65},{193,129... | collective-permute-start | bytes 3080 | tf_op jit(solution)/shard_map/ppermute | solution.py:253
  37.5 10.5 %collective-permute-start.7 = (f32[8,32]{1,0:T(8,128)S(1)}, f32[8,32]{1,0:T(8,128)S(1)}, u32[]{:S(2)}, u32[]{:S(2)}) collective-permute-start(f32[8,32]{1,0:T(8,128)S(1)} %select_reduce_fusion), channel_id=1, source_target_pairs={{0,128},{64,192},{128,0},{192,64},{1,129},{65,193},{129,1},{193,65... | collective-permute-start | bytes 3080 | tf_op jit(solution)/shard_map/ppermute | solution.py:253
  39.9 8.4 %copy-start.5 = (bf16[32,16,128]{2,1,0:T(8,128)(2,1)}, bf16[32,16,128]{2,1,0:T(8,128)(2,1)S(1)}, u32[]{:S(2)}) copy-start(bf16[32,16,128]{2,1,0:T(8,128)(2,1)S(1)} %collective-permute-done.3.two) | copy-start | bytes 393220
  39.9 8.2 %collective-permute-start.6 = (f32[8,32]{1,0:T(8,128)S(1)}, f32[8,32]{1,0:T(8,128)S(1)}, u32[]{:S(2)}, u32[]{:S(2)}) collective-permute-start(f32[8,32]{1,0:T(8,128)S(1)} %select_reduce_fusion), channel_id=1, source_target_pairs={{0,64},{64,128},{128,192},{192,0},{1,65},{65,129},{129,193},{193,1... | collective-permute-start | bytes 3080 | tf_op jit(solution)/shard_map/ppermute | solution.py:253
  40.3 7.9 %copy-start.7 = (bf16[32,16,128]{2,1,0:T(8,128)(2,1)}, bf16[32,16,128]{2,1,0:T(8,128)(2,1)S(1)}, u32[]{:S(2)}) copy-start(bf16[32,16,128]{2,1,0:T(8,128)(2,1)S(1)} %collective-permute-done.4.three) | copy-start | bytes 393220
  41.2 8.6 %collective-permute-start.5 = (bf16[4,32,16,128]{3,2,1,0:T(8,128)(2,1)}, bf16[4,32,16,128]{3,2,1,0:T(8,128)(2,1)}, u32[]{:S(2)}, u32[]{:S(2)}) collective-permute-start(bf16[4,32,16,128]{3,2,1,0:T(8,128)(2,1)} %pad_maximum_fusion), channel_id=1, source_target_pairs={{0,1},{1,0},{2,3},{3,2},{4,5},{5,4},{6,7},{7,6},{8,9},{9,8},{10,11... | collective-permute-start | bytes 1572872 | tf_op jit(solution)/shard_map/ppermute | solution.py:291
  48.0 10.6 %collective-permute-start.1 = (bf16[8,64,256]{2,1,0:T(8,128)(2,1)}, bf16[8,64,256]{2,1,0:T(8,128)(2,1)S(1)}, u32[]{:S(2)}, u32[]{:S(2)}) collective-permute-start(bf16[8,64,256]{2,1,0:T(8,128)(2,1)} %refs_4_.1), channel_id=1, source_target_pairs={{0,1},{1,0},{2,3},{3,2},{4,5},{5,4},{6,7},{7,6},{8,9},{9,8},{10,11... | collective-permute-start | bytes 786440 | tf_op jit(solution)/shard_map/ppermute | solution.py:266
  48.3 10.3 %copy-start.1 = (bf16[8,256,512]{2,1,0:T(8,128)(2,1)S(1)}, bf16[8,256,512]{2,1,0:T(8,128)(2,1)}, u32[]{:S(2)}) copy-start(bf16[8,256,512]{2,1,0:T(8,128)(2,1)} %refs_2_.1) | copy-start | bytes 6291460
  49.8 1.5 %copy-start.2 = (bf16[7168,128]{1,0:T(8,128)(2,1)S(1)}, bf16[7168,128]{1,0:T(8,128)(2,1)}, u32[]{:S(2)}) copy-start(bf16[7168,128]{1,0:T(8,128)(2,1)} %gate.1) | copy-start | bytes 5505028
  51.3 1.5 %copy-start.3 = (bf16[7168,128]{1,0:T(8,128)(2,1)S(1)}, bf16[7168,128]{1,0:T(8,128)(2,1)}, u32[]{:S(2)}) copy-start(bf16[7168,128]{1,0:T(8,128)(2,1)} %up.1) | copy-start | bytes 5505028
  65.7 21.3 %copy-start.9 = (bf16[2,512,128]{2,1,0:T(8,128)(2,1)S(1)}, bf16[2,512,128]{2,1,0:T(8,128)(2,1)}, u32[]{:S(2)}) copy-start(bf16[2,512,128]{2,1,0:T(8,128)(2,1)} %value.1) | copy-start | bytes 786436
  65.7 21.3 %all-to-all-start.1 = ((bf16[32,80,128]{2,1,0:T(8,128)(2,1)}), bf16[32,80,128]{2,1,0:T(8,128)(2,1)S(1)}, u32[]{:S(2)}, u32[]{:S(2)}) async-start(bf16[32,80,128]{2,1,0:T(8,128)(2,1)} %attention.1), calls=%async_computation.1 | async-start | bytes 1310720 | tf_op jit(solution)/shard_map/all_to_all | solution.py:289
  71.3 5.9 %collective-permute-start.9 = (bf16[8,7168]{1,0:T(8,128)(2,1)S(1)}, bf16[8,7168]{1,0:T(8,128)(2,1)S(1)}, u32[]{:S(2)}, u32[]{:S(2)}) collective-permute-start(bf16[8,7168]{1,0:T(8,128)(2,1)S(1)} %get-tuple-element.6), channel_id=1, source_target_pairs={{0,192},{64,0},{128,64},{192,128},{1,193},{65,1},{129,65},{193,129... | collective-permute-start | bytes 344072 | tf_op jit(solution)/shard_map/ppermute | solution.py:253
  73.7 5.3 %collective-permute-start.10 = (bf16[8,7168]{1,0:T(8,128)(2,1)S(1)}, bf16[8,7168]{1,0:T(8,128)(2,1)S(1)}, u32[]{:S(2)}, u32[]{:S(2)}) collective-permute-start(bf16[8,7168]{1,0:T(8,128)(2,1)S(1)} %get-tuple-element.5), channel_id=1, source_target_pairs={{0,128},{64,192},{128,0},{192,64},{1,129},{65,193},{129,1},{193,65... | collective-permute-start | bytes 344072 | tf_op jit(solution)/shard_map/ppermute | solution.py:253
  73.7 8.3 %collective-permute-start.11 = (bf16[8,7168]{1,0:T(8,128)(2,1)S(1)}, bf16[8,7168]{1,0:T(8,128)(2,1)S(1)}, u32[]{:S(2)}, u32[]{:S(2)}) collective-permute-start(bf16[8,7168]{1,0:T(8,128)(2,1)S(1)} %get-tuple-element.4), channel_id=1, source_target_pairs={{0,64},{64,128},{128,192},{192,0},{1,65},{65,129},{129,193},{193,1... | collective-permute-start | bytes 344072 | tf_op jit(solution)/shard_map/ppermute | solution.py:253
  87.0 2.0 %copy-start = (bf16[256,7168]{1,0:T(8,128)(2,1)S(1)}, bf16[256,7168]{1,0:T(8,128)(2,1)}, u32[]{:S(2)}) copy-start(bf16[256,7168]{1,0:T(8,128)(2,1)} %project.1) | copy-start | bytes 11010052
  (3 other events, 3.3 us)

commit v2 on v0

v2 whole, which is shorter than its diff:
```python
import jax
import jax.numpy as jnp
from jax import lax
from jax.experimental import pallas as pl
from jax.experimental.pallas import tpu as pltpu
from jax.sharding import Mesh
from jax.sharding import PartitionSpec as P

FF = 1024
CAP = 4
ROWS = 8
F32 = jnp.float32
BF16 = jnp.bfloat16
LANES = 128
KV = ("y", "z", "c")
VMEM = pl.BlockSpec(memory_space=pltpu.VMEM)
SMEM = pl.BlockSpec(memory_space=pltpu.SMEM)
HBM = pl.BlockSpec(memory_space=pltpu.HBM)


def three_terms(value):
    high = value.astype(BF16).astype(F32)
    rest = value - high
    middle = rest.astype(BF16).astype(F32)
    return high, middle, rest - middle


def params(mebibytes):
    return pltpu.CompilerParams(vmem_limit_bytes=mebibytes * 2**20)


def payload_kernel(query_lat, query_rope, tokens, out):
    peers = out.shape[0]
    latent, rope = query_lat.shape[2], query_rope.shape[2]
    heads = query_lat.shape[1]
    half = tokens.shape[1] // heads
    lat = query_lat[...].astype(F32)
    rot = query_rope[...].astype(F32)
    tok = tokens[...].astype(F32)
    spare = jnp.zeros((ROWS, out.shape[2] - latent - rope - half), F32)
    rows = []
    for head in range(heads):
        tail = jnp.concatenate(
            [rot[:, head, :], tok[:, head * half : (head + 1) * half], spare], axis=1
        )
        rows.append(jnp.concatenate([lat[:, head, :], tail], axis=1))
    chunk = jnp.concatenate(rows, axis=0).astype(BF16)
    for peer in range(peers):
        out[peer] = chunk


def payload(query_lat, query_rope, tokens, peers):
    requests, heads, latent = query_lat.shape
    return pl.pallas_call(
        payload_kernel,
        out_shape=jax.ShapeDtypeStruct((peers, heads * requests, latent + LANES), BF16),
        in_specs=[VMEM] * 3,
        out_specs=VMEM,
        compiler_params=params(20),
        name="payload",
    )(query_lat, query_rope, tokens)


def attention_kernel(
    lengths,
    query,
    lat_own,
    lat_far,
    rope_own,
    rope_far,
    ids,
    route,
    out,
    send_0,
    send_1,
    send_2,
    send_3,
    mix_out,
    query_rows,
    out_rows,
    stat_rows,
    token_rows,
    *,
    scale,
    units,
):
    peers, chunk, width = query.shape
    requests, positions, latent = lat_own.shape
    rope = rope_own.shape[1]
    tiles = latent // LANES
    heads = chunk // requests
    group, groups = lax.axis_index("x"), lax.axis_size("x")
    shard, shards_here = lax.axis_index(KV), lax.axis_size(KV)
    core = lax.axis_index("c")
    rows = peers * heads

    for tile in range(tiles + 1):
        piece = query[:, :, tile * LANES : (tile + 1) * LANES].astype(F32)
        query_rows[tile] = piece.reshape(peers * chunk, LANES)

    lane = lax.broadcasted_iota(jnp.int32, (rows, LANES), 1)
    stats = jnp.zeros((rows, LANES), F32)
    base_own = shard * positions
    base_far = (shard + 1 - 2 * core) * positions
    place = lax.broadcasted_iota(jnp.int32, (rows, positions), 1)
    for request in range(requests):
        mine = jnp.concatenate(
            [
                jnp.concatenate(
                    [
                        query_rows[tile, pl.ds(requests * head + request, peers, stride=chunk), :]
                        for tile in range(tiles + 1)
                    ],
                    axis=1,
                )
                for head in range(heads)
            ],
            axis=0,
        ).astype(BF16)
        length = lengths[request]
        parts = []
        for lat, rot, base in ((lat_own, rope_own, base_own), (lat_far, rope_far, base_far)):
            score = (
                lax.dot_general(
                    mine[:, :latent],
                    lat[request],
                    (((1,), (1,)), ((), ())),
                    preferred_element_type=F32,
                )
                + jnp.dot(
                    mine[:, latent : latent + rope], rot[request], preferred_element_type=F32
                )
            ) * scale
            usable = place < length - base
            parts.append((jnp.where(usable, score, -1e30), usable, lat))
        top = jnp.max(jnp.maximum(parts[0][0], parts[1][0]), axis=1, keepdims=True)
        weights = [jnp.where(usable, jnp.exp(score - top), 0.0) for score, usable, _ in parts]
        total = jnp.sum(weights[0] + weights[1], axis=1, keepdims=True)
        weighted = jnp.dot(
            weights[0].astype(BF16), lat_own[request], preferred_element_type=F32
        ) + jnp.dot(weights[1].astype(BF16), lat_far[request], preferred_element_type=F32)
        partial = weighted / jnp.maximum(total, 1.0)
        for index, term in enumerate(three_terms(top) + three_terms(total)):
            stats = jnp.where(lane == ROWS * request + index, term, stats)
        for head in range(heads):
            for tile in range(tiles):
                out_rows[tile, pl.ds(requests * head + request, peers, stride=chunk), :] = partial[
                    peers * head : peers * (head + 1), tile * LANES : (tile + 1) * LANES
                ]

    for tile in range(tiles):
        out[:, tile * chunk : (tile + 1) * chunk, :] = (
            out_rows[tile].reshape(peers, chunk, LANES).astype(BF16)
        )
    stat_rows[...] = jnp.zeros_like(stat_rows)
    for head in range(heads):
        stat_rows[pl.ds(head, peers, stride=ROWS), :] = stats[peers * head : peers * (head + 1)]
    out[:, tiles * chunk :, :] = stat_rows[...].reshape(peers, ROWS, LANES).astype(BF16)

    half = token_rows.shape[1] // (peers * heads)
    for peer in range(peers):
        begin = peer * chunk
        pieces = [
            query_rows[tiles, begin + requests * head : begin + requests * (head + 1), :][
                :, rope : rope + half
            ]
            for head in range(heads)
        ]
        token_rows[:, peer * heads * half : (peer + 1) * heads * half] = jnp.concatenate(
            pieces, axis=1
        )
    tokens = token_rows[...].astype(BF16)
    named = ids[...]
    strength = route[...]
    lower = (
        lax.broadcasted_iota(jnp.int32, (ROWS, ROWS), 1)
        < lax.broadcasted_iota(jnp.int32, (ROWS, ROWS), 0)
    ).astype(F32)
    slot_lane = lax.broadcasted_iota(jnp.int32, (ROWS, LANES), 1)
    placing = jnp.zeros((ROWS, LANES), F32)
    mix = jnp.zeros((ROWS, LANES), F32)
    for step in range(4):
        expert = (lax.rem(group + step, groups) * shards_here + shard) * units // FF
        hit = named == expert
        chosen = jnp.max(jnp.where(hit, 1.0, 0.0), axis=1, keepdims=True)
        weight = jnp.sum(jnp.where(hit, strength, 0.0), axis=1, keepdims=True)
        chosen_wide = jnp.broadcast_to(chosen, (ROWS, LANES))
        rank = jnp.dot(lower, chosen_wide, preferred_element_type=F32)
        picked = (rank == (slot_lane - CAP * step).astype(F32)) & (chosen_wide > 0.0)
        picked = picked & (slot_lane >= CAP * step) & (slot_lane < CAP * (step + 1))
        placing = jnp.where(picked, 1.0, placing)
        mix = jnp.where(picked, weight, mix)
    mix_out[...] = mix
    select = placing.T[: 4 * CAP, :].astype(BF16)
    chosen_rows = jnp.dot(select, tokens, preferred_element_type=F32).astype(BF16)
    for step, send in enumerate((send_0, send_1, send_2, send_3)):
        send[...] = chosen_rows[CAP * step : CAP * (step + 1)]


def attention(lengths, query, lat_own, lat_far, rope_own, rope_far, ids, route, scale, span, units):
    peers, chunk, width = query.shape
    requests, positions, latent = lat_own.shape
    rope = rope_own.shape[1]
    tiles = latent // LANES
    return pl.pallas_call(
        lambda *refs: attention_kernel(*refs, scale=scale, units=units),
        out_shape=[jax.ShapeDtypeStruct((peers, tiles * chunk + ROWS, LANES), BF16)]
        + [jax.ShapeDtypeStruct((CAP, peers * span), BF16)] * 4
        + [jax.ShapeDtypeStruct((ROWS, LANES), F32)],
        in_specs=[SMEM] + [VMEM] * 7,
        out_specs=[VMEM] * 6,
        scratch_shapes=[
            pltpu.VMEM((width // LANES, peers * chunk, LANES), F32),
            pltpu.VMEM((tiles, peers * chunk, LANES), F32),
            pltpu.VMEM((peers * ROWS, LANES), F32),
            pltpu.VMEM((requests, peers * span), F32),
        ],
        compiler_params=params(24),
        cost_estimate=pl.CostEstimate(
            flops=2 * peers * chunk * 2 * positions * (2 * latent + rope),
            bytes_accessed=6 * 2**20,
            transcendentals=peers * chunk * 2 * positions,
        ),
        name="attention",
    )(lengths, query, lat_own, lat_far, rope_own, rope_far, ids, route)


def experts_kernel(
    own, far, gate, up, down, out_0, out_1, out_2, out_3, gate_in, up_in, down_in, sems
):
    depth = gate.shape[0]
    span = 112
    blocks = depth // (2 * span)
    pieces = 4
    piece = depth // pieces
    core = lax.axis_index("c")
    copies = []
    for index in range(pieces):
        rows = pl.ds(index * piece, piece)
        for number, (source, target) in enumerate(((gate, gate_in), (up, up_in))):
            copies.append(
                pltpu.make_async_copy(
                    source.at[rows, :], target.at[rows, :], sems.at[2 * index + number]
                )
            )
    last = pltpu.make_async_copy(down, down_in, sems.at[2 * pieces])
    for copy in copies:
        copy.start()
    last.start()
    total = jnp.zeros((own.shape[0], 2 * gate.shape[1]), F32)
    each = blocks // pieces
    for index in range(pieces):
        copies[2 * index].wait()
        copies[2 * index + 1].wait()
        for tokens, parity in ((own, core), (far, 1 - core)):
            columns = []
            for source in (gate_in, up_in):
                columns.append(
                    jnp.concatenate(
                        [
                            source[
                                pl.ds(
                                    pl.multiple_of(2 * span * block + span * parity, 16), span
                                ),
                                :,
                            ]
                            for block in range(each * index, each * (index + 1))
                        ],
                        axis=0,
                    )
                )
            total += jnp.dot(
                tokens[:, each * span * index : each * span * (index + 1)],
                jnp.concatenate(columns, axis=1),
                preferred_element_type=F32,
            )
    units = gate.shape[1]
    gate_proj, up_proj = total[:, :units], total[:, units:]
    hidden = (gate_proj * jax.nn.sigmoid(gate_proj) * up_proj).astype(BF16)
    last.wait()
    width = down.shape[1]
    step = 1024
    for start in range(0, width, step):
        result = jnp.dot(hidden, down_in[:, start : start + step], preferred_element_type=F32)
        result = result.astype(BF16)
        for block, out in enumerate((out_0, out_1, out_2, out_3)):
            out[:, start : start + step] = result[CAP * block : CAP * (block + 1)]


def experts(own, far, gate, up, down):
    depth, units = gate.shape
    width = down.shape[1]
    return pl.pallas_call(
        experts_kernel,
        out_shape=[jax.ShapeDtypeStruct((CAP, width), BF16)] * 4,
        in_specs=[VMEM] * 2 + [HBM] * 3,
        out_specs=[VMEM] * 4,
        scratch_shapes=[
            pltpu.VMEM((depth, units), BF16),
            pltpu.VMEM((depth, units), BF16),
            pltpu.VMEM((units, width), BF16),
            pltpu.SemaphoreType.DMA((9,)),
        ],
        compiler_params=params(24),
        cost_estimate=pl.CostEstimate(
            flops=2 * 16 * 3 * depth * units, bytes_accessed=6 * 2**20, transcendentals=0
        ),
        name="experts",
    )(own, far, gate, up, down)


def merge_kernel(
    got, value, project, mix, back_0, back_1, back_2, back_3, keep, send, project_in, sem
):
    copy = pltpu.make_async_copy(project, project_in, sem)
    copy.start()
    peers, height, _ = got.shape
    heads = value.shape[0]
    chunk = ROWS * heads
    tiles = height // chunk
    core = lax.axis_index("c")
    stats = got[:, tiles * chunk :, :].astype(F32)
    lane = lax.broadcasted_iota(jnp.int32, (peers, ROWS, LANES), 2)
    first = lane - ROWS * lax.broadcasted_iota(jnp.int32, (peers, ROWS, LANES), 1)
    tops, totals = [], []
    for head in range(heads):
        row = jnp.broadcast_to(stats[:, head : head + 1, :], (peers, ROWS, LANES))
        tops.append(
            jnp.sum(jnp.where((first >= 0) & (first < 3), row, 0.0), axis=2, keepdims=True)
        )
        totals.append(
            jnp.sum(jnp.where((first >= 3) & (first < 6), row, 0.0), axis=2, keepdims=True)
        )
    top = jnp.concatenate(tops, axis=1)
    total = jnp.concatenate(totals, axis=1)
    peak = jnp.max(top, axis=0, keepdims=True)
    share = total * jnp.exp(top - peak)
    denominator = jnp.sum(share, axis=0)
    columns = []
    for tile in range(tiles):
        piece = got[:, tile * chunk : (tile + 1) * chunk, :].astype(F32)
        columns.append(jnp.sum(piece * share, axis=0) / denominator)
    merged = jnp.concatenate(columns, axis=1)
    values = []
    for head in range(heads):
        rows = merged[ROWS * head : ROWS * (head + 1)].astype(BF16)
        values.append(jnp.dot(rows, value[head], preferred_element_type=F32))
    head_values = jnp.concatenate(values, axis=1).astype(BF16)

    back = jnp.concatenate(
        [ref[...].astype(F32) for ref in (back_0, back_1, back_2, back_3)], axis=0
    ).astype(BF16)
    mixing = mix[...][:, : 4 * CAP]
    high = mixing.astype(BF16)
    low = (mixing - high.astype(F32)).astype(BF16)
    routed = jnp.dot(high, back, preferred_element_type=F32) + jnp.dot(
        low, back, preferred_element_type=F32
    )
    copy.wait()
    attended = jnp.dot(head_values, project_in[...], preferred_element_type=F32)
    both = jnp.concatenate([attended, routed], axis=0)
    span = keep.shape[2]
    for peer in range(peers):
        even = both[:, 2 * peer * span : (2 * peer + 1) * span]
        odd = both[:, (2 * peer + 1) * span : (2 * peer + 2) * span]
        keep[peer] = jnp.where(core == 1, odd, even).astype(BF16)
        send[peer] = jnp.where(core == 1, even, odd).astype(BF16)


def merge(got, value, project, mix, back, span):
    peers = got.shape[0]
    depth, width = project.shape
    shape = jax.ShapeDtypeStruct((peers, 2 * ROWS, span), BF16)
    return pl.pallas_call(
        merge_kernel,
        out_shape=[shape, shape],
        in_specs=[VMEM, VMEM, HBM, VMEM] + [VMEM] * 4,
        out_specs=[VMEM] * 2,
        scratch_shapes=[pltpu.VMEM((depth, width), BF16), pltpu.SemaphoreType.DMA],
        compiler_params=params(24),
        cost_estimate=pl.CostEstimate(
            flops=2 * 8 * depth * width, bytes_accessed=6 * 2**20, transcendentals=0
        ),
        name="merge",
    )(got, value, project, mix, *back)


def shards(
    query_lat,
    query_rope,
    cache_lat,
    cache_rope,
    lengths,
    w_value,
    w_out,
    moe_tokens,
    expert_ids,
    route_weights,
    w_gate,
    w_up,
    w_down,
):
    plane = ("y", "z")
    group_count = lax.axis_size("x")
    peers = lax.axis_size(plane)
    requests = cache_lat.shape[0]
    span = moe_tokens.shape[1]
    swap = [(0, 1), (1, 0)]

    def along_x(value, shift):
        return lax.ppermute(
            value, "x", [(i, (i + shift) % group_count) for i in range(group_count)]
        )

    query = lax.all_to_all(
        payload(query_lat, query_rope, moe_tokens, peers), plane, 0, 0, tiled=True
    )
    lat_far = lax.ppermute(cache_lat, "c", swap)
    rope_far = lax.ppermute(cache_rope, "c", swap)
    scale = (w_value.shape[2] + query_rope.shape[2]) ** (-0.5)
    part, *send, mix = attention(
        lengths,
        query,
        cache_lat,
        lat_far,
        cache_rope,
        rope_far,
        expert_ids,
        route_weights,
        scale,
        span,
        w_gate.shape[1],
    )
    got = lax.all_to_all(part, plane, 0, 0, tiled=True)

    near = [send[0]] + [along_x(send[d], d) for d in range(1, group_count)]
    own = jnp.concatenate(near, axis=0)
    far = lax.ppermute(own, "c", swap)
    routed = experts(own, far, w_gate, w_up, w_down)
    back = [routed[0]] + [along_x(routed[d], -d) for d in range(1, group_count)]

    keep, give = merge(got, w_value, w_out, mix, back, span)
    taken = lax.ppermute(give, "c", swap)
    terms = (keep.astype(F32) + taken.astype(F32)).astype(BF16)
    arrived = lax.all_to_all(terms, plane, 0, 0, tiled=True)
    summed = jnp.sum(arrived.astype(F32), axis=0).astype(BF16)
    return (summed[:requests], summed[requests:])


def solution(mesh):
    groups = mesh.shape["grp"]
    split = Mesh(mesh.devices.reshape(groups, 4, 8, 2), ("x",) + KV)
    both = ("x",) + KV
    return jax.shard_map(
        shards,
        mesh=split,
        in_specs=(
            P("x", KV, None),
            P("x", KV, None),
            P("x", KV, None),
            P("x", None, KV),
            P("x"),
            P(KV, None, None),
            P(KV, None),
            P("x", KV),
            P("x", None),
            P("x", None),
            P(None, both),
            P(None, both),
            P(both, None),
        ),
        out_specs=(P("x", KV), P("x", KV)),
        check_vma=False,
    )
```

time: 470 us -> 106 us (0.23); the launches traced: 464 us -> 105 us
  waiting for transfers between devices: 292 us -> 25.7 us
  blocking collectives: 97.7 us -> 18.5 us
  matrix products: 19.8 us -> 0 us
  Pallas kernels: 0 us -> 14.7 us
  between operations: 13.9 us -> 0.71 us
  starting transfers between devices: 26.4 us -> 32.8 us
    unnamed x5 -> x0, waiting for transfers between devices: 251 us -> none
    all_gather x2 -> x0, blocking collectives: 97.7 us -> none  [the longest x1 54.3 us: shards(): token_rows = lax.all_gather(moe_tokens, 'kv', axis=1, tiled=True)]
    all_to_all x5 -> x2, waiting for transfers between devices: 40.9 us -> 15.7 us  [the longest x1 15.7 us: shards(): lax.all_to_all(payload(query_lat, query_rope, moe_tokens, peers), plane,...]
    all_to_all x0 -> x1, blocking collectives: none -> 18.5 us  [shards(): arrived = lax.all_to_all(terms, plane, 0, 0, tiled=True)]
    ppermute x0 -> x10, starting transfers between devices: none -> 15.8 us  [the longest x6 8.01 us: along_x(): lax.ppermute(value, 'x', [(i, (i + shift) % group_count) for i in range(g...]
    pallas_call x0 -> x4, Pallas kernels: none -> 14.7 us  [the longest x1 5.74 us: attention(): pl.pallas_call(lambda *refs: attention_kernel(*refs, scale=scale, units=u...]
    dot_general x8 -> x0, matrix products: 14.3 us -> none  [the longest x1 2.7 us: shards(): jnp.einsum('gct,gcd->td', mixing, returned, preferred_element_type=jnp.fl...]
    ppermute x0 -> x10, waiting for transfers between devices: none -> 10.1 us  [the longest x6 6.66 us: along_x(): lax.ppermute(value, 'x', [(i, (i + shift) % group_count) for i in range(g...]
  transfers between devices with their start and end apart: 8 -> 12, of which waited for: 6 -> 9; matrix products, arithmetic and copies ran while one was open for 7% -> 0% of each run, Pallas kernels for 0% -> 5%
where the time goes in v2:
time: 106 us; the launch traced here: 105 us
  starting transfers between devices  32.8 us (31%)
  waiting for transfers between devices  25.7 us (24%)
  blocking collectives  18.5 us (17%)
  Pallas kernels  14.7 us (14%)
  local copies, waits for them, and re-layouts  12.8 us (12%)
    all_to_all x1, blocking collectives, shards(): arrived = lax.all_to_all(terms, plane, 0, 0, tiled=True)  18.5 us
    all_to_all x1, waiting for transfers between devices, shards(): lax.all_to_all(payload(query_lat, query_rope, moe_tokens, peers), plane,...  15.7 us
    unnamed x26, local copies, waits for them, and re-layouts  12.2 us
    all_to_all x1, starting transfers between devices, shards(): lax.all_to_all(payload(query_lat, query_rope, moe_tokens, peers), plane,...  9.47 us
    ppermute x6, starting transfers between devices, along_x(): lax.ppermute(value, 'x', [(i, (i + shift) % group_count) for i in range(g...  8.01 us
    all_to_all x1, starting transfers between devices, shards(): got = lax.all_to_all(part, plane, 0, 0, tiled=True)  7.5 us
    ppermute x6, waiting for transfers between devices, along_x(): lax.ppermute(value, 'x', [(i, (i + shift) % group_count) for i in range(g...  6.66 us
    pallas_call x1, Pallas kernels, attention(): pl.pallas_call(lambda *refs: attention_kernel(*refs, scale=scale, units=u...  5.74 us
  transfers between devices with their start and end apart: 12, of which 9 were waited for; matrix products, arithmetic and copies ran while one was open for 0% of the time, Pallas kernels for 5%

profile of v2, /device:TPU:1, one launch (start us, length us, event | category | flops | bytes accessed | tf_op | source)
XLA Modules:
  0.0 105.4 jit_solution(2398134470151175537)
XLA Ops:
  0.6 3.3 %collective-permute-start = (bf16[8,256,512]{2,1,0:T(8,128)(2,1)}, bf16[8,256,512]{2,1,0:T(8,128)(2,1)S(1)}, u32[]{:S(2)}, u32[]{:S(2)}) collective-permute-start(bf16[8,256,512]{2,1,0:T(8,128)(2,1)} %refs_2_.1), channel_id=1, source_target_pairs={{0,1},{1,0},{2,3},{3,2},{4,5},{5,4},{6,7},{7,6},{8,9},{9,8},{10,11... | collective-permute-start | bytes 6291464 | tf_op jit(solution)/shard_map/ppermute | solution.py:418
  7.0 9.5 %all-to-all-start = ((bf16[32,16,640]{2,1,0:T(8,128)(2,1)}), bf16[32,16,640]{2,1,0:T(8,128)(2,1)S(1)}, u32[]{:S(2)}, u32[]{:S(2)}) async-start(bf16[32,16,640]{2,1,0:T(8,128)(2,1)} %payload.1), calls=%async_computation | async-start | bytes 1310720 | tf_op jit(solution)/shard_map/all_to_all | solution.py:415
  16.9 1.4 %collective-permute-done.1.refs_5_ = bf16[8,64,256]{2,1,0:T(8,128)(2,1)S(1)} collective-permute-done((bf16[8,64,256]{2,1,0:T(8,128)(2,1)}, bf16[8,64,256]{2,1,0:T(8,128)(2,1)S(1)}, u32[]{:S(2)}, u32[]{:S(2)}) %collective-permute-start.1) | collective-permute-done | bytes 262176 | tf_op jit(solution)/shard_map/ppermute | solution.py:419
  18.3 15.7 %all-to-all-done.refs_1_ = bf16[32,16,640]{2,1,0:T(8,128)(2,1)S(1)} async-done(((bf16[32,16,640]{2,1,0:T(8,128)(2,1)}), bf16[32,16,640]{2,1,0:T(8,128)(2,1)S(1)}, u32[]{:S(2)}, u32[]{:S(2)}) %all-to-all-start) | async-done | bytes 655392 | tf_op jit(solution)/shard_map/all_to_all | solution.py:415
  34.0 1.6 %copy-done.1 = bf16[8,256,512]{2,1,0:T(8,128)(2,1)S(1)} copy-done((bf16[8,256,512]{2,1,0:T(8,128)(2,1)S(1)}, bf16[8,256,512]{2,1,0:T(8,128)(2,1)}, u32[]{:S(2)}) %copy-start.1) | copy-done | bytes 2097176
  37.6 5.7 %attention.1 = (bf16[32,72,128]{2,1,0:T(8,128)(2,1)}, bf16[4,3584]{1,0:T(4,128)(2,1)S(1)}, bf16[4,3584]{1,0:T(4,128)(2,1)S(1)}, bf16[4,3584]{1,0:T(4,128)(2,1)S(...) custom-call(s32[8]{0:T(128)S(1)} %copy-done.12, bf16[32,16,640]{2,1,0:T(8,128)(2,1)S(1)} %all-to-all-done.refs_1_, ...), custom_call_target="tpu_custom_call" | custom-call | flops 570425344 | bytes 6291456 | tf_op jit(solution)/shard_map/attention/pallas_call | solution.py:205
  43.4 7.5 %all-to-all-start.1 = ((bf16[32,72,128]{2,1,0:T(8,128)(2,1)}), bf16[32,72,128]{2,1,0:T(8,128)(2,1)S(1)}, u32[]{:S(2)}, u32[]{:S(2)}) async-start(bf16[32,72,128]{2,1,0:T(8,128)(2,1)} %get-tuple-element.14), calls=%async_computation.1 | async-start | bytes 1179648 | tf_op jit(solution)/shard_map/all_to_all | solution.py:434
  50.9 1.3 %collective-permute-start.2 = (bf16[4,3584]{1,0:T(4,128)(2,1)S(1)}, bf16[4,3584]{1,0:T(4,128)(2,1)S(1)}, u32[]{:S(2)}, u32[]{:S(2)}) collective-permute-start(bf16[4,3584]{1,0:T(4,128)(2,1)S(1)} %get-tuple-element.17), channel_id=1, source_target_pairs={{0,64},{64,128},{128,192},{192,0},{1,65},{65,129},{129,193},{193,1... | collective-permute-start | bytes 86024 | tf_op jit(solution)/shard_map/ppermute | solution.py:411
  52.2 2.4 %collective-permute-start.3 = (bf16[4,3584]{1,0:T(4,128)(2,1)S(1)}, bf16[4,3584]{1,0:T(4,128)(2,1)S(1)}, u32[]{:S(2)}, u32[]{:S(2)}) collective-permute-start(bf16[4,3584]{1,0:T(4,128)(2,1)S(1)} %get-tuple-element.18), channel_id=1, source_target_pairs={{0,128},{64,192},{128,0},{192,64},{1,129},{65,193},{129,1},{193,65... | collective-permute-start | bytes 86024 | tf_op jit(solution)/shard_map/ppermute | solution.py:411
  54.6 1.2 %collective-permute-start.4 = (bf16[4,3584]{1,0:T(4,128)(2,1)S(1)}, bf16[4,3584]{1,0:T(4,128)(2,1)S(1)}, u32[]{:S(2)}, u32[]{:S(2)}) collective-permute-start(bf16[4,3584]{1,0:T(4,128)(2,1)S(1)} %get-tuple-element.19), channel_id=1, source_target_pairs={{0,192},{64,0},{128,64},{192,128},{1,193},{65,1},{129,65},{193,129... | collective-permute-start | bytes 86024 | tf_op jit(solution)/shard_map/ppermute | solution.py:411
  56.4 1.4 %collective-permute-done.4 = bf16[4,3584]{1,0:T(4,128)(2,1)S(1)} collective-permute-done((bf16[4,3584]{1,0:T(4,128)(2,1)S(1)}, bf16[4,3584]{1,0:T(4,128)(2,1)S(1)}, u32[]{:S(2)}, u32[]{:S(2)}) %collective-permute-start.4) | collective-permute-done | bytes 28704 | tf_op jit(solution)/shard_map/ppermute | solution.py:411
  57.9 2.5 %collective-permute-start.5 = (bf16[16,3584]{1,0:T(8,128)(2,1)S(1)}, bf16[16,3584]{1,0:T(8,128)(2,1)S(1)}, u32[]{:S(2)}, u32[]{:S(2)}) collective-permute-start(bf16[16,3584]{1,0:T(8,128)(2,1)S(1)} %pad_maximum_fusion.own), channel_id=1, source_target_pairs={{0,1},{1,0},{2,3},{3,2},{4,5},{5,4},{6,7},{7,6},{8,9},{9,8},{10,11... | collective-permute-start | bytes 344072 | tf_op jit(solution)/shard_map/ppermute | solution.py:438
  60.4 1.0 collective-permute-done.5.far
  61.4 1.5 %copy-done.2 = bf16[7168,128]{1,0:T(8,128)(2,1)S(1)} copy-done((bf16[7168,128]{1,0:T(8,128)(2,1)S(1)}, bf16[7168,128]{1,0:T(8,128)(2,1)}, u32[]{:S(2)}) %copy-start.2) | copy-done | bytes 1835032
  62.9 1.5 %copy-done.3 = bf16[7168,128]{1,0:T(8,128)(2,1)S(1)} copy-done((bf16[7168,128]{1,0:T(8,128)(2,1)S(1)}, bf16[7168,128]{1,0:T(8,128)(2,1)}, u32[]{:S(2)}) %copy-start.3) | copy-done | bytes 1835032
  64.4 1.5 %copy-done.4 = bf16[128,7168]{1,0:T(8,128)(2,1)S(1)} copy-done((bf16[128,7168]{1,0:T(8,128)(2,1)S(1)}, bf16[128,7168]{1,0:T(8,128)(2,1)}, u32[]{:S(2)}) %copy-start.4) | copy-done | bytes 1835032
  65.9 4.1 %experts.1 = (bf16[4,7168]{1,0:T(4,128)(2,1)S(1)}, bf16[4,7168]{1,0:T(4,128)(2,1)S(1)}, bf16[4,7168]{1,0:T(4,128)(2,1)S(1)}, bf16[4,7168]{1,0:T(4,128)(2,1)S(1)}) custom-call(bf16[16,3584]{1,0:T(8,128)(2,1)S(1)} %pad_maximum_fusion.own, bf16[16,3584]{1,0:T(8,128)(2,1)S(1)} %collective-permute-done.5.far, bf16[7168,128]{1,0:T(8,128)(2,1)S(1)} %copy-done.2, ...), custom_call_target="tpu_custom_call" | custom-call | flops 88080384 | bytes 6291456 | tf_op jit(solution)/shard_map/experts/pallas_call | solution.py:293
  70.0 2.4 %collective-permute-start.6 = (bf16[4,7168]{1,0:T(4,128)(2,1)S(1)}, bf16[4,7168]{1,0:T(4,128)(2,1)S(1)}, u32[]{:S(2)}, u32[]{:S(2)}) collective-permute-start(bf16[4,7168]{1,0:T(4,128)(2,1)S(1)} %get-tuple-element.21), channel_id=1, source_target_pairs={{0,192},{64,0},{128,64},{192,128},{1,193},{65,1},{129,65},{193,129... | collective-permute-start | bytes 172040 | tf_op jit(solution)/shard_map/ppermute | solution.py:411
  73.7 3.4 %collective-permute-done.7.back_2 = bf16[4,7168]{1,0:T(4,128)(2,1)S(1)} collective-permute-done((bf16[4,7168]{1,0:T(4,128)(2,1)S(1)}, bf16[4,7168]{1,0:T(4,128)(2,1)S(1)}, u32[]{:S(2)}, u32[]{:S(2)}) %collective-permute-start.7) | collective-permute-done | bytes 57376 | tf_op jit(solution)/shard_map/ppermute | solution.py:411
  77.7 2.0 %copy-done = bf16[256,7168]{1,0:T(8,128)(2,1)S(1)} copy-done((bf16[256,7168]{1,0:T(8,128)(2,1)S(1)}, bf16[256,7168]{1,0:T(8,128)(2,1)}, u32[]{:S(2)}) %copy-start) | copy-done | bytes 3670040
  79.8 3.9 %merge.1 = (bf16[32,16,112]{2,1,0:T(8,128)(2,1)S(1)}, bf16[32,16,112]{2,1,0:T(8,128)(2,1)S(1)}) custom-call(bf16[32,72,128]{2,1,0:T(8,128)(2,1)S(1)} %all-to-all-done.1.got, bf16[2,512,128]{2,1,0:T(8,128)(2,1)S(1)} %copy-done.6, bf16[256,7168]{1,0:T(8,128)(2,1)S(1)} %copy-done, f32[8,128]{1,0:T(8,128)S(1)} %get-tuple-element.15.mix, ...), custom_call_target="tpu_custom_call" | custom-call | flops 29360128 | bytes 6291456 | tf_op jit(solution)/shard_map/merge/pallas_call | solution.py:374
  83.7 1.6 %collective-permute-start.9 = (bf16[32,16,112]{2,1,0:T(8,128)(2,1)S(1)}, bf16[32,16,112]{2,1,0:T(8,128)(2,1)S(1)}, u32[]{:S(2)}, u32[]{:S(2)}) collective-permute-start(bf16[32,16,112]{2,1,0:T(8,128)(2,1)S(1)} %get-tuple-element.25), channel_id=1, source_target_pairs={{0,1},{1,0},{2,3},{3,2},{4,5},{5,4},{6,7},{7,6},{8,9},{9,8},{10,11... | collective-permute-start | bytes 344072 | tf_op jit(solution)/shard_map/ppermute | solution.py:443
  85.3 1.0 collective-permute-done.9
  86.3 18.5 %all_to_all.15 = bf16[32,16,112]{2,1,0:T(8,128)(2,1)S(1)} all-to-all(bf16[32,16,112]{2,1,0:T(8,128)(2,1)S(1)} %add_convert_fusion), channel_id=1, replica_groups=mesh['x'=4,'y'=4,'z'=8,'c'=2] {'y','z'}, dimensions={0} | all-to-all | bytes 229376 | tf_op jit(solution)/shard_map/all_to_all | solution.py:445
  (35 shorter events, 8.7 us)
Async XLA Ops:
  0.6 33.4 %copy-start.5 = (bf16[8,64,256]{2,1,0:T(8,128)(2,1)S(1)}, bf16[8,64,256]{2,1,0:T(8,128)(2,1)}, u32[]{:S(2)}) copy-start(bf16[8,64,256]{2,1,0:T(8,128)(2,1)} %refs_4_.1) | copy-start | bytes 786436
  0.6 33.3 %collective-permute-start = (bf16[8,256,512]{2,1,0:T(8,128)(2,1)}, bf16[8,256,512]{2,1,0:T(8,128)(2,1)S(1)}, u32[]{:S(2)}, u32[]{:S(2)}) collective-permute-start(bf16[8,256,512]{2,1,0:T(8,128)(2,1)} %refs_2_.1), channel_id=1, source_target_pairs={{0,1},{1,0},{2,3},{3,2},{4,5},{5,4},{6,7},{7,6},{8,9},{9,8},{10,11... | collective-permute-start | bytes 6291464 | tf_op jit(solution)/shard_map/ppermute | solution.py:418
  4.0 0.7 copy-start.7
  4.7 0.7 copy-start.8
  5.4 0.7 copy-start.11
  7.0 27.0 %all-to-all-start = ((bf16[32,16,640]{2,1,0:T(8,128)(2,1)}), bf16[32,16,640]{2,1,0:T(8,128)(2,1)S(1)}, u32[]{:S(2)}, u32[]{:S(2)}) async-start(bf16[32,16,640]{2,1,0:T(8,128)(2,1)} %payload.1), calls=%async_computation | async-start | bytes 1310720 | tf_op jit(solution)/shard_map/all_to_all | solution.py:415
  16.5 1.8 %collective-permute-start.1 = (bf16[8,64,256]{2,1,0:T(8,128)(2,1)}, bf16[8,64,256]{2,1,0:T(8,128)(2,1)S(1)}, u32[]{:S(2)}, u32[]{:S(2)}) collective-permute-start(bf16[8,64,256]{2,1,0:T(8,128)(2,1)} %refs_4_.1), channel_id=1, source_target_pairs={{0,1},{1,0},{2,3},{3,2},{4,5},{5,4},{6,7},{7,6},{8,9},{9,8},{10,11... | collective-permute-start | bytes 786440 | tf_op jit(solution)/shard_map/ppermute | solution.py:419
  34.0 1.6 %copy-start.1 = (bf16[8,256,512]{2,1,0:T(8,128)(2,1)S(1)}, bf16[8,256,512]{2,1,0:T(8,128)(2,1)}, u32[]{:S(2)}) copy-start(bf16[8,256,512]{2,1,0:T(8,128)(2,1)} %refs_2_.1) | copy-start | bytes 6291460
  35.6 0.7 copy-start.9
  36.3 0.7 copy-start.10
  43.4 34.4 %all-to-all-start.1 = ((bf16[32,72,128]{2,1,0:T(8,128)(2,1)}), bf16[32,72,128]{2,1,0:T(8,128)(2,1)S(1)}, u32[]{:S(2)}, u32[]{:S(2)}) async-start(bf16[32,72,128]{2,1,0:T(8,128)(2,1)} %get-tuple-element.14), calls=%async_computation.1 | async-start | bytes 1179648 | tf_op jit(solution)/shard_map/all_to_all | solution.py:434
  50.9 4.9 %collective-permute-start.2 = (bf16[4,3584]{1,0:T(4,128)(2,1)S(1)}, bf16[4,3584]{1,0:T(4,128)(2,1)S(1)}, u32[]{:S(2)}, u32[]{:S(2)}) collective-permute-start(bf16[4,3584]{1,0:T(4,128)(2,1)S(1)} %get-tuple-element.17), channel_id=1, source_target_pairs={{0,64},{64,128},{128,192},{192,0},{1,65},{65,129},{129,193},{193,1... | collective-permute-start | bytes 86024 | tf_op jit(solution)/shard_map/ppermute | solution.py:411
  52.2 4.2 %collective-permute-start.3 = (bf16[4,3584]{1,0:T(4,128)(2,1)S(1)}, bf16[4,3584]{1,0:T(4,128)(2,1)S(1)}, u32[]{:S(2)}, u32[]{:S(2)}) collective-permute-start(bf16[4,3584]{1,0:T(4,128)(2,1)S(1)} %get-tuple-element.18), channel_id=1, source_target_pairs={{0,128},{64,192},{128,0},{192,64},{1,129},{65,193},{129,1},{193,65... | collective-permute-start | bytes 86024 | tf_op jit(solution)/shard_map/ppermute | solution.py:411
  54.6 3.2 %collective-permute-start.4 = (bf16[4,3584]{1,0:T(4,128)(2,1)S(1)}, bf16[4,3584]{1,0:T(4,128)(2,1)S(1)}, u32[]{:S(2)}, u32[]{:S(2)}) collective-permute-start(bf16[4,3584]{1,0:T(4,128)(2,1)S(1)} %get-tuple-element.19), channel_id=1, source_target_pairs={{0,192},{64,0},{128,64},{192,128},{1,193},{65,1},{129,65},{193,129... | collective-permute-start | bytes 86024 | tf_op jit(solution)/shard_map/ppermute | solution.py:411
  57.9 3.5 %collective-permute-start.5 = (bf16[16,3584]{1,0:T(8,128)(2,1)S(1)}, bf16[16,3584]{1,0:T(8,128)(2,1)S(1)}, u32[]{:S(2)}, u32[]{:S(2)}) collective-permute-start(bf16[16,3584]{1,0:T(8,128)(2,1)S(1)} %pad_maximum_fusion.own), channel_id=1, source_target_pairs={{0,1},{1,0},{2,3},{3,2},{4,5},{5,4},{6,7},{7,6},{8,9},{9,8},{10,11... | collective-permute-start | bytes 344072 | tf_op jit(solution)/shard_map/ppermute | solution.py:438
  61.4 1.5 %copy-start.2 = (bf16[7168,128]{1,0:T(8,128)(2,1)S(1)}, bf16[7168,128]{1,0:T(8,128)(2,1)}, u32[]{:S(2)}) copy-start(bf16[7168,128]{1,0:T(8,128)(2,1)} %gate.1) | copy-start | bytes 5505028
  62.9 1.5 %copy-start.3 = (bf16[7168,128]{1,0:T(8,128)(2,1)S(1)}, bf16[7168,128]{1,0:T(8,128)(2,1)}, u32[]{:S(2)}) copy-start(bf16[7168,128]{1,0:T(8,128)(2,1)} %up.1) | copy-start | bytes 5505028
  64.4 1.5 %copy-start.4 = (bf16[128,7168]{1,0:T(8,128)(2,1)S(1)}, bf16[128,7168]{1,0:T(8,128)(2,1)}, u32[]{:S(2)}) copy-start(bf16[128,7168]{1,0:T(8,128)(2,1)} %down.1) | copy-start | bytes 5505028
  65.9 11.8 %copy-start.6 = (bf16[2,512,128]{2,1,0:T(8,128)(2,1)S(1)}, bf16[2,512,128]{2,1,0:T(8,128)(2,1)}, u32[]{:S(2)}) copy-start(bf16[2,512,128]{2,1,0:T(8,128)(2,1)} %value.1) | copy-start | bytes 786436
  70.0 3.7 %collective-permute-start.6 = (bf16[4,7168]{1,0:T(4,128)(2,1)S(1)}, bf16[4,7168]{1,0:T(4,128)(2,1)S(1)}, u32[]{:S(2)}, u32[]{:S(2)}) collective-permute-start(bf16[4,7168]{1,0:T(4,128)(2,1)S(1)} %get-tuple-element.21), channel_id=1, source_target_pairs={{0,192},{64,0},{128,64},{192,128},{1,193},{65,1},{129,65},{193,129... | collective-permute-start | bytes 172040 | tf_op jit(solution)/shard_map/ppermute | solution.py:411
  72.4 4.6 %collective-permute-start.7 = (bf16[4,7168]{1,0:T(4,128)(2,1)S(1)}, bf16[4,7168]{1,0:T(4,128)(2,1)S(1)}, u32[]{:S(2)}, u32[]{:S(2)}) collective-permute-start(bf16[4,7168]{1,0:T(4,128)(2,1)S(1)} %get-tuple-element.22), channel_id=1, source_target_pairs={{0,128},{64,192},{128,0},{192,64},{1,129},{65,193},{129,1},{193,65... | collective-permute-start | bytes 172040 | tf_op jit(solution)/shard_map/ppermute | solution.py:411
  72.5 5.3 %collective-permute-start.8 = (bf16[4,7168]{1,0:T(4,128)(2,1)S(1)}, bf16[4,7168]{1,0:T(4,128)(2,1)S(1)}, u32[]{:S(2)}, u32[]{:S(2)}) collective-permute-start(bf16[4,7168]{1,0:T(4,128)(2,1)S(1)} %get-tuple-element.23), channel_id=1, source_target_pairs={{0,64},{64,128},{128,192},{192,0},{1,65},{65,129},{129,193},{193,1... | collective-permute-start | bytes 172040 | tf_op jit(solution)/shard_map/ppermute | solution.py:411
  77.7 2.0 %copy-start = (bf16[256,7168]{1,0:T(8,128)(2,1)S(1)}, bf16[256,7168]{1,0:T(8,128)(2,1)}, u32[]{:S(2)}) copy-start(bf16[256,7168]{1,0:T(8,128)(2,1)} %project.1) | copy-start | bytes 11010052
  83.7 2.6 %collective-permute-start.9 = (bf16[32,16,112]{2,1,0:T(8,128)(2,1)S(1)}, bf16[32,16,112]{2,1,0:T(8,128)(2,1)S(1)}, u32[]{:S(2)}, u32[]{:S(2)}) collective-permute-start(bf16[32,16,112]{2,1,0:T(8,128)(2,1)S(1)} %get-tuple-element.25), channel_id=1, source_target_pairs={{0,1},{1,0},{2,3},{3,2},{4,5},{5,4},{6,7},{7,6},{8,9},{9,8},{10,11... | collective-permute-start | bytes 344072 | tf_op jit(solution)/shard_map/ppermute | solution.py:443
  (1 other events, 0.7 us)

commit v3 on v2

--- a/solution.py
+++ b/solution.py
@@ -23,6 +23,10 @@
     rest = value - high
     middle = rest.astype(BF16).astype(F32)
     return high, middle, rest - middle
+
+
+def pinned(*values):
+    return [pltpu.with_memory_space_constraint(value, pltpu.HBM) for value in values]
 
 
 def params(mebibytes):
@@ -58,7 +62,7 @@
         out_specs=VMEM,
         compiler_params=params(20),
         name="payload",
-    )(query_lat, query_rope, tokens)
+    )(*pinned(query_lat, query_rope, tokens))
 
 
 def attention_kernel(
@@ -80,12 +84,30 @@
     out_rows,
     stat_rows,
     token_rows,
+    lengths_in,
+    lat_in,
+    rope_in,
+    ids_in,
+    route_in,
+    sems,
     *,
     scale,
     units,
 ):
     peers, chunk, width = query.shape
     requests, positions, latent = lat_own.shape
+    small = [
+        pltpu.make_async_copy(lengths, lengths_in, sems.at[requests]),
+        pltpu.make_async_copy(rope_own, rope_in, sems.at[requests + 1]),
+        pltpu.make_async_copy(ids, ids_in, sems.at[requests + 2]),
+        pltpu.make_async_copy(route, route_in, sems.at[requests + 3]),
+    ]
+    large = [
+        pltpu.make_async_copy(lat_own.at[request], lat_in.at[request], sems.at[request])
+        for request in range(requests)
+    ]
+    for copy in small[:2] + large + small[2:]:
+        copy.start()
     rope = rope_own.shape[1]
     tiles = latent // LANES
     heads = chunk // requests
@@ -103,7 +125,11 @@
     base_own = shard * positions
     base_far = (shard + 1 - 2 * core) * positions
     place = lax.broadcasted_iota(jnp.int32, (rows, positions), 1)
+    small[0].wait()
     for request in range(requests):
+        if request == 0:
+            small[1].wait()
+        large[request].wait()
         mine = jnp.concatenate(
             [
                 jnp.concatenate(
@@ -117,9 +143,9 @@
             ],
             axis=0,
         ).astype(BF16)
-        length = lengths[request]
+        length = lengths_in[request]
         parts = []
-        for lat, rot, base in ((lat_own, rope_own, base_own), (lat_far, rope_far, base_far)):
+        for lat, rot, base in ((lat_in, rope_in, base_own), (lat_far, rope_far, base_far)):
             score = (
                 lax.dot_general(
                     mine[:, :latent],
@@ -137,7 +163,7 @@
         weights = [jnp.where(usable, jnp.exp(score - top), 0.0) for score, usable, _ in parts]
         total = jnp.sum(weights[0] + weights[1], axis=1, keepdims=True)
         weighted = jnp.dot(
-            weights[0].astype(BF16), lat_own[request], preferred_element_type=F32
+            weights[0].astype(BF16), lat_in[request], preferred_element_type=F32
         ) + jnp.dot(weights[1].astype(BF16), lat_far[request], preferred_element_type=F32)
         partial = weighted / jnp.maximum(total, 1.0)
         for index, term in enumerate(three_terms(top) + three_terms(total)):
@@ -170,8 +196,10 @@
             pieces, axis=1
         )
     tokens = token_rows[...].astype(BF16)
-    named = ids[...]
-    strength = route[...]
+    small[2].wait()
+    small[3].wait()
+    named = ids_in[...]
+    strength = route_in[...]
     lower = (
         lax.broadcasted_iota(jnp.int32, (ROWS, ROWS), 1)
         < lax.broadcasted_iota(jnp.int32, (ROWS, ROWS), 0)
@@ -202,18 +230,25 @@
     requests, positions, latent = lat_own.shape
     rope = rope_own.shape[1]
     tiles = latent // LANES
+    lengths, lat_own, rope_own, ids, route = pinned(lengths, lat_own, rope_own, ids, route)
     return pl.pallas_call(
         lambda *refs: attention_kernel(*refs, scale=scale, units=units),
         out_shape=[jax.ShapeDtypeStruct((peers, tiles * chunk + ROWS, LANES), BF16)]
         + [jax.ShapeDtypeStruct((CAP, peers * span), BF16)] * 4
         + [jax.ShapeDtypeStruct((ROWS, LANES), F32)],
-        in_specs=[SMEM] + [VMEM] * 7,
+        in_specs=[HBM, VMEM, HBM, VMEM, HBM, VMEM, HBM, HBM],
         out_specs=[VMEM] * 6,
         scratch_shapes=[
             pltpu.VMEM((width // LANES, peers * chunk, LANES), F32),
             pltpu.VMEM((tiles, peers * chunk, LANES), F32),
             pltpu.VMEM((peers * ROWS, LANES), F32),
             pltpu.VMEM((requests, peers * span), F32),
+            pltpu.SMEM(lengths.shape, jnp.int32),
+            pltpu.VMEM(lat_own.shape, BF16),
+            pltpu.VMEM(rope_own.shape, BF16),
+            pltpu.VMEM(ids.shape, jnp.int32),
+            pltpu.VMEM(route.shape, F32),
+            pltpu.SemaphoreType.DMA((requests + 4,)),
         ],
         compiler_params=params(24),
         cost_estimate=pl.CostEstimate(
@@ -225,36 +260,45 @@
     )(lengths, query, lat_own, lat_far, rope_own, rope_far, ids, route)
 
 
-def experts_kernel(
-    own, far, gate, up, down, out_0, out_1, out_2, out_3, gate_in, up_in, down_in, sems
-):
-    depth = gate.shape[0]
+def fetch_kernel(after, *refs):
+    del after
+    count = len(refs) // 2
+    sems = refs[-1]
+    copies = [
+        pltpu.make_async_copy(refs[index], refs[count + index], sems.at[index])
+        for index in range(count)
+    ]
+    for copy in copies:
+        copy.start()
+    for copy in copies:
+        copy.wait()
+
+
+def fetch(after, *weights):
+    return pl.pallas_call(
+        fetch_kernel,
+        out_shape=[pltpu.VMEM(weight.shape, weight.dtype) for weight in weights],
+        in_specs=[pl.BlockSpec(memory_space=pl.ANY)] + [HBM] * len(weights),
+        out_specs=[VMEM] * len(weights),
+        scratch_shapes=[pltpu.SemaphoreType.DMA((len(weights),))],
+        compiler_params=params(1),
+        cost_estimate=pl.CostEstimate(flops=0, bytes_accessed=10 * 2**20, transcendentals=0),
+        name="fetch",
+    )(after, *pinned(*weights))
+
+
+def experts_kernel(own, far, gate, up, down, keep, send):
+    depth, units = gate.shape
+    width = down.shape[1]
     span = 112
     blocks = depth // (2 * span)
-    pieces = 4
-    piece = depth // pieces
     core = lax.axis_index("c")
-    copies = []
-    for index in range(pieces):
-        rows = pl.ds(index * piece, piece)
-        for number, (source, target) in enumerate(((gate, gate_in), (up, up_in))):
-            copies.append(
-                pltpu.make_async_copy(
-                    source.at[rows, :], target.at[rows, :], sems.at[2 * index + number]
-                )
-            )
-    last = pltpu.make_async_copy(down, down_in, sems.at[2 * pieces])
-    for copy in copies:
-        copy.start()
-    last.start()
-    total = jnp.zeros((own.shape[0], 2 * gate.shape[1]), F32)
-    each = blocks // pieces
-    for index in range(pieces):
-        copies[2 * index].wait()
-        copies[2 * index + 1].wait()
+    each = 8
+    total = jnp.zeros((own.shape[0], 2 * units), F32)
+    for index in range(blocks // each):
         for tokens, parity in ((own, core), (far, 1 - core)):
             columns = []
-            for source in (gate_in, up_in):
+            for source in (gate, up):
                 columns.append(
                     jnp.concatenate(
                         [
@@ -274,34 +318,32 @@
                 jnp.concatenate(columns, axis=1),
                 preferred_element_type=F32,
             )
-    units = gate.shape[1]
     gate_proj, up_proj = total[:, :units], total[:, units:]
     hidden = (gate_proj * jax.nn.sigmoid(gate_proj) * up_proj).astype(BF16)
-    last.wait()
-    width = down.shape[1]
-    step = 1024
+    pair = 2 * span
+    step = 8 * span
     for start in range(0, width, step):
-        result = jnp.dot(hidden, down_in[:, start : start + step], preferred_element_type=F32)
-        result = result.astype(BF16)
-        for block, out in enumerate((out_0, out_1, out_2, out_3)):
-            out[:, start : start + step] = result[CAP * block : CAP * (block + 1)]
+        result = jnp.dot(hidden, down[:, start : start + step], preferred_element_type=F32)
+        evens, odds = [], []
+        for inner in range(0, step, pair):
+            evens.append(result[:, inner : inner + span])
+            odds.append(result[:, inner + span : inner + pair])
+        even, odd = jnp.concatenate(evens, axis=1), jnp.concatenate(odds, axis=1)
+        here = slice(start // 2, (start + step) // 2)
+        keep[:, here] = jnp.where(core == 1, odd, even)
+        send[:, here] = jnp.where(core == 1, even, odd).astype(BF16)
 
 
 def experts(own, far, gate, up, down):
     depth, units = gate.shape
     width = down.shape[1]
+    shape = (own.shape[0], width // 2)
     return pl.pallas_call(
         experts_kernel,
-        out_shape=[jax.ShapeDtypeStruct((CAP, width), BF16)] * 4,
-        in_specs=[VMEM] * 2 + [HBM] * 3,
-        out_specs=[VMEM] * 4,
-        scratch_shapes=[
-            pltpu.VMEM((depth, units), BF16),
-            pltpu.VMEM((depth, units), BF16),
-            pltpu.VMEM((units, width), BF16),
-            pltpu.SemaphoreType.DMA((9,)),
-        ],
-        compiler_params=params(24),
+        out_shape=[jax.ShapeDtypeStruct(shape, F32), jax.ShapeDtypeStruct(shape, BF16)],
+        in_specs=[VMEM] * 5,
+        out_specs=[VMEM] * 2,
+        compiler_params=params(16),
         cost_estimate=pl.CostEstimate(
             flops=2 * 16 * 3 * depth * units, bytes_accessed=6 * 2**20, transcendentals=0
         ),
@@ -309,11 +351,25 @@
     )(own, far, gate, up, down)
 
 
-def merge_kernel(
-    got, value, project, mix, back_0, back_1, back_2, back_3, keep, send, project_in, sem
-):
-    copy = pltpu.make_async_copy(project, project_in, sem)
-    copy.start()
+def pair_kernel(keep, taken, *outs):
+    total = (keep[...] + taken[...].astype(F32)).astype(BF16)
+    for block, out in enumerate(outs):
+        out[...] = total[CAP * block : CAP * (block + 1)]
+
+
+def pair(keep, taken):
+    width = keep.shape[1]
+    return pl.pallas_call(
+        pair_kernel,
+        out_shape=[jax.ShapeDtypeStruct((CAP, width), BF16)] * 4,
+        in_specs=[VMEM] * 2,
+        out_specs=[VMEM] * 4,
+        compiler_params=params(8),
+        name="pair",
+    )(keep, taken)
+
+
+def merge_kernel(got, value, project, keep, send):
     peers, height, _ = got.shape
     heads = value.shape[0]
     chunk = ROWS * heads
@@ -346,7 +402,34 @@
         rows = merged[ROWS * head : ROWS * (head + 1)].astype(BF16)
         values.append(jnp.dot(rows, value[head], preferred_element_type=F32))
     head_values = jnp.concatenate(values, axis=1).astype(BF16)
-
+    attended = jnp.dot(head_values, project[...], preferred_element_type=F32)
+    span = keep.shape[2]
+    for peer in range(peers):
+        even = attended[:, 2 * peer * span : (2 * peer + 1) * span]
+        odd = attended[:, (2 * peer + 1) * span : (2 * peer + 2) * span]
+        keep[peer] = jnp.where(core == 1, odd, even)
+        send[peer] = jnp.where(core == 1, even, odd).astype(BF16)
+
+
+def merge(got, value, project, span):
+    peers = got.shape[0]
+    depth, width = project.shape
+    shape = (peers, ROWS, span)
+    return pl.pallas_call(
+        merge_kernel,
+        out_shape=[jax.ShapeDtypeStruct(shape, F32), jax.ShapeDtypeStruct(shape, BF16)],
+        in_specs=[VMEM] * 3,
+        out_specs=[VMEM] * 2,
+        compiler_params=params(16),
+        cost_estimate=pl.CostEstimate(
+            flops=2 * 8 * depth * width, bytes_accessed=6 * 2**20, transcendentals=0
+        ),
+        name="merge",
+    )(got, value, project)
+
+
+def finish_kernel(keep, taken, mix, back_0, back_1, back_2, back_3, out):
+    peers, _, span = keep.shape
     back = jnp.concatenate(
         [ref[...].astype(F32) for ref in (back_0, back_1, back_2, back_3)], axis=0
     ).astype(BF16)
@@ -356,33 +439,22 @@
     routed = jnp.dot(high, back, preferred_element_type=F32) + jnp.dot(
         low, back, preferred_element_type=F32
     )
-    copy.wait()
-    attended = jnp.dot(head_values, project_in[...], preferred_element_type=F32)
-    both = jnp.concatenate([attended, routed], axis=0)
-    span = keep.shape[2]
     for peer in range(peers):
-        even = both[:, 2 * peer * span : (2 * peer + 1) * span]
-        odd = both[:, (2 * peer + 1) * span : (2 * peer + 2) * span]
-        keep[peer] = jnp.where(core == 1, odd, even).astype(BF16)
-        send[peer] = jnp.where(core == 1, even, odd).astype(BF16)
-
-
-def merge(got, value, project, mix, back, span):
-    peers = got.shape[0]
-    depth, width = project.shape
-    shape = jax.ShapeDtypeStruct((peers, 2 * ROWS, span), BF16)
-    return pl.pallas_call(
-        merge_kernel,
-        out_shape=[shape, shape],
-        in_specs=[VMEM, VMEM, HBM, VMEM] + [VMEM] * 4,
-        out_specs=[VMEM] * 2,
-        scratch_shapes=[pltpu.VMEM((depth, width), BF16), pltpu.SemaphoreType.DMA],
-        compiler_params=params(24),
-        cost_estimate=pl.CostEstimate(
-            flops=2 * 8 * depth * width, bytes_accessed=6 * 2**20, transcendentals=0
-        ),
-        name="merge",
-    )(got, value, project, mix, *back)
+        attended = keep[peer] + taken[peer].astype(F32)
+        both = jnp.concatenate([attended, routed[:, peer * span : (peer + 1) * span]], axis=0)
+        out[peer] = both.astype(BF16)
+
+
+def finish(keep, taken, mix, back):
+    peers, rows, span = keep.shape
+    return pl.pallas_call(
+        finish_kernel,
+        out_shape=jax.ShapeDtypeStruct((peers, 2 * rows, span), BF16),
+        in_specs=[VMEM] * 7,
+        out_specs=VMEM,
+        compiler_params=params(8),
+        name="finish",
+    )(keep, taken, mix, *back)
 
 
 def shards(
@@ -436,12 +508,13 @@
     near = [send[0]] + [along_x(send[d], d) for d in range(1, group_count)]
     own = jnp.concatenate(near, axis=0)
     far = lax.ppermute(own, "c", swap)
-    routed = experts(own, far, w_gate, w_up, w_down)
+    gate, up, down, project, value = fetch(part, w_gate, w_up, w_down, w_out, w_value)
+    keep, give = experts(own, far, gate, up, down)
+    routed = pair(keep, lax.ppermute(give, "c", swap))
     back = [routed[0]] + [along_x(routed[d], -d) for d in range(1, group_count)]
 
-    keep, give = merge(got, w_value, w_out, mix, back, span)
-    taken = lax.ppermute(give, "c", swap)
-    terms = (keep.astype(F32) + taken.astype(F32)).astype(BF16)
+    keep, give = merge(got, value, project, span)
+    terms = finish(keep, lax.ppermute(give, "c", swap), mix, back)
     arrived = lax.all_to_all(terms, plane, 0, 0, tiled=True)
     summed = jnp.sum(arrived.astype(F32), axis=0).astype(BF16)
     return (summed[:requests], summed[requests:])

time: 106 us -> 96.1 us (0.907)
  local copies, waits for them, and re-layouts: 12.8 us -> 4.4 us
  waiting for transfers between devices: 25.7 us -> 21.9 us
  starting transfers between devices: 32.8 us -> 35.4 us
  blocking collectives: 18.5 us -> 16.1 us
  Pallas kernels: 14.7 us -> 16.1 us
    unnamed x26 -> x6, local copies, waits for them, and re-layouts: 12.2 us -> 3.81 us
    all_to_all x1, blocking collectives: 18.5 us -> 16.1 us  [shards(): arrived = lax.all_to_all(terms, plane, 0, 0, tiled=True)]
    ppermute x6, waiting for transfers between devices: 6.66 us -> 4.77 us  [along_x(): lax.ppermute(value, 'x', [(i, (i + shift) % group_count) for i in range(g...]
    pallas_call x1, Pallas kernels: 5.74 us -> 7.58 us  [attention(): pl.pallas_call(lambda *refs: attention_kernel(*refs, scale=scale, units=u...]
    ppermute x1 -> x2, starting transfers between devices: 1.6 us -> 3.05 us  [the longest x1 2.95 us: shards(): terms = finish(keep, lax.ppermute(give, 'c', swap), mix, back)]
    ppermute x6, starting transfers between devices: 8.01 us -> 9.18 us  [along_x(): lax.ppermute(value, 'x', [(i, (i + shift) % group_count) for i in range(g...]
    pallas_call x2 -> x5, Pallas kernels: 8.02 us -> 6.88 us  [the longest x1 3.74 us: fetch(): pl.pallas_call(fetch_kernel, out_shape=[pltpu.VMEM(weight.shape, weight.d...]
  transfers between devices with their start and end apart: 12 -> 13, of which waited for: 9 -> 5; matrix products, arithmetic and copies ran while one was open for 0% -> 0% of each run, Pallas kernels for 5% -> 9%
where the time goes in v3:
time: 96.1 us; the launch traced here: 94.8 us
  starting transfers between devices  35.4 us (37%)
  waiting for transfers between devices  21.9 us (23%)
  Pallas kernels  16.1 us (17%)
  blocking collectives  16.1 us (17%)
  local copies, waits for them, and re-layouts  4.4 us (5%)
    all_to_all x1, blocking collectives, shards(): arrived = lax.all_to_all(terms, plane, 0, 0, tiled=True)  16.1 us
    all_to_all x1, waiting for transfers between devices, shards(): lax.all_to_all(payload(query_lat, query_rope, moe_tokens, peers), plane,...  15.9 us
    all_to_all x1, starting transfers between devices, shards(): lax.all_to_all(payload(query_lat, query_rope, moe_tokens, peers), plane,...  9.47 us
    ppermute x6, starting transfers between devices, along_x(): lax.ppermute(value, 'x', [(i, (i + shift) % group_count) for i in range(g...  9.18 us
    pallas_call x1, Pallas kernels, attention(): pl.pallas_call(lambda *refs: attention_kernel(*refs, scale=scale, units=u...  7.58 us
    all_to_all x1, starting transfers between devices, shards(): got = lax.all_to_all(part, plane, 0, 0, tiled=True)  7.51 us
    ppermute x6, waiting for transfers between devices, along_x(): lax.ppermute(value, 'x', [(i, (i + shift) % group_count) for i in range(g...  4.77 us
    unnamed x6, local copies, waits for them, and re-layouts  3.81 us
  transfers between devices with their start and end apart: 13, of which 5 were waited for; matrix products, arithmetic and copies ran while one was open for 0% of the time, Pallas kernels for 9%

profile of v3, /device:TPU:1, one launch (start us, length us, event | category | flops | bytes accessed | tf_op | source)
XLA Modules:
  0.0 94.8 jit_solution(16373665739858577185)
XLA Ops:
  0.6 3.3 %collective-permute-start = (bf16[8,256,512]{2,1,0:T(8,128)(2,1)}, bf16[8,256,512]{2,1,0:T(8,128)(2,1)S(1)}, u32[]{:S(2)}, u32[]{:S(2)}) collective-permute-start(bf16[8,256,512]{2,1,0:T(8,128)(2,1)} %refs_2_.2), channel_id=1, source_target_pairs={{0,1},{1,0},{2,3},{3,2},{4,5},{5,4},{6,7},{7,6},{8,9},{9,8},{10,11... | collective-permute-start | bytes 6291464 | tf_op jit(solution)/shard_map/ppermute | solution.py:490
  4.0 1.7 %payload.1 = bf16[32,16,640]{2,1,0:T(8,128)(2,1)} custom-call(bf16[8,2,512]{2,1,0:T(2,128)(2,1)} %query_lat.1, bf16[8,2,64]{2,1,0:T(2,128)(2,1)} %query_rope.1, bf16[8,112]{1,0:T(8,128)(2,1)} %tokens.1), custom_call_target="tpu_custom_call" | custom-call | tf_op jit(solution)/shard_map/payload/pallas_call | solution.py:58
  5.7 9.5 %all-to-all-start = ((bf16[32,16,640]{2,1,0:T(8,128)(2,1)}), bf16[32,16,640]{2,1,0:T(8,128)(2,1)S(1)}, u32[]{:S(2)}, u32[]{:S(2)}) async-start(bf16[32,16,640]{2,1,0:T(8,128)(2,1)} %payload.1), calls=%async_computation | async-start | bytes 1310720 | tf_op jit(solution)/shard_map/all_to_all | solution.py:487
  15.5 1.2 %collective-permute-done.1.refs_5_ = bf16[8,64,256]{2,1,0:T(8,128)(2,1)S(1)} collective-permute-done((bf16[8,64,256]{2,1,0:T(8,128)(2,1)S(1)}, bf16[8,64,256]{2,1,0:T(8,128)(2,1)S(1)}, u32[]{:S(2)}, u32[]{:S(2)}) %collective-permute-start.1) | collective-permute-done | bytes 262176 | tf_op jit(solution)/shard_map/ppermute | solution.py:491
  16.8 15.9 %all-to-all-done.refs_1_ = bf16[32,16,640]{2,1,0:T(8,128)(2,1)S(1)} async-done(((bf16[32,16,640]{2,1,0:T(8,128)(2,1)}), bf16[32,16,640]{2,1,0:T(8,128)(2,1)S(1)}, u32[]{:S(2)}, u32[]{:S(2)}) %all-to-all-start) | async-done | bytes 655392 | tf_op jit(solution)/shard_map/all_to_all | solution.py:487
  32.6 7.6 %attention.1 = (bf16[32,72,128]{2,1,0:T(8,128)(2,1)}, bf16[4,3584]{1,0:T(4,128)(2,1)S(1)}, bf16[4,3584]{1,0:T(4,128)(2,1)S(1)}, bf16[4,3584]{1,0:T(4,128)(2,1)S(...) custom-call(s32[8]{0:T(128)} %refs_0_.2, bf16[32,16,640]{2,1,0:T(8,128)(2,1)S(1)} %all-to-all-done.refs_1_, ...), custom_call_target="tpu_custom_call" | custom-call | flops 570425344 | bytes 6291456 | tf_op jit(solution)/shard_map/attention/pallas_call | solution.py:234
  40.2 7.5 %all-to-all-start.1 = ((bf16[32,72,128]{2,1,0:T(8,128)(2,1)}), bf16[32,72,128]{2,1,0:T(8,128)(2,1)S(1)}, u32[]{:S(2)}, u32[]{:S(2)}) async-start(bf16[32,72,128]{2,1,0:T(8,128)(2,1)} %get-tuple-element.21.after), calls=%async_computation.1 | async-start | bytes 1179648 | tf_op jit(solution)/shard_map/all_to_all | solution.py:506
  47.8 1.3 %collective-permute-start.3 = (bf16[4,3584]{1,0:T(4,128)(2,1)S(1)}, bf16[4,3584]{1,0:T(4,128)(2,1)S(1)}, u32[]{:S(2)}, u32[]{:S(2)}) collective-permute-start(bf16[4,3584]{1,0:T(4,128)(2,1)S(1)} %get-tuple-element.28), channel_id=1, source_target_pairs={{0,64},{64,128},{128,192},{192,0},{1,65},{65,129},{129,193},{193,1... | collective-permute-start | bytes 86024 | tf_op jit(solution)/shard_map/ppermute | solution.py:483
  49.0 2.4 %collective-permute-start.4 = (bf16[4,3584]{1,0:T(4,128)(2,1)S(1)}, bf16[4,3584]{1,0:T(4,128)(2,1)S(1)}, u32[]{:S(2)}, u32[]{:S(2)}) collective-permute-start(bf16[4,3584]{1,0:T(4,128)(2,1)S(1)} %get-tuple-element.29), channel_id=1, source_target_pairs={{0,128},{64,192},{128,0},{192,64},{1,129},{65,193},{129,1},{193,65... | collective-permute-start | bytes 86024 | tf_op jit(solution)/shard_map/ppermute | solution.py:483
  51.5 1.2 %collective-permute-start.5 = (bf16[4,3584]{1,0:T(4,128)(2,1)S(1)}, bf16[4,3584]{1,0:T(4,128)(2,1)S(1)}, u32[]{:S(2)}, u32[]{:S(2)}) collective-permute-start(bf16[4,3584]{1,0:T(4,128)(2,1)S(1)} %get-tuple-element.30), channel_id=1, source_target_pairs={{0,192},{64,0},{128,64},{192,128},{1,193},{65,1},{129,65},{193,129... | collective-permute-start | bytes 86024 | tf_op jit(solution)/shard_map/ppermute | solution.py:483
  52.7 0.6 collective-permute-done.4
  53.3 1.4 %collective-permute-done.5 = bf16[4,3584]{1,0:T(4,128)(2,1)S(1)} collective-permute-done((bf16[4,3584]{1,0:T(4,128)(2,1)S(1)}, bf16[4,3584]{1,0:T(4,128)(2,1)S(1)}, u32[]{:S(2)}, u32[]{:S(2)}) %collective-permute-start.5) | collective-permute-done | bytes 28704 | tf_op jit(solution)/shard_map/ppermute | solution.py:483
  54.8 2.5 %collective-permute-start.6 = (bf16[16,3584]{1,0:T(8,128)(2,1)S(1)}, bf16[16,3584]{1,0:T(8,128)(2,1)S(1)}, u32[]{:S(2)}, u32[]{:S(2)}) collective-permute-start(bf16[16,3584]{1,0:T(8,128)(2,1)S(1)} %pad_maximum_fusion.own), channel_id=1, source_target_pairs={{0,1},{1,0},{2,3},{3,2},{4,5},{5,4},{6,7},{7,6},{8,9},{9,8},{10,11... | collective-permute-start | bytes 344072 | tf_op jit(solution)/shard_map/ppermute | solution.py:510
  57.3 3.7 %fetch.1 = (bf16[7168,128]{1,0:T(8,128)(2,1)S(1)}, bf16[7168,128]{1,0:T(8,128)(2,1)S(1)}, bf16[128,7168]{1,0:T(8,128)(2,1)S(1)}, bf16[256,7168]{1,0:T(8,128)(2,1)S(1)}, bf16[2,512,128]{2,1,0:T(8,128)(2,1)S(1)}) custom-call(bf16[32,72,128]{2,1,0:T(8,128)(2,1)} %get-tuple-element.21.after, bf16[7168,128]{1,0:T(8,128)(2,1)} %refs_0_.3, ...), custom_call_target="tpu_custom_call" | custom-call | bytes 10485760 | tf_op jit(solution)/shard_map/fetch/pallas_call | solution.py:278
  61.1 1.8 %copy-done = bf16[256,7168]{1,0:T(8,128)(2,1)} copy-done((bf16[256,7168]{1,0:T(8,128)(2,1)}, bf16[256,7168]{1,0:T(8,128)(2,1)S(1)}, u32[]{:S(2)}) %copy-start) | copy-done | bytes 3670040
  62.8 1.7 %experts.1 = (f32[16,3584]{1,0:T(8,128)S(1)}, bf16[16,3584]{1,0:T(8,128)(2,1)S(1)}) custom-call(bf16[16,3584]{1,0:T(8,128)(2,1)S(1)} %pad_maximum_fusion.own, bf16[16,3584]{1,0:T(8,128)(2,1)S(1)} %collective-permute-done.6.far, bf16[7168,128]{1,0:T(8,128)(2,1)S(1)} %get-tuple-element.31.gate, bf16[7168,128]{1,0:T(8,128)(2,1)S(1)} %get-tuple-element.32.up, ...), custom_call_target="tpu_custom_call" | custom-call | flops 88080384 | bytes 6291456 | tf_op jit(solution)/shard_map/experts/pallas_call | solution.py:341
  64.6 2.0 %copy-done.1 = bf16[256,7168]{1,0:T(8,128)(2,1)S(1)} copy-done((bf16[256,7168]{1,0:T(8,128)(2,1)S(1)}, bf16[256,7168]{1,0:T(8,128)(2,1)}, u32[]{:S(2)}) %copy-start.1) | copy-done | bytes 3670040
  66.7 1.2 %merge.1 = (f32[32,8,112]{2,1,0:T(8,128)S(1)}, bf16[32,8,112]{2,1,0:T(8,128)(2,1)S(1)}) custom-call(bf16[32,72,128]{2,1,0:T(8,128)(2,1)S(1)} %all-to-all-done.1.got, bf16[2,512,128]{2,1,0:T(8,128)(2,1)S(1)} %get-tuple-element.22.value, bf16[256,7168]{1,0:T(8,128)(2,1)S(1)} %copy-done.1), custom_call_target="tpu_custom_call" | custom-call | flops 29360128 | bytes 6291456 | tf_op jit(solution)/shard_map/merge/pallas_call | solution.py:418
  67.8 3.0 %collective-permute-start.2 = (bf16[32,8,112]{2,1,0:T(8,128)(2,1)S(1)}, bf16[32,8,112]{2,1,0:T(8,128)(2,1)S(1)}, u32[]{:S(2)}, u32[]{:S(2)}) collective-permute-start(bf16[32,8,112]{2,1,0:T(8,128)(2,1)S(1)} %get-tuple-element.25), channel_id=1, source_target_pairs={{0,1},{1,0},{2,3},{3,2},{4,5},{5,4},{6,7},{7,6},{8,9},{9,8},{10,11... | collective-permute-start | bytes 172040 | tf_op jit(solution)/shard_map/ppermute | solution.py:517
  70.8 1.3 %collective-permute-start.10 = (bf16[4,3584]{1,0:T(4,128)(2,1)S(1)}, bf16[4,3584]{1,0:T(4,128)(2,1)S(1)}, u32[]{:S(2)}, u32[]{:S(2)}) collective-permute-start(bf16[4,3584]{1,0:T(4,128)(2,1)S(1)} %get-tuple-element.39), channel_id=1, source_target_pairs={{0,64},{64,128},{128,192},{192,0},{1,65},{65,129},{129,193},{193,1... | collective-permute-start | bytes 86024 | tf_op jit(solution)/shard_map/ppermute | solution.py:483
  72.1 1.5 %collective-permute-start.8 = (bf16[4,3584]{1,0:T(4,128)(2,1)S(1)}, bf16[4,3584]{1,0:T(4,128)(2,1)S(1)}, u32[]{:S(2)}, u32[]{:S(2)}) collective-permute-start(bf16[4,3584]{1,0:T(4,128)(2,1)S(1)} %get-tuple-element.37), channel_id=1, source_target_pairs={{0,192},{64,0},{128,64},{192,128},{1,193},{65,1},{129,65},{193,129... | collective-permute-start | bytes 86024 | tf_op jit(solution)/shard_map/ppermute | solution.py:483
  73.6 1.5 %collective-permute-start.9 = (bf16[4,3584]{1,0:T(4,128)(2,1)S(1)}, bf16[4,3584]{1,0:T(4,128)(2,1)S(1)}, u32[]{:S(2)}, u32[]{:S(2)}) collective-permute-start(bf16[4,3584]{1,0:T(4,128)(2,1)S(1)} %get-tuple-element.38), channel_id=1, source_target_pairs={{0,128},{64,192},{128,0},{192,64},{1,129},{65,193},{129,1},{193,65... | collective-permute-start | bytes 86024 | tf_op jit(solution)/shard_map/ppermute | solution.py:483
  75.1 2.7 %collective-permute-done.9.back_2 = bf16[4,3584]{1,0:T(4,128)(2,1)S(1)} collective-permute-done((bf16[4,3584]{1,0:T(4,128)(2,1)S(1)}, bf16[4,3584]{1,0:T(4,128)(2,1)S(1)}, u32[]{:S(2)}, u32[]{:S(2)}) %collective-permute-start.9) | collective-permute-done | bytes 28704 | tf_op jit(solution)/shard_map/ppermute | solution.py:483
  78.1 16.1 %all_to_all.15 = bf16[32,16,112]{2,1,0:T(8,128)(2,1)S(1)} all-to-all(bf16[32,16,112]{2,1,0:T(8,128)(2,1)S(1)} %finish.1), channel_id=1, replica_groups=mesh['x'=4,'y'=4,'z'=8,'c'=2] {'y','z'}, dimensions={0} | all-to-all | bytes 229376 | tf_op jit(solution)/shard_map/all_to_all | solution.py:518
  (19 shorter events, 1.5 us)
Async XLA Ops:
  0.6 14.5 %copy-start.2 = (bf16[8,64,256]{2,1,0:T(8,128)(2,1)S(1)}, bf16[8,64,256]{2,1,0:T(8,128)(2,1)}, u32[]{:S(2)}) copy-start(bf16[8,64,256]{2,1,0:T(8,128)(2,1)} %refs_4_.2) | copy-start | bytes 786436
  0.6 32.0 %collective-permute-start = (bf16[8,256,512]{2,1,0:T(8,128)(2,1)}, bf16[8,256,512]{2,1,0:T(8,128)(2,1)S(1)}, u32[]{:S(2)}, u32[]{:S(2)}) collective-permute-start(bf16[8,256,512]{2,1,0:T(8,128)(2,1)} %refs_2_.2), channel_id=1, source_target_pairs={{0,1},{1,0},{2,3},{3,2},{4,5},{5,4},{6,7},{7,6},{8,9},{9,8},{10,11... | collective-permute-start | bytes 6291464 | tf_op jit(solution)/shard_map/ppermute | solution.py:490
  5.7 27.0 %all-to-all-start = ((bf16[32,16,640]{2,1,0:T(8,128)(2,1)}), bf16[32,16,640]{2,1,0:T(8,128)(2,1)S(1)}, u32[]{:S(2)}, u32[]{:S(2)}) async-start(bf16[32,16,640]{2,1,0:T(8,128)(2,1)} %payload.1), calls=%async_computation | async-start | bytes 1310720 | tf_op jit(solution)/shard_map/all_to_all | solution.py:487
  15.1 1.6 %collective-permute-start.1 = (bf16[8,64,256]{2,1,0:T(8,128)(2,1)S(1)}, bf16[8,64,256]{2,1,0:T(8,128)(2,1)S(1)}, u32[]{:S(2)}, u32[]{:S(2)}) collective-permute-start(bf16[8,64,256]{2,1,0:T(8,128)(2,1)S(1)} %copy-done.2), channel_id=1, source_target_pairs={{0,1},{1,0},{2,3},{3,2},{4,5},{5,4},{6,7},{7,6},{8,9},{9,8},{10,11... | collective-permute-start | bytes 786440 | tf_op jit(solution)/shard_map/ppermute | solution.py:491
  40.2 24.4 %all-to-all-start.1 = ((bf16[32,72,128]{2,1,0:T(8,128)(2,1)}), bf16[32,72,128]{2,1,0:T(8,128)(2,1)S(1)}, u32[]{:S(2)}, u32[]{:S(2)}) async-start(bf16[32,72,128]{2,1,0:T(8,128)(2,1)} %get-tuple-element.21.after), calls=%async_computation.1 | async-start | bytes 1179648 | tf_op jit(solution)/shard_map/all_to_all | solution.py:506
  47.8 4.9 %collective-permute-start.3 = (bf16[4,3584]{1,0:T(4,128)(2,1)S(1)}, bf16[4,3584]{1,0:T(4,128)(2,1)S(1)}, u32[]{:S(2)}, u32[]{:S(2)}) collective-permute-start(bf16[4,3584]{1,0:T(4,128)(2,1)S(1)} %get-tuple-element.28), channel_id=1, source_target_pairs={{0,64},{64,128},{128,192},{192,0},{1,65},{65,129},{129,193},{193,1... | collective-permute-start | bytes 86024 | tf_op jit(solution)/shard_map/ppermute | solution.py:483
  49.0 4.2 %collective-permute-start.4 = (bf16[4,3584]{1,0:T(4,128)(2,1)S(1)}, bf16[4,3584]{1,0:T(4,128)(2,1)S(1)}, u32[]{:S(2)}, u32[]{:S(2)}) collective-permute-start(bf16[4,3584]{1,0:T(4,128)(2,1)S(1)} %get-tuple-element.29), channel_id=1, source_target_pairs={{0,128},{64,192},{128,0},{192,64},{1,129},{65,193},{129,1},{193,65... | collective-permute-start | bytes 86024 | tf_op jit(solution)/shard_map/ppermute | solution.py:483
  51.5 3.2 %collective-permute-start.5 = (bf16[4,3584]{1,0:T(4,128)(2,1)S(1)}, bf16[4,3584]{1,0:T(4,128)(2,1)S(1)}, u32[]{:S(2)}, u32[]{:S(2)}) collective-permute-start(bf16[4,3584]{1,0:T(4,128)(2,1)S(1)} %get-tuple-element.30), channel_id=1, source_target_pairs={{0,192},{64,0},{128,64},{192,128},{1,193},{65,1},{129,65},{193,129... | collective-permute-start | bytes 86024 | tf_op jit(solution)/shard_map/ppermute | solution.py:483
  54.8 8.0 %collective-permute-start.6 = (bf16[16,3584]{1,0:T(8,128)(2,1)S(1)}, bf16[16,3584]{1,0:T(8,128)(2,1)S(1)}, u32[]{:S(2)}, u32[]{:S(2)}) collective-permute-start(bf16[16,3584]{1,0:T(8,128)(2,1)S(1)} %pad_maximum_fusion.own), channel_id=1, source_target_pairs={{0,1},{1,0},{2,3},{3,2},{4,5},{5,4},{6,7},{7,6},{8,9},{9,8},{10,11... | collective-permute-start | bytes 344072 | tf_op jit(solution)/shard_map/ppermute | solution.py:510
  61.1 1.8 %copy-start = (bf16[256,7168]{1,0:T(8,128)(2,1)}, bf16[256,7168]{1,0:T(8,128)(2,1)S(1)}, u32[]{:S(2)}) copy-start(bf16[256,7168]{1,0:T(8,128)(2,1)S(1)} %get-tuple-element.23.project) | copy-start | bytes 11010052
  64.5 6.3 %collective-permute-start.7 = (bf16[16,3584]{1,0:T(8,128)(2,1)S(1)}, bf16[16,3584]{1,0:T(8,128)(2,1)S(1)}, u32[]{:S(2)}, u32[]{:S(2)}) collective-permute-start(bf16[16,3584]{1,0:T(8,128)(2,1)S(1)} %get-tuple-element.35), channel_id=1, source_target_pairs={{0,1},{1,0},{2,3},{3,2},{4,5},{5,4},{6,7},{7,6},{8,9},{9,8},{10,11... | collective-permute-start | bytes 344072 | tf_op jit(solution)/shard_map/ppermute | solution.py:513
  64.6 2.0 %copy-start.1 = (bf16[256,7168]{1,0:T(8,128)(2,1)S(1)}, bf16[256,7168]{1,0:T(8,128)(2,1)}, u32[]{:S(2)}) copy-start(bf16[256,7168]{1,0:T(8,128)(2,1)} %copy-done) | copy-start | bytes 11010052
  67.8 10.0 %collective-permute-start.2 = (bf16[32,8,112]{2,1,0:T(8,128)(2,1)S(1)}, bf16[32,8,112]{2,1,0:T(8,128)(2,1)S(1)}, u32[]{:S(2)}, u32[]{:S(2)}) collective-permute-start(bf16[32,8,112]{2,1,0:T(8,128)(2,1)S(1)} %get-tuple-element.25), channel_id=1, source_target_pairs={{0,1},{1,0},{2,3},{3,2},{4,5},{5,4},{6,7},{7,6},{8,9},{9,8},{10,11... | collective-permute-start | bytes 172040 | tf_op jit(solution)/shard_map/ppermute | solution.py:517
  70.8 4.3 %collective-permute-start.10 = (bf16[4,3584]{1,0:T(4,128)(2,1)S(1)}, bf16[4,3584]{1,0:T(4,128)(2,1)S(1)}, u32[]{:S(2)}, u32[]{:S(2)}) collective-permute-start(bf16[4,3584]{1,0:T(4,128)(2,1)S(1)} %get-tuple-element.39), channel_id=1, source_target_pairs={{0,64},{64,128},{128,192},{192,0},{1,65},{65,129},{129,193},{193,1... | collective-permute-start | bytes 86024 | tf_op jit(solution)/shard_map/ppermute | solution.py:483
  72.1 3.0 %collective-permute-start.8 = (bf16[4,3584]{1,0:T(4,128)(2,1)S(1)}, bf16[4,3584]{1,0:T(4,128)(2,1)S(1)}, u32[]{:S(2)}, u32[]{:S(2)}) collective-permute-start(bf16[4,3584]{1,0:T(4,128)(2,1)S(1)} %get-tuple-element.37), channel_id=1, source_target_pairs={{0,192},{64,0},{128,64},{192,128},{1,193},{65,1},{129,65},{193,129... | collective-permute-start | bytes 86024 | tf_op jit(solution)/shard_map/ppermute | solution.py:483
  73.6 4.2 %collective-permute-start.9 = (bf16[4,3584]{1,0:T(4,128)(2,1)S(1)}, bf16[4,3584]{1,0:T(4,128)(2,1)S(1)}, u32[]{:S(2)}, u32[]{:S(2)}) collective-permute-start(bf16[4,3584]{1,0:T(4,128)(2,1)S(1)} %get-tuple-element.38), channel_id=1, source_target_pairs={{0,128},{64,192},{128,0},{192,64},{1,129},{65,193},{129,1},{193,65... | collective-permute-start | bytes 86024 | tf_op jit(solution)/shard_map/ppermute | solution.py:483

commit v4 on v3

--- a/solution.py
+++ b/solution.py
@@ -33,14 +33,24 @@
     return pltpu.CompilerParams(vmem_limit_bytes=mebibytes * 2**20)
 
 
-def payload_kernel(query_lat, query_rope, tokens, out):
+def payload_kernel(query_lat, query_rope, tokens, out, lat_in, rope_in, tokens_in, sems):
+    copies = [
+        pltpu.make_async_copy(source, target, sems.at[index])
+        for index, (source, target) in enumerate(
+            ((query_lat, lat_in), (query_rope, rope_in), (tokens, tokens_in))
+        )
+    ]
+    for copy in copies:
+        copy.start()
+    for copy in copies:
+        copy.wait()
     peers = out.shape[0]
     latent, rope = query_lat.shape[2], query_rope.shape[2]
     heads = query_lat.shape[1]
     half = tokens.shape[1] // heads
-    lat = query_lat[...].astype(F32)
-    rot = query_rope[...].astype(F32)
-    tok = tokens[...].astype(F32)
+    lat = lat_in[...].astype(F32)
+    rot = rope_in[...].astype(F32)
+    tok = tokens_in[...].astype(F32)
     spare = jnp.zeros((ROWS, out.shape[2] - latent - rope - half), F32)
     rows = []
     for head in range(heads):
@@ -58,8 +68,14 @@
     return pl.pallas_call(
         payload_kernel,
         out_shape=jax.ShapeDtypeStruct((peers, heads * requests, latent + LANES), BF16),
-        in_specs=[VMEM] * 3,
+        in_specs=[HBM] * 3,
         out_specs=VMEM,
+        scratch_shapes=[
+            pltpu.VMEM(query_lat.shape, BF16),
+            pltpu.VMEM(query_rope.shape, BF16),
+            pltpu.VMEM(tokens.shape, BF16),
+            pltpu.SemaphoreType.DMA((3,)),
+        ],
         compiler_params=params(20),
         name="payload",
     )(*pinned(query_lat, query_rope, tokens))
@@ -97,16 +113,13 @@
     peers, chunk, width = query.shape
     requests, positions, latent = lat_own.shape
     small = [
-        pltpu.make_async_copy(lengths, lengths_in, sems.at[requests]),
-        pltpu.make_async_copy(rope_own, rope_in, sems.at[requests + 1]),
-        pltpu.make_async_copy(ids, ids_in, sems.at[requests + 2]),
-        pltpu.make_async_copy(route, route_in, sems.at[requests + 3]),
+        pltpu.make_async_copy(lengths, lengths_in, sems.at[0]),
+        pltpu.make_async_copy(rope_own, rope_in, sems.at[1]),
+        pltpu.make_async_copy(ids, ids_in, sems.at[2]),
+        pltpu.make_async_copy(route, route_in, sems.at[3]),
     ]
-    large = [
-        pltpu.make_async_copy(lat_own.at[request], lat_in.at[request], sems.at[request])
-        for request in range(requests)
-    ]
-    for copy in small[:2] + large + small[2:]:
+    large = pltpu.make_async_copy(lat_own, lat_in, sems.at[4])
+    for copy in small[2:] + small[:2] + [large]:
         copy.start()
     rope = rope_own.shape[1]
     tiles = latent // LANES
@@ -120,16 +133,56 @@
         piece = query[:, :, tile * LANES : (tile + 1) * LANES].astype(F32)
         query_rows[tile] = piece.reshape(peers * chunk, LANES)
 
+    half = token_rows.shape[1] // (peers * heads)
+    for peer in range(peers):
+        begin = peer * chunk
+        pieces = [
+            query_rows[tiles, begin + requests * head : begin + requests * (head + 1), :][
+                :, rope : rope + half
+            ]
+            for head in range(heads)
+        ]
+        token_rows[:, peer * heads * half : (peer + 1) * heads * half] = jnp.concatenate(
+            pieces, axis=1
+        )
+    tokens = token_rows[...].astype(BF16)
+    small[2].wait()
+    small[3].wait()
+    named = ids_in[...]
+    strength = route_in[...]
+    lower = (
+        lax.broadcasted_iota(jnp.int32, (ROWS, ROWS), 1)
+        < lax.broadcasted_iota(jnp.int32, (ROWS, ROWS), 0)
+    ).astype(F32)
+    slot_lane = lax.broadcasted_iota(jnp.int32, (ROWS, LANES), 1)
+    placing = jnp.zeros((ROWS, LANES), F32)
+    mix = jnp.zeros((ROWS, LANES), F32)
+    for step in range(4):
+        expert = (lax.rem(group + step, groups) * shards_here + shard) * units // FF
+        hit = named == expert
+        chosen = jnp.max(jnp.where(hit, 1.0, 0.0), axis=1, keepdims=True)
+        weight = jnp.sum(jnp.where(hit, strength, 0.0), axis=1, keepdims=True)
+        chosen_wide = jnp.broadcast_to(chosen, (ROWS, LANES))
+        rank = jnp.dot(lower, chosen_wide, preferred_element_type=F32)
+        picked = (rank == (slot_lane - CAP * step).astype(F32)) & (chosen_wide > 0.0)
+        picked = picked & (slot_lane >= CAP * step) & (slot_lane < CAP * (step + 1))
+        placing = jnp.where(picked, 1.0, placing)
+        mix = jnp.where(picked, weight, mix)
+    mix_out[...] = mix
+    select = placing.T[: 4 * CAP, :].astype(BF16)
+    chosen_rows = jnp.dot(select, tokens, preferred_element_type=F32).astype(BF16)
+    for step, send in enumerate((send_0, send_1, send_2, send_3)):
+        send[...] = chosen_rows[CAP * step : CAP * (step + 1)]
+
     lane = lax.broadcasted_iota(jnp.int32, (rows, LANES), 1)
     stats = jnp.zeros((rows, LANES), F32)
     base_own = shard * positions
     base_far = (shard + 1 - 2 * core) * positions
     place = lax.broadcasted_iota(jnp.int32, (rows, positions), 1)
     small[0].wait()
+    small[1].wait()
+    large.wait()
     for request in range(requests):
-        if request == 0:
-            small[1].wait()
-        large[request].wait()
         mine = jnp.concatenate(
             [
                 jnp.concatenate(
@@ -165,7 +218,7 @@
         weighted = jnp.dot(
             weights[0].astype(BF16), lat_in[request], preferred_element_type=F32
         ) + jnp.dot(weights[1].astype(BF16), lat_far[request], preferred_element_type=F32)
-        partial = weighted / jnp.maximum(total, 1.0)
+        partial = weighted * (1.0 / jnp.maximum(total, 1.0))
         for index, term in enumerate(three_terms(top) + three_terms(total)):
             stats = jnp.where(lane == ROWS * request + index, term, stats)
         for head in range(heads):
@@ -182,47 +235,6 @@
     for head in range(heads):
         stat_rows[pl.ds(head, peers, stride=ROWS), :] = stats[peers * head : peers * (head + 1)]
     out[:, tiles * chunk :, :] = stat_rows[...].reshape(peers, ROWS, LANES).astype(BF16)
-
-    half = token_rows.shape[1] // (peers * heads)
-    for peer in range(peers):
-        begin = peer * chunk
-        pieces = [
-            query_rows[tiles, begin + requests * head : begin + requests * (head + 1), :][
-                :, rope : rope + half
-            ]
-            for head in range(heads)
-        ]
-        token_rows[:, peer * heads * half : (peer + 1) * heads * half] = jnp.concatenate(
-            pieces, axis=1
-        )
-    tokens = token_rows[...].astype(BF16)
-    small[2].wait()
-    small[3].wait()
-    named = ids_in[...]
-    strength = route_in[...]
-    lower = (
-        lax.broadcasted_iota(jnp.int32, (ROWS, ROWS), 1)
-        < lax.broadcasted_iota(jnp.int32, (ROWS, ROWS), 0)
-    ).astype(F32)
-    slot_lane = lax.broadcasted_iota(jnp.int32, (ROWS, LANES), 1)
-    placing = jnp.zeros((ROWS, LANES), F32)
-    mix = jnp.zeros((ROWS, LANES), F32)
-    for step in range(4):
-        expert = (lax.rem(group + step, groups) * shards_here + shard) * units // FF
-        hit = named == expert
-        chosen = jnp.max(jnp.where(hit, 1.0, 0.0), axis=1, keepdims=True)
-        weight = jnp.sum(jnp.where(hit, strength, 0.0), axis=1, keepdims=True)
-        chosen_wide = jnp.broadcast_to(chosen, (ROWS, LANES))
-        rank = jnp.dot(lower, chosen_wide, preferred_element_type=F32)
-        picked = (rank == (slot_lane - CAP * step).astype(F32)) & (chosen_wide > 0.0)
-        picked = picked & (slot_lane >= CAP * step) & (slot_lane < CAP * (step + 1))
-        placing = jnp.where(picked, 1.0, placing)
-        mix = jnp.where(picked, weight, mix)
-    mix_out[...] = mix
-    select = placing.T[: 4 * CAP, :].astype(BF16)
-    chosen_rows = jnp.dot(select, tokens, preferred_element_type=F32).astype(BF16)
-    for step, send in enumerate((send_0, send_1, send_2, send_3)):
-        send[...] = chosen_rows[CAP * step : CAP * (step + 1)]
 
 
 def attention(lengths, query, lat_own, lat_far, rope_own, rope_far, ids, route, scale, span, units):
@@ -248,7 +260,7 @@
             pltpu.VMEM(rope_own.shape, BF16),
             pltpu.VMEM(ids.shape, jnp.int32),
             pltpu.VMEM(route.shape, F32),
-            pltpu.SemaphoreType.DMA((requests + 4,)),
+            pltpu.SemaphoreType.DMA((5,)),
         ],
         compiler_params=params(24),
         cost_estimate=pl.CostEstimate(
@@ -260,45 +272,34 @@
     )(lengths, query, lat_own, lat_far, rope_own, rope_far, ids, route)
 
 
-def fetch_kernel(after, *refs):
-    del after
-    count = len(refs) // 2
-    sems = refs[-1]
-    copies = [
-        pltpu.make_async_copy(refs[index], refs[count + index], sems.at[index])
-        for index in range(count)
-    ]
-    for copy in copies:
-        copy.start()
-    for copy in copies:
-        copy.wait()
-
-
-def fetch(after, *weights):
-    return pl.pallas_call(
-        fetch_kernel,
-        out_shape=[pltpu.VMEM(weight.shape, weight.dtype) for weight in weights],
-        in_specs=[pl.BlockSpec(memory_space=pl.ANY)] + [HBM] * len(weights),
-        out_specs=[VMEM] * len(weights),
-        scratch_shapes=[pltpu.SemaphoreType.DMA((len(weights),))],
-        compiler_params=params(1),
-        cost_estimate=pl.CostEstimate(flops=0, bytes_accessed=10 * 2**20, transcendentals=0),
-        name="fetch",
-    )(after, *pinned(*weights))
-
-
-def experts_kernel(own, far, gate, up, down, keep, send):
+def experts_kernel(own, far, gate, up, down, keep, send, gate_in, up_in, down_in, sems):
     depth, units = gate.shape
     width = down.shape[1]
     span = 112
     blocks = depth // (2 * span)
     core = lax.axis_index("c")
     each = 8
+    copies = []
+    for index in range(blocks // each):
+        rows = pl.ds(2 * span * each * index, 2 * span * each)
+        copies.append(
+            [
+                pltpu.make_async_copy(
+                    source.at[rows, :], target.at[rows, :], sems.at[2 * index + number]
+                )
+                for number, (source, target) in enumerate(((gate, gate_in), (up, up_in)))
+            ]
+        )
+    last = pltpu.make_async_copy(down, down_in, sems.at[2 * blocks // each])
+    for copy in sum(copies, []) + [last]:
+        copy.start()
     total = jnp.zeros((own.shape[0], 2 * units), F32)
     for index in range(blocks // each):
+        for copy in copies[index]:
+            copy.wait()
         for tokens, parity in ((own, core), (far, 1 - core)):
             columns = []
-            for source in (gate, up):
+            for source in (gate_in, up_in):
                 columns.append(
                     jnp.concatenate(
                         [
@@ -320,10 +321,11 @@
             )
     gate_proj, up_proj = total[:, :units], total[:, units:]
     hidden = (gate_proj * jax.nn.sigmoid(gate_proj) * up_proj).astype(BF16)
+    last.wait()
     pair = 2 * span
     step = 8 * span
     for start in range(0, width, step):
-        result = jnp.dot(hidden, down[:, start : start + step], preferred_element_type=F32)
+        result = jnp.dot(hidden, down_in[:, start : start + step], preferred_element_type=F32)
         evens, odds = [], []
         for inner in range(0, step, pair):
             evens.append(result[:, inner : inner + span])
@@ -341,14 +343,20 @@
     return pl.pallas_call(
         experts_kernel,
         out_shape=[jax.ShapeDtypeStruct(shape, F32), jax.ShapeDtypeStruct(shape, BF16)],
-        in_specs=[VMEM] * 5,
+        in_specs=[VMEM] * 2 + [HBM] * 3,
         out_specs=[VMEM] * 2,
+        scratch_shapes=[
+            pltpu.VMEM(gate.shape, BF16),
+            pltpu.VMEM(up.shape, BF16),
+            pltpu.VMEM(down.shape, BF16),
+            pltpu.SemaphoreType.DMA((9,)),
+        ],
         compiler_params=params(16),
         cost_estimate=pl.CostEstimate(
             flops=2 * 16 * 3 * depth * units, bytes_accessed=6 * 2**20, transcendentals=0
         ),
         name="experts",
-    )(own, far, gate, up, down)
+    )(own, far, *pinned(gate, up, down))
 
 
 def pair_kernel(keep, taken, *outs):
@@ -369,7 +377,20 @@
     )(keep, taken)
 
 
-def merge_kernel(got, value, project, keep, send):
+def merge_kernel(got, value, project, keep, send, value_in, project_in, sems):
+    depth, width = project.shape
+    step = 16 * keep.shape[2]
+    first_copy = pltpu.make_async_copy(value, value_in, sems.at[width // step])
+    first_copy.start()
+    copies = []
+    for index in range(width // step):
+        columns = pl.ds(index * step, step)
+        copies.append(
+            pltpu.make_async_copy(
+                project.at[:, columns], project_in.at[:, columns], sems.at[index]
+            )
+        )
+        copies[index].start()
     peers, height, _ = got.shape
     heads = value.shape[0]
     chunk = ROWS * heads
@@ -398,17 +419,25 @@
         columns.append(jnp.sum(piece * share, axis=0) / denominator)
     merged = jnp.concatenate(columns, axis=1)
     values = []
+    first_copy.wait()
     for head in range(heads):
         rows = merged[ROWS * head : ROWS * (head + 1)].astype(BF16)
-        values.append(jnp.dot(rows, value[head], preferred_element_type=F32))
+        values.append(jnp.dot(rows, value_in[head], preferred_element_type=F32))
     head_values = jnp.concatenate(values, axis=1).astype(BF16)
-    attended = jnp.dot(head_values, project[...], preferred_element_type=F32)
     span = keep.shape[2]
-    for peer in range(peers):
-        even = attended[:, 2 * peer * span : (2 * peer + 1) * span]
-        odd = attended[:, (2 * peer + 1) * span : (2 * peer + 2) * span]
-        keep[peer] = jnp.where(core == 1, odd, even)
-        send[peer] = jnp.where(core == 1, even, odd).astype(BF16)
+    for index, copy in enumerate(copies):
+        copy.wait()
+        attended = jnp.dot(
+            head_values,
+            project_in[:, index * step : (index + 1) * step],
+            preferred_element_type=F32,
+        )
+        for inner in range(step // (2 * span)):
+            even = attended[:, 2 * inner * span : (2 * inner + 1) * span]
+            odd = attended[:, (2 * inner + 1) * span : (2 * inner + 2) * span]
+            peer = index * step // (2 * span) + inner
+            keep[peer] = jnp.where(core == 1, odd, even)
+            send[peer] = jnp.where(core == 1, even, odd).astype(BF16)
 
 
 def merge(got, value, project, span):
@@ -418,14 +447,19 @@
     return pl.pallas_call(
         merge_kernel,
         out_shape=[jax.ShapeDtypeStruct(shape, F32), jax.ShapeDtypeStruct(shape, BF16)],
-        in_specs=[VMEM] * 3,
+        in_specs=[VMEM] + [HBM] * 2,
         out_specs=[VMEM] * 2,
+        scratch_shapes=[
+            pltpu.VMEM(value.shape, BF16),
+            pltpu.VMEM(project.shape, BF16),
+            pltpu.SemaphoreType.DMA((5,)),
+        ],
         compiler_params=params(16),
         cost_estimate=pl.CostEstimate(
             flops=2 * 8 * depth * width, bytes_accessed=6 * 2**20, transcendentals=0
         ),
         name="merge",
-    )(got, value, project)
+    )(got, *pinned(value, project))
 
 
 def finish_kernel(keep, taken, mix, back_0, back_1, back_2, back_3, out):
@@ -508,12 +542,11 @@
     near = [send[0]] + [along_x(send[d], d) for d in range(1, group_count)]
     own = jnp.concatenate(near, axis=0)
     far = lax.ppermute(own, "c", swap)
-    gate, up, down, project, value = fetch(part, w_gate, w_up, w_down, w_out, w_value)
-    keep, give = experts(own, far, gate, up, down)
+    keep, give = experts(own, far, w_gate, w_up, w_down)
     routed = pair(keep, lax.ppermute(give, "c", swap))
     back = [routed[0]] + [along_x(routed[d], -d) for d in range(1, group_count)]
 
-    keep, give = merge(got, value, project, span)
+    keep, give = merge(got, w_value, w_out, span)
     terms = finish(keep, lax.ppermute(give, "c", swap), mix, back)
     arrived = lax.all_to_all(terms, plane, 0, 0, tiled=True)
     summed = jnp.sum(arrived.astype(F32), axis=0).astype(BF16)

time: 96.1 us -> 92.9 us (0.967)
  local copies, waits for them, and re-layouts: 4.4 us -> 0.59 us
  waiting for transfers between devices: 21.9 us -> 24.9 us
  blocking collectives: 16.1 us -> 13.8 us
    unnamed x6 -> x0, local copies, waits for them, and re-layouts: 3.81 us -> none
    pallas_call x1 -> x0, Pallas kernels: 3.74 us -> none  [fetch(): pl.pallas_call(fetch_kernel, out_shape=[pltpu.VMEM(weight.shape, weight.d...]
    all_to_all x1, blocking collectives: 16.1 us -> 13.8 us  [shards(): arrived = lax.all_to_all(terms, plane, 0, 0, tiled=True)]
    pallas_call x1, Pallas kernels: 1.67 us -> 3.51 us  [experts(): pl.pallas_call(experts_kernel, out_shape=[jax.ShapeDtypeStruct(shape, F32...]
    pallas_call x1, Pallas kernels: 1.17 us -> 2.91 us  [merge(): pl.pallas_call(merge_kernel, out_shape=[jax.ShapeDtypeStruct(shape, F32),...]
    all_to_all x1, waiting for transfers between devices: 0.01 us -> 1.31 us  [shards(): got = lax.all_to_all(part, plane, 0, 0, tiled=True)]
    ppermute x1, starting transfers between devices: 2.95 us -> 4.03 us  [shards(): terms = finish(keep, lax.ppermute(give, 'c', swap), mix, back)]
    ppermute x1, waiting for transfers between devices: 0.01 us -> 0.97 us  [shards(): far = lax.ppermute(own, 'c', swap)]
  transfers between devices with their start and end apart: 13 -> 13, of which waited for: 5 -> 8; matrix products, arithmetic and copies ran while one was open for 0% -> 0% of each run, Pallas kernels for 9% -> 9%
where the time goes in v4:
time: 92.9 us; the launch traced here: 91.6 us
  starting transfers between devices  36.2 us (39%)
  waiting for transfers between devices  24.9 us (27%)
  Pallas kernels  15.3 us (16%)
  blocking collectives  13.8 us (15%)
    all_to_all x1, waiting for transfers between devices, shards(): lax.all_to_all(payload(query_lat, query_rope, moe_tokens, peers), plane,...  15.7 us
    all_to_all x1, blocking collectives, shards(): arrived = lax.all_to_all(terms, plane, 0, 0, tiled=True)  13.8 us
    all_to_all x1, starting transfers between devices, shards(): lax.all_to_all(payload(query_lat, query_rope, moe_tokens, peers), plane,...  9.48 us
    ppermute x6, starting transfers between devices, along_x(): lax.ppermute(value, 'x', [(i, (i + shift) % group_count) for i in range(g...  8.57 us
    all_to_all x1, starting transfers between devices, shards(): got = lax.all_to_all(part, plane, 0, 0, tiled=True)  7.51 us
    pallas_call x1, Pallas kernels, attention(): pl.pallas_call(lambda *refs: attention_kernel(*refs, scale=scale, units=u...  6.89 us
    ppermute x6, waiting for transfers between devices, along_x(): lax.ppermute(value, 'x', [(i, (i + shift) % group_count) for i in range(g...  5.49 us
    ppermute x1, starting transfers between devices, shards(): terms = finish(keep, lax.ppermute(give, 'c', swap), mix, back)  4.03 us
  transfers between devices with their start and end apart: 13, of which 8 were waited for; matrix products, arithmetic and copies ran while one was open for 0% of the time, Pallas kernels for 9%

profile of v4, /device:TPU:1, one launch (start us, length us, event | category | flops | bytes accessed | tf_op | source)
XLA Modules:
  0.0 91.6 jit_solution(16818338044688925462)
XLA Ops:
  0.6 3.3 %collective-permute-start = (bf16[8,256,512]{2,1,0:T(8,128)(2,1)}, bf16[8,256,512]{2,1,0:T(8,128)(2,1)S(1)}, u32[]{:S(2)}, u32[]{:S(2)}) collective-permute-start(bf16[8,256,512]{2,1,0:T(8,128)(2,1)} %refs_2_.1), channel_id=1, source_target_pairs={{0,1},{1,0},{2,3},{3,2},{4,5},{5,4},{6,7},{7,6},{8,9},{9,8},{10,11... | collective-permute-start | bytes 6291464 | tf_op jit(solution)/shard_map/ppermute | solution.py:524
  4.0 1.7 %payload.1 = bf16[32,16,640]{2,1,0:T(8,128)(2,1)} custom-call(bf16[8,2,512]{2,1,0:T(2,128)(2,1)} %query_lat.1, bf16[8,2,64]{2,1,0:T(2,128)(2,1)} %query_rope.1, bf16[8,112]{1,0:T(8,128)(2,1)} %tokens.1), custom_call_target="tpu_custom_call" | custom-call | tf_op jit(solution)/shard_map/payload/pallas_call | solution.py:68
  5.6 9.5 %all-to-all-start = ((bf16[32,16,640]{2,1,0:T(8,128)(2,1)}), bf16[32,16,640]{2,1,0:T(8,128)(2,1)S(1)}, u32[]{:S(2)}, u32[]{:S(2)}) async-start(bf16[32,16,640]{2,1,0:T(8,128)(2,1)} %payload.1), calls=%async_computation | async-start | bytes 1310720 | tf_op jit(solution)/shard_map/all_to_all | solution.py:521
  15.5 1.4 %collective-permute-done.1.refs_5_ = bf16[8,64,256]{2,1,0:T(8,128)(2,1)S(1)} collective-permute-done((bf16[8,64,256]{2,1,0:T(8,128)(2,1)}, bf16[8,64,256]{2,1,0:T(8,128)(2,1)S(1)}, u32[]{:S(2)}, u32[]{:S(2)}) %collective-permute-start.1) | collective-permute-done | bytes 262176 | tf_op jit(solution)/shard_map/ppermute | solution.py:525
  17.0 15.7 %all-to-all-done.refs_1_ = bf16[32,16,640]{2,1,0:T(8,128)(2,1)S(1)} async-done(((bf16[32,16,640]{2,1,0:T(8,128)(2,1)}), bf16[32,16,640]{2,1,0:T(8,128)(2,1)S(1)}, u32[]{:S(2)}, u32[]{:S(2)}) %all-to-all-start) | async-done | bytes 655392 | tf_op jit(solution)/shard_map/all_to_all | solution.py:521
  32.6 6.9 %attention.1 = (bf16[32,72,128]{2,1,0:T(8,128)(2,1)}, bf16[4,3584]{1,0:T(4,128)(2,1)S(1)}, bf16[4,3584]{1,0:T(4,128)(2,1)S(1)}, bf16[4,3584]{1,0:T(4,128)(2,1)S(...) custom-call(s32[8]{0:T(128)} %refs_0_.1, bf16[32,16,640]{2,1,0:T(8,128)(2,1)S(1)} %all-to-all-done.refs_1_, ...), custom_call_target="tpu_custom_call" | custom-call | flops 570425344 | bytes 6291456 | tf_op jit(solution)/shard_map/attention/pallas_call | solution.py:246
  39.5 7.5 %all-to-all-start.1 = ((bf16[32,72,128]{2,1,0:T(8,128)(2,1)}), bf16[32,72,128]{2,1,0:T(8,128)(2,1)S(1)}, u32[]{:S(2)}, u32[]{:S(2)}) async-start(bf16[32,72,128]{2,1,0:T(8,128)(2,1)} %get-tuple-element.16), calls=%async_computation.1 | async-start | bytes 1179648 | tf_op jit(solution)/shard_map/all_to_all | solution.py:540
  47.1 1.3 %collective-permute-start.3 = (bf16[4,3584]{1,0:T(4,128)(2,1)S(1)}, bf16[4,3584]{1,0:T(4,128)(2,1)S(1)}, u32[]{:S(2)}, u32[]{:S(2)}) collective-permute-start(bf16[4,3584]{1,0:T(4,128)(2,1)S(1)} %get-tuple-element.21), channel_id=1, source_target_pairs={{0,64},{64,128},{128,192},{192,0},{1,65},{65,129},{129,193},{193,1... | collective-permute-start | bytes 86024 | tf_op jit(solution)/shard_map/ppermute | solution.py:517
  48.4 2.5 %collective-permute-start.4 = (bf16[4,3584]{1,0:T(4,128)(2,1)S(1)}, bf16[4,3584]{1,0:T(4,128)(2,1)S(1)}, u32[]{:S(2)}, u32[]{:S(2)}) collective-permute-start(bf16[4,3584]{1,0:T(4,128)(2,1)S(1)} %get-tuple-element.22), channel_id=1, source_target_pairs={{0,128},{64,192},{128,0},{192,64},{1,129},{65,193},{129,1},{193,65... | collective-permute-start | bytes 86024 | tf_op jit(solution)/shard_map/ppermute | solution.py:517
  50.8 1.1 %collective-permute-start.5 = (bf16[4,3584]{1,0:T(4,128)(2,1)S(1)}, bf16[4,3584]{1,0:T(4,128)(2,1)S(1)}, u32[]{:S(2)}, u32[]{:S(2)}) collective-permute-start(bf16[4,3584]{1,0:T(4,128)(2,1)S(1)} %get-tuple-element.23), channel_id=1, source_target_pairs={{0,192},{64,0},{128,64},{192,128},{1,193},{65,1},{129,65},{193,129... | collective-permute-start | bytes 86024 | tf_op jit(solution)/shard_map/ppermute | solution.py:517
  52.0 0.6 collective-permute-done.4
  52.6 1.5 %collective-permute-done.5 = bf16[4,3584]{1,0:T(4,128)(2,1)S(1)} collective-permute-done((bf16[4,3584]{1,0:T(4,128)(2,1)S(1)}, bf16[4,3584]{1,0:T(4,128)(2,1)S(1)}, u32[]{:S(2)}, u32[]{:S(2)}) %collective-permute-start.5) | collective-permute-done | bytes 28704 | tf_op jit(solution)/shard_map/ppermute | solution.py:517
  54.1 2.5 %collective-permute-start.6 = (bf16[16,3584]{1,0:T(8,128)(2,1)S(1)}, bf16[16,3584]{1,0:T(8,128)(2,1)S(1)}, u32[]{:S(2)}, u32[]{:S(2)}) collective-permute-start(bf16[16,3584]{1,0:T(8,128)(2,1)S(1)} %pad_maximum_fusion.own), channel_id=1, source_target_pairs={{0,1},{1,0},{2,3},{3,2},{4,5},{5,4},{6,7},{7,6},{8,9},{9,8},{10,11... | collective-permute-start | bytes 344072 | tf_op jit(solution)/shard_map/ppermute | solution.py:544
  56.6 1.0 %collective-permute-done.6.far = bf16[16,3584]{1,0:T(8,128)(2,1)S(1)} collective-permute-done((bf16[16,3584]{1,0:T(8,128)(2,1)S(1)}, bf16[16,3584]{1,0:T(8,128)(2,1)S(1)}, u32[]{:S(2)}, u32[]{:S(2)}) %collective-permute-start.6) | collective-permute-done | bytes 114720 | tf_op jit(solution)/shard_map/ppermute | solution.py:544
  57.6 3.5 %experts.1 = (f32[16,3584]{1,0:T(8,128)S(1)}, bf16[16,3584]{1,0:T(8,128)(2,1)S(1)}) custom-call(bf16[16,3584]{1,0:T(8,128)(2,1)S(1)} %pad_maximum_fusion.own, bf16[16,3584]{1,0:T(8,128)(2,1)S(1)} %collective-permute-done.6.far, bf16[7168,128]{1,0:T(8,128)(2,1)} %gate.1, bf16[7168,128]{1,0:T(8,128)(2,1)} %up.1, bf16[128,7168]{1,0:T(8,128)(2,1)} %down.1), custom_call_target="tpu_custom_call" | custom-call | flops 88080384 | bytes 6291456 | tf_op jit(solution)/shard_map/experts/pallas_call | solution.py:343
  61.5 1.3 %all-to-all-done.1.got = bf16[32,72,128]{2,1,0:T(8,128)(2,1)S(1)} async-done(((bf16[32,72,128]{2,1,0:T(8,128)(2,1)}), bf16[32,72,128]{2,1,0:T(8,128)(2,1)S(1)}, u32[]{:S(2)}, u32[]{:S(2)}) %all-to-all-start.1) | async-done | bytes 589856 | tf_op jit(solution)/shard_map/all_to_all | solution.py:540
  62.9 2.9 %merge.1 = (f32[32,8,112]{2,1,0:T(8,128)S(1)}, bf16[32,8,112]{2,1,0:T(8,128)(2,1)S(1)}) custom-call(bf16[32,72,128]{2,1,0:T(8,128)(2,1)S(1)} %all-to-all-done.1.got, bf16[2,512,128]{2,1,0:T(8,128)(2,1)} %value.1, bf16[256,7168]{1,0:T(8,128)(2,1)} %project.1), custom_call_target="tpu_custom_call" | custom-call | flops 29360128 | bytes 6291456 | tf_op jit(solution)/shard_map/merge/pallas_call | solution.py:447
  65.8 4.0 %collective-permute-start.2 = (bf16[32,8,112]{2,1,0:T(8,128)(2,1)S(1)}, bf16[32,8,112]{2,1,0:T(8,128)(2,1)S(1)}, u32[]{:S(2)}, u32[]{:S(2)}) collective-permute-start(bf16[32,8,112]{2,1,0:T(8,128)(2,1)S(1)} %get-tuple-element.18), channel_id=1, source_target_pairs={{0,1},{1,0},{2,3},{3,2},{4,5},{5,4},{6,7},{7,6},{8,9},{9,8},{10,11... | collective-permute-start | bytes 172040 | tf_op jit(solution)/shard_map/ppermute | solution.py:550
  69.8 2.6 %collective-permute-start.8 = (bf16[4,3584]{1,0:T(4,128)(2,1)S(1)}, bf16[4,3584]{1,0:T(4,128)(2,1)S(1)}, u32[]{:S(2)}, u32[]{:S(2)}) collective-permute-start(bf16[4,3584]{1,0:T(4,128)(2,1)S(1)} %get-tuple-element.27), channel_id=1, source_target_pairs={{0,192},{64,0},{128,64},{192,128},{1,193},{65,1},{129,65},{193,129... | collective-permute-start | bytes 86024 | tf_op jit(solution)/shard_map/ppermute | solution.py:517
  72.4 0.5 collective-permute-start.9
  72.9 0.6 collective-permute-start.10
  73.5 3.1 %collective-permute-done.9.back_2 = bf16[4,3584]{1,0:T(4,128)(2,1)S(1)} collective-permute-done((bf16[4,3584]{1,0:T(4,128)(2,1)S(1)}, bf16[4,3584]{1,0:T(4,128)(2,1)S(1)}, u32[]{:S(2)}, u32[]{:S(2)}) %collective-permute-start.9) | collective-permute-done | bytes 28704 | tf_op jit(solution)/shard_map/ppermute | solution.py:517
  77.2 13.8 %all_to_all.15 = bf16[32,16,112]{2,1,0:T(8,128)(2,1)S(1)} all-to-all(bf16[32,16,112]{2,1,0:T(8,128)(2,1)S(1)} %finish.1), channel_id=1, replica_groups=mesh['x'=4,'y'=4,'z'=8,'c'=2] {'y','z'}, dimensions={0} | all-to-all | bytes 229376 | tf_op jit(solution)/shard_map/all_to_all | solution.py:551
  91.0 0.6 fusion
  (12 shorter events, 1.6 us)
Async XLA Ops:
  0.6 32.0 %collective-permute-start = (bf16[8,256,512]{2,1,0:T(8,128)(2,1)}, bf16[8,256,512]{2,1,0:T(8,128)(2,1)S(1)}, u32[]{:S(2)}, u32[]{:S(2)}) collective-permute-start(bf16[8,256,512]{2,1,0:T(8,128)(2,1)} %refs_2_.1), channel_id=1, source_target_pairs={{0,1},{1,0},{2,3},{3,2},{4,5},{5,4},{6,7},{7,6},{8,9},{9,8},{10,11... | collective-permute-start | bytes 6291464 | tf_op jit(solution)/shard_map/ppermute | solution.py:524
  5.6 27.0 %all-to-all-start = ((bf16[32,16,640]{2,1,0:T(8,128)(2,1)}), bf16[32,16,640]{2,1,0:T(8,128)(2,1)S(1)}, u32[]{:S(2)}, u32[]{:S(2)}) async-start(bf16[32,16,640]{2,1,0:T(8,128)(2,1)} %payload.1), calls=%async_computation | async-start | bytes 1310720 | tf_op jit(solution)/shard_map/all_to_all | solution.py:521
  15.1 1.8 %collective-permute-start.1 = (bf16[8,64,256]{2,1,0:T(8,128)(2,1)}, bf16[8,64,256]{2,1,0:T(8,128)(2,1)S(1)}, u32[]{:S(2)}, u32[]{:S(2)}) collective-permute-start(bf16[8,64,256]{2,1,0:T(8,128)(2,1)} %refs_4_.1), channel_id=1, source_target_pairs={{0,1},{1,0},{2,3},{3,2},{4,5},{5,4},{6,7},{7,6},{8,9},{9,8},{10,11... | collective-permute-start | bytes 786440 | tf_op jit(solution)/shard_map/ppermute | solution.py:525
  39.5 23.3 %all-to-all-start.1 = ((bf16[32,72,128]{2,1,0:T(8,128)(2,1)}), bf16[32,72,128]{2,1,0:T(8,128)(2,1)S(1)}, u32[]{:S(2)}, u32[]{:S(2)}) async-start(bf16[32,72,128]{2,1,0:T(8,128)(2,1)} %get-tuple-element.16), calls=%async_computation.1 | async-start | bytes 1179648 | tf_op jit(solution)/shard_map/all_to_all | solution.py:540
  47.1 4.9 %collective-permute-start.3 = (bf16[4,3584]{1,0:T(4,128)(2,1)S(1)}, bf16[4,3584]{1,0:T(4,128)(2,1)S(1)}, u32[]{:S(2)}, u32[]{:S(2)}) collective-permute-start(bf16[4,3584]{1,0:T(4,128)(2,1)S(1)} %get-tuple-element.21), channel_id=1, source_target_pairs={{0,64},{64,128},{128,192},{192,0},{1,65},{65,129},{129,193},{193,1... | collective-permute-start | bytes 86024 | tf_op jit(solution)/shard_map/ppermute | solution.py:517
  48.4 4.2 %collective-permute-start.4 = (bf16[4,3584]{1,0:T(4,128)(2,1)S(1)}, bf16[4,3584]{1,0:T(4,128)(2,1)S(1)}, u32[]{:S(2)}, u32[]{:S(2)}) collective-permute-start(bf16[4,3584]{1,0:T(4,128)(2,1)S(1)} %get-tuple-element.22), channel_id=1, source_target_pairs={{0,128},{64,192},{128,0},{192,64},{1,129},{65,193},{129,1},{193,65... | collective-permute-start | bytes 86024 | tf_op jit(solution)/shard_map/ppermute | solution.py:517
  50.8 3.2 %collective-permute-start.5 = (bf16[4,3584]{1,0:T(4,128)(2,1)S(1)}, bf16[4,3584]{1,0:T(4,128)(2,1)S(1)}, u32[]{:S(2)}, u32[]{:S(2)}) collective-permute-start(bf16[4,3584]{1,0:T(4,128)(2,1)S(1)} %get-tuple-element.23), channel_id=1, source_target_pairs={{0,192},{64,0},{128,64},{192,128},{1,193},{65,1},{129,65},{193,129... | collective-permute-start | bytes 86024 | tf_op jit(solution)/shard_map/ppermute | solution.py:517
  54.1 3.5 %collective-permute-start.6 = (bf16[16,3584]{1,0:T(8,128)(2,1)S(1)}, bf16[16,3584]{1,0:T(8,128)(2,1)S(1)}, u32[]{:S(2)}, u32[]{:S(2)}) collective-permute-start(bf16[16,3584]{1,0:T(8,128)(2,1)S(1)} %pad_maximum_fusion.own), channel_id=1, source_target_pairs={{0,1},{1,0},{2,3},{3,2},{4,5},{5,4},{6,7},{7,6},{8,9},{9,8},{10,11... | collective-permute-start | bytes 344072 | tf_op jit(solution)/shard_map/ppermute | solution.py:544
  61.1 8.7 %collective-permute-start.7 = (bf16[16,3584]{1,0:T(8,128)(2,1)S(1)}, bf16[16,3584]{1,0:T(8,128)(2,1)S(1)}, u32[]{:S(2)}, u32[]{:S(2)}) collective-permute-start(bf16[16,3584]{1,0:T(8,128)(2,1)S(1)} %get-tuple-element.25), channel_id=1, source_target_pairs={{0,1},{1,0},{2,3},{3,2},{4,5},{5,4},{6,7},{7,6},{8,9},{9,8},{10,11... | collective-permute-start | bytes 344072 | tf_op jit(solution)/shard_map/ppermute | solution.py:546
  65.8 11.2 %collective-permute-start.2 = (bf16[32,8,112]{2,1,0:T(8,128)(2,1)S(1)}, bf16[32,8,112]{2,1,0:T(8,128)(2,1)S(1)}, u32[]{:S(2)}, u32[]{:S(2)}) collective-permute-start(bf16[32,8,112]{2,1,0:T(8,128)(2,1)S(1)} %get-tuple-element.18), channel_id=1, source_target_pairs={{0,1},{1,0},{2,3},{3,2},{4,5},{5,4},{6,7},{7,6},{8,9},{9,8},{10,11... | collective-permute-start | bytes 172040 | tf_op jit(solution)/shard_map/ppermute | solution.py:550
  69.8 3.7 %collective-permute-start.8 = (bf16[4,3584]{1,0:T(4,128)(2,1)S(1)}, bf16[4,3584]{1,0:T(4,128)(2,1)S(1)}, u32[]{:S(2)}, u32[]{:S(2)}) collective-permute-start(bf16[4,3584]{1,0:T(4,128)(2,1)S(1)} %get-tuple-element.27), channel_id=1, source_target_pairs={{0,192},{64,0},{128,64},{192,128},{1,193},{65,1},{129,65},{193,129... | collective-permute-start | bytes 86024 | tf_op jit(solution)/shard_map/ppermute | solution.py:517
  72.4 4.2 %collective-permute-start.9 = (bf16[4,3584]{1,0:T(4,128)(2,1)S(1)}, bf16[4,3584]{1,0:T(4,128)(2,1)S(1)}, u32[]{:S(2)}, u32[]{:S(2)}) collective-permute-start(bf16[4,3584]{1,0:T(4,128)(2,1)S(1)} %get-tuple-element.28), channel_id=1, source_target_pairs={{0,128},{64,192},{128,0},{192,64},{1,129},{65,193},{129,1},{193,65... | collective-permute-start | bytes 86024 | tf_op jit(solution)/shard_map/ppermute | solution.py:517
  72.9 4.0 %collective-permute-start.10 = (bf16[4,3584]{1,0:T(4,128)(2,1)S(1)}, bf16[4,3584]{1,0:T(4,128)(2,1)S(1)}, u32[]{:S(2)}, u32[]{:S(2)}) collective-permute-start(bf16[4,3584]{1,0:T(4,128)(2,1)S(1)} %get-tuple-element.29), channel_id=1, source_target_pairs={{0,64},{64,128},{128,192},{192,0},{1,65},{65,129},{129,193},{193,1... | collective-permute-start | bytes 86024 | tf_op jit(solution)/shard_map/ppermute | solution.py:517

commit v5 on v4

--- a/solution.py
+++ b/solution.py
@@ -15,6 +15,7 @@
 KV = ("y", "z", "c")
 VMEM = pl.BlockSpec(memory_space=pltpu.VMEM)
 SMEM = pl.BlockSpec(memory_space=pltpu.SMEM)
+ANY = pl.BlockSpec(memory_space=pl.ANY)
 HBM = pl.BlockSpec(memory_space=pltpu.HBM)
 
 
@@ -31,6 +32,34 @@
 
 def params(mebibytes):
     return pltpu.CompilerParams(vmem_limit_bytes=mebibytes * 2**20)
+
+
+def fetch_kernel(after, *refs):
+    del after
+    count = len(refs) // 2
+    sems = refs[-1]
+    copies = [
+        pltpu.make_async_copy(refs[index], refs[count + index], sems.at[index])
+        for index in range(count)
+    ]
+    for copy in copies:
+        copy.start()
+    for copy in copies:
+        copy.wait()
+
+
+def fetch(after, *values):
+    moved = sum(value.size * value.dtype.itemsize for value in values)
+    return pl.pallas_call(
+        fetch_kernel,
+        out_shape=[pltpu.VMEM(value.shape, value.dtype) for value in values],
+        in_specs=[ANY] + [HBM] * len(values),
+        out_specs=[VMEM] * len(values),
+        scratch_shapes=[pltpu.SemaphoreType.DMA((len(values),))],
+        compiler_params=params(1),
+        cost_estimate=pl.CostEstimate(flops=0, bytes_accessed=moved, transcendentals=0),
+        name="fetch",
+    )(after, *pinned(*values))
 
 
 def payload_kernel(query_lat, query_rope, tokens, out, lat_in, rope_in, tokens_in, sems):
@@ -101,8 +130,6 @@
     stat_rows,
     token_rows,
     lengths_in,
-    lat_in,
-    rope_in,
     ids_in,
     route_in,
     sems,
@@ -114,12 +141,10 @@
     requests, positions, latent = lat_own.shape
     small = [
         pltpu.make_async_copy(lengths, lengths_in, sems.at[0]),
-        pltpu.make_async_copy(rope_own, rope_in, sems.at[1]),
-        pltpu.make_async_copy(ids, ids_in, sems.at[2]),
-        pltpu.make_async_copy(route, route_in, sems.at[3]),
+        pltpu.make_async_copy(ids, ids_in, sems.at[1]),
+        pltpu.make_async_copy(route, route_in, sems.at[2]),
     ]
-    large = pltpu.make_async_copy(lat_own, lat_in, sems.at[4])
-    for copy in small[2:] + small[:2] + [large]:
+    for copy in small:
         copy.start()
     rope = rope_own.shape[1]
     tiles = latent // LANES
@@ -146,8 +171,8 @@
             pieces, axis=1
         )
     tokens = token_rows[...].astype(BF16)
-    small[2].wait()
-    small[3].wait()
+    for copy in small:
+        copy.wait()
     named = ids_in[...]
     strength = route_in[...]
     lower = (
@@ -179,9 +204,6 @@
     base_own = shard * positions
     base_far = (shard + 1 - 2 * core) * positions
     place = lax.broadcasted_iota(jnp.int32, (rows, positions), 1)
-    small[0].wait()
-    small[1].wait()
-    large.wait()
     for request in range(requests):
         mine = jnp.concatenate(
             [
@@ -198,7 +220,7 @@
         ).astype(BF16)
         length = lengths_in[request]
         parts = []
-        for lat, rot, base in ((lat_in, rope_in, base_own), (lat_far, rope_far, base_far)):
+        for lat, rot, base in ((lat_own, rope_own, base_own), (lat_far, rope_far, base_far)):
             score = (
                 lax.dot_general(
                     mine[:, :latent],
@@ -216,7 +238,7 @@
         weights = [jnp.where(usable, jnp.exp(score - top), 0.0) for score, usable, _ in parts]
         total = jnp.sum(weights[0] + weights[1], axis=1, keepdims=True)
         weighted = jnp.dot(
-            weights[0].astype(BF16), lat_in[request], preferred_element_type=F32
+            weights[0].astype(BF16), lat_own[request], preferred_element_type=F32
         ) + jnp.dot(weights[1].astype(BF16), lat_far[request], preferred_element_type=F32)
         partial = weighted * (1.0 / jnp.maximum(total, 1.0))
         for index, term in enumerate(three_terms(top) + three_terms(total)):
@@ -242,13 +264,13 @@
     requests, positions, latent = lat_own.shape
     rope = rope_own.shape[1]
     tiles = latent // LANES
-    lengths, lat_own, rope_own, ids, route = pinned(lengths, lat_own, rope_own, ids, route)
+    lengths, ids, route = pinned(lengths, ids, route)
     return pl.pallas_call(
         lambda *refs: attention_kernel(*refs, scale=scale, units=units),
         out_shape=[jax.ShapeDtypeStruct((peers, tiles * chunk + ROWS, LANES), BF16)]
         + [jax.ShapeDtypeStruct((CAP, peers * span), BF16)] * 4
         + [jax.ShapeDtypeStruct((ROWS, LANES), F32)],
-        in_specs=[HBM, VMEM, HBM, VMEM, HBM, VMEM, HBM, HBM],
+        in_specs=[HBM] + [VMEM] * 5 + [HBM] * 2,
         out_specs=[VMEM] * 6,
         scratch_shapes=[
             pltpu.VMEM((width // LANES, peers * chunk, LANES), F32),
@@ -256,11 +278,9 @@
             pltpu.VMEM((peers * ROWS, LANES), F32),
             pltpu.VMEM((requests, peers * span), F32),
             pltpu.SMEM(lengths.shape, jnp.int32),
-            pltpu.VMEM(lat_own.shape, BF16),
-            pltpu.VMEM(rope_own.shape, BF16),
             pltpu.VMEM(ids.shape, jnp.int32),
             pltpu.VMEM(route.shape, F32),
-            pltpu.SemaphoreType.DMA((5,)),
+            pltpu.SemaphoreType.DMA((3,)),
         ],
         compiler_params=params(24),
         cost_estimate=pl.CostEstimate(
@@ -272,34 +292,36 @@
     )(lengths, query, lat_own, lat_far, rope_own, rope_far, ids, route)
 
 
-def experts_kernel(own, far, gate, up, down, keep, send, gate_in, up_in, down_in, sems):
+def stack_kernel(after, *refs):
+    del after
+    out = refs[-1]
+    out[...] = jnp.concatenate([ref[...].astype(F32) for ref in refs[:-1]], axis=0).astype(BF16)
+
+
+def stack(after, *values):
+    rows, width = values[0].shape
+    return pl.pallas_call(
+        stack_kernel,
+        out_shape=jax.ShapeDtypeStruct((len(values) * rows, width), BF16),
+        in_specs=[ANY] + [VMEM] * len(values),
+        out_specs=VMEM,
+        compiler_params=params(4),
+        name="stack",
+    )(after, *values)
+
+
+def experts_kernel(own, far, gate, up, down, keep, send):
     depth, units = gate.shape
     width = down.shape[1]
     span = 112
     blocks = depth // (2 * span)
     core = lax.axis_index("c")
     each = 8
-    copies = []
-    for index in range(blocks // each):
-        rows = pl.ds(2 * span * each * index, 2 * span * each)
-        copies.append(
-            [
-                pltpu.make_async_copy(
-                    source.at[rows, :], target.at[rows, :], sems.at[2 * index + number]
-                )
-                for number, (source, target) in enumerate(((gate, gate_in), (up, up_in)))
-            ]
-        )
-    last = pltpu.make_async_copy(down, down_in, sems.at[2 * blocks // each])
-    for copy in sum(copies, []) + [last]:
-        copy.start()
     total = jnp.zeros((own.shape[0], 2 * units), F32)
     for index in range(blocks // each):
-        for copy in copies[index]:
-            copy.wait()
         for tokens, parity in ((own, core), (far, 1 - core)):
             columns = []
-            for source in (gate_in, up_in):
+            for source in (gate, up):
                 columns.append(
                     jnp.concatenate(
                         [
@@ -321,11 +343,10 @@
             )
     gate_proj, up_proj = total[:, :units], total[:, units:]
     hidden = (gate_proj * jax.nn.sigmoid(gate_proj) * up_proj).astype(BF16)
-    last.wait()
     pair = 2 * span
     step = 8 * span
     for start in range(0, width, step):
-        result = jnp.dot(hidden, down_in[:, start : start + step], preferred_element_type=F32)
+        result = jnp.dot(hidden, down[:, start : start + step], preferred_element_type=F32)
         evens, odds = [], []
         for inner in range(0, step, pair):
             evens.append(result[:, inner : inner + span])
@@ -343,20 +364,14 @@
     return pl.pallas_call(
         experts_kernel,
         out_shape=[jax.ShapeDtypeStruct(shape, F32), jax.ShapeDtypeStruct(shape, BF16)],
-        in_specs=[VMEM] * 2 + [HBM] * 3,
+        in_specs=[VMEM] * 5,
         out_specs=[VMEM] * 2,
-        scratch_shapes=[
-            pltpu.VMEM(gate.shape, BF16),
-            pltpu.VMEM(up.shape, BF16),
-            pltpu.VMEM(down.shape, BF16),
-            pltpu.SemaphoreType.DMA((9,)),
-        ],
         compiler_params=params(16),
         cost_estimate=pl.CostEstimate(
             flops=2 * 16 * 3 * depth * units, bytes_accessed=6 * 2**20, transcendentals=0
         ),
         name="experts",
-    )(own, far, *pinned(gate, up, down))
+    )(own, far, gate, up, down)
 
 
 def pair_kernel(keep, taken, *outs):
@@ -377,25 +392,12 @@
     )(keep, taken)
 
 
-def merge_kernel(got, value, project, keep, send, value_in, project_in, sems):
-    depth, width = project.shape
-    step = 16 * keep.shape[2]
-    first_copy = pltpu.make_async_copy(value, value_in, sems.at[width // step])
-    first_copy.start()
-    copies = []
-    for index in range(width // step):
-        columns = pl.ds(index * step, step)
-        copies.append(
-            pltpu.make_async_copy(
-                project.at[:, columns], project_in.at[:, columns], sems.at[index]
-            )
-        )
-        copies[index].start()
+def merge_kernel(after, got, value, out):
+    del after
     peers, height, _ = got.shape
     heads = value.shape[0]
     chunk = ROWS * heads
     tiles = height // chunk
-    core = lax.axis_index("c")
     stats = got[:, tiles * chunk :, :].astype(F32)
     lane = lax.broadcasted_iota(jnp.int32, (peers, ROWS, LANES), 2)
     first = lane - ROWS * lax.broadcasted_iota(jnp.int32, (peers, ROWS, LANES), 1)
@@ -419,76 +421,95 @@
         columns.append(jnp.sum(piece * share, axis=0) / denominator)
     merged = jnp.concatenate(columns, axis=1)
     values = []
-    first_copy.wait()
     for head in range(heads):
         rows = merged[ROWS * head : ROWS * (head + 1)].astype(BF16)
-        values.append(jnp.dot(rows, value_in[head], preferred_element_type=F32))
-    head_values = jnp.concatenate(values, axis=1).astype(BF16)
-    span = keep.shape[2]
-    for index, copy in enumerate(copies):
-        copy.wait()
-        attended = jnp.dot(
-            head_values,
-            project_in[:, index * step : (index + 1) * step],
-            preferred_element_type=F32,
-        )
-        for inner in range(step // (2 * span)):
-            even = attended[:, 2 * inner * span : (2 * inner + 1) * span]
-            odd = attended[:, (2 * inner + 1) * span : (2 * inner + 2) * span]
-            peer = index * step // (2 * span) + inner
-            keep[peer] = jnp.where(core == 1, odd, even)
-            send[peer] = jnp.where(core == 1, even, odd).astype(BF16)
-
-
-def merge(got, value, project, span):
-    peers = got.shape[0]
-    depth, width = project.shape
-    shape = (peers, ROWS, span)
+        values.append(jnp.dot(rows, value[head], preferred_element_type=F32))
+    out[...] = jnp.concatenate(values, axis=1).astype(BF16)
+
+
+def merge(after, got, value):
+    heads, latent, width = value.shape
     return pl.pallas_call(
         merge_kernel,
-        out_shape=[jax.ShapeDtypeStruct(shape, F32), jax.ShapeDtypeStruct(shape, BF16)],
-        in_specs=[VMEM] + [HBM] * 2,
-        out_specs=[VMEM] * 2,
-        scratch_shapes=[
-            pltpu.VMEM(value.shape, BF16),
-            pltpu.VMEM(project.shape, BF16),
-            pltpu.SemaphoreType.DMA((5,)),
-        ],
+        out_shape=jax.ShapeDtypeStruct((ROWS, heads * width), BF16),
+        in_specs=[ANY] + [VMEM] * 2,
+        out_specs=VMEM,
         compiler_params=params(16),
         cost_estimate=pl.CostEstimate(
-            flops=2 * 8 * depth * width, bytes_accessed=6 * 2**20, transcendentals=0
+            flops=2 * ROWS * heads * latent * width, bytes_accessed=2**20, transcendentals=0
         ),
         name="merge",
-    )(got, *pinned(value, project))
-
-
-def finish_kernel(keep, taken, mix, back_0, back_1, back_2, back_3, out):
-    peers, _, span = keep.shape
+    )(after, got, value)
+
+
+def finish_kernel(
+    values, values_far, project, project_far, mix, back_0, back_1, back_2, back_3, out
+):
+    peers, _, span = out.shape
     back = jnp.concatenate(
         [ref[...].astype(F32) for ref in (back_0, back_1, back_2, back_3)], axis=0
     ).astype(BF16)
     mixing = mix[...][:, : 4 * CAP]
     high = mixing.astype(BF16)
     low = (mixing - high.astype(F32)).astype(BF16)
-    routed = jnp.dot(high, back, preferred_element_type=F32) + jnp.dot(
-        low, back, preferred_element_type=F32
-    )
-    for peer in range(peers):
-        attended = keep[peer] + taken[peer].astype(F32)
-        both = jnp.concatenate([attended, routed[:, peer * span : (peer + 1) * span]], axis=0)
-        out[peer] = both.astype(BF16)
-
-
-def finish(keep, taken, mix, back):
-    peers, rows, span = keep.shape
+    step = 8 * span
+    for start in range(0, peers * span, step):
+        here = slice(start, start + step)
+        routed = jnp.dot(high, back[:, here], preferred_element_type=F32) + jnp.dot(
+            low, back[:, here], preferred_element_type=F32
+        )
+        attended = jnp.dot(
+            values[...], project[:, here], preferred_element_type=F32
+        ) + jnp.dot(values_far[...], project_far[:, here], preferred_element_type=F32)
+        both = jnp.concatenate([attended, routed], axis=0)
+        for inner in range(8):
+            out[start // span + inner] = both[:, inner * span : (inner + 1) * span].astype(BF16)
+
+
+def finish(values, values_far, project, project_far, mix, back, peers, span):
     return pl.pallas_call(
         finish_kernel,
-        out_shape=jax.ShapeDtypeStruct((peers, 2 * rows, span), BF16),
-        in_specs=[VMEM] * 7,
+        out_shape=jax.ShapeDtypeStruct((peers, 2 * ROWS, span), BF16),
+        in_specs=[VMEM] * 9,
         out_specs=VMEM,
-        compiler_params=params(8),
+        compiler_params=params(16),
         name="finish",
-    )(keep, taken, mix, *back)
+    )(values, values_far, project, project_far, mix, *back)
+
+
+def split_kernel(after, project, mine, theirs):
+    del after
+    span = 112
+    step = 8 * span
+    core = lax.axis_index("c")
+
+    @pl.loop(0, project.shape[0] // 32)
+    def _(block):
+        rows = pl.ds(pl.multiple_of(block * 32, 32), 32)
+        for start in range(0, project.shape[1], 2 * step):
+            piece = project[rows, start : start + 2 * step].astype(F32)
+            even = jnp.concatenate(
+                [piece[:, 2 * i * span : (2 * i + 1) * span] for i in range(8)], axis=1
+            )
+            odd = jnp.concatenate(
+                [piece[:, (2 * i + 1) * span : (2 * i + 2) * span] for i in range(8)], axis=1
+            )
+            here = slice(start // 2, start // 2 + step)
+            mine[rows, here] = jnp.where(core == 1, odd, even).astype(BF16)
+            theirs[rows, here] = jnp.where(core == 1, even, odd).astype(BF16)
+
+
+def split(after, project):
+    depth, width = project.shape
+    return pl.pallas_call(
+        split_kernel,
+        out_shape=[pltpu.HBM((depth, width // 2), BF16)] * 2,
+        in_specs=[ANY, VMEM],
+        out_specs=[VMEM] * 2,
+        compiler_params=params(20),
+        cost_estimate=pl.CostEstimate(flops=0, bytes_accessed=8 * 2**20, transcendentals=0),
+        name="split",
+    )(after, *pinned(project))
 
 
 def shards(
@@ -523,13 +544,16 @@
     )
     lat_far = lax.ppermute(cache_lat, "c", swap)
     rope_far = lax.ppermute(cache_rope, "c", swap)
+    project, theirs = split(rope_far, w_out)
+    project_far = lax.ppermute(theirs, "c", swap)
+    lat_own, rope_own = fetch(rope_far, cache_lat, cache_rope)
     scale = (w_value.shape[2] + query_rope.shape[2]) ** (-0.5)
     part, *send, mix = attention(
         lengths,
         query,
-        cache_lat,
+        lat_own,
         lat_far,
-        cache_rope,
+        rope_own,
         rope_far,
         expert_ids,
         route_weights,
@@ -540,14 +564,17 @@
     got = lax.all_to_all(part, plane, 0, 0, tiled=True)
 
     near = [send[0]] + [along_x(send[d], d) for d in range(1, group_count)]
-    own = jnp.concatenate(near, axis=0)
+    gate, up, down = fetch(part, w_gate, w_up, w_down)
+    own = stack(gate, *near)
     far = lax.ppermute(own, "c", swap)
-    keep, give = experts(own, far, w_gate, w_up, w_down)
+    keep, give = experts(own, far, gate, up, down)
     routed = pair(keep, lax.ppermute(give, "c", swap))
     back = [routed[0]] + [along_x(routed[d], -d) for d in range(1, group_count)]
 
-    keep, give = merge(got, w_value, w_out, span)
-    terms = finish(keep, lax.ppermute(give, "c", swap), mix, back)
+    project, value = fetch(routed[0], project, w_value)
+    values = merge(routed[0], got, value)
+    values_far = lax.ppermute(values, "c", swap)
+    terms = finish(values, values_far, project, project_far, mix, back, peers, span)
     arrived = lax.all_to_all(terms, plane, 0, 0, tiled=True)
     summed = jnp.sum(arrived.astype(F32), axis=0).astype(BF16)
     return (summed[:requests], summed[requests:])

time: 92.9 us -> 91.5 us (0.985)
  waiting for transfers between devices: 24.9 us -> 10.7 us
  Pallas kernels: 15.3 us -> 24 us
  blocking collectives: 13.8 us -> 18.5 us
  local copies, waits for them, and re-layouts: 0.59 us -> 3.52 us
  starting transfers between devices: 36.2 us -> 33.4 us
    pallas_call x1 -> x6, Pallas kernels: 2.91 us -> 12.2 us  [the longest x1 5.9 us: split(): pl.pallas_call(split_kernel, out_shape=[pltpu.HBM((depth, width // 2), BF...]
    all_to_all x1, waiting for transfers between devices: 15.7 us -> 6.73 us  [shards(): lax.all_to_all(payload(query_lat, query_rope, moe_tokens, peers), plane,...]
    ppermute x6, waiting for transfers between devices: 5.49 us -> 0.02 us  [along_x(): lax.ppermute(value, 'x', [(i, (i + shift) % group_count) for i in range(g...]
    all_to_all x1, blocking collectives: 13.8 us -> 18.5 us  [shards(): arrived = lax.all_to_all(terms, plane, 0, 0, tiled=True)]
    unnamed x0 -> x6, local copies, waits for them, and re-layouts: none -> 2.93 us
    ppermute x1 -> x2, starting transfers between devices: 4.03 us -> 1.5 us  [the longest x1 1.2 us: shards(): values_far = lax.ppermute(values, 'c', swap)]
    pallas_call x1, Pallas kernels: 0.27 us -> 2.22 us  [finish(): pl.pallas_call(finish_kernel, out_shape=jax.ShapeDtypeStruct((peers, 2 *...]
    pallas_call x1, Pallas kernels: 3.51 us -> 1.67 us  [experts(): pl.pallas_call(experts_kernel, out_shape=[jax.ShapeDtypeStruct(shape, F32...]
  transfers between devices with their start and end apart: 13 -> 14, of which waited for: 8 -> 5; matrix products, arithmetic and copies ran while one was open for 0% -> 0% of each run, Pallas kernels for 9% -> 24%
where the time goes in v5:
time: 91.5 us; the launch traced here: 91 us
  starting transfers between devices  33.4 us (37%)
  Pallas kernels  24 us (26%)
  blocking collectives  18.5 us (20%)
  waiting for transfers between devices  10.7 us (12%)
  local copies, waits for them, and re-layouts  3.52 us (4%)
    all_to_all x1, blocking collectives, shards(): arrived = lax.all_to_all(terms, plane, 0, 0, tiled=True)  18.5 us
    all_to_all x1, starting transfers between devices, shards(): lax.all_to_all(payload(query_lat, query_rope, moe_tokens, peers), plane,...  9.48 us
    ppermute x6, starting transfers between devices, along_x(): lax.ppermute(value, 'x', [(i, (i + shift) % group_count) for i in range(g...  8.64 us
    all_to_all x1, starting transfers between devices, shards(): got = lax.all_to_all(part, plane, 0, 0, tiled=True)  7.51 us
    all_to_all x1, waiting for transfers between devices, shards(): lax.all_to_all(payload(query_lat, query_rope, moe_tokens, peers), plane,...  6.73 us
    pallas_call x1, Pallas kernels, attention(): pl.pallas_call(lambda *refs: attention_kernel(*refs, scale=scale, units=u...  6.17 us
    pallas_call x1, Pallas kernels, split(): pl.pallas_call(split_kernel, out_shape=[pltpu.HBM((depth, width // 2), BF...  5.9 us
    pallas_call x3, Pallas kernels, fetch(): pl.pallas_call(fetch_kernel, out_shape=[pltpu.VMEM(value.shape, value.dty...  5.76 us
  transfers between devices with their start and end apart: 14, of which 5 were waited for; matrix products, arithmetic and copies ran while one was open for 0% of the time, Pallas kernels for 24%

profile of v5, /device:TPU:1, one launch (start us, length us, event | category | flops | bytes accessed | tf_op | source)
XLA Modules:
  0.0 91.0 jit_solution(12063783335247848728)
XLA Ops:
  0.6 3.3 %collective-permute-start.1 = (bf16[8,256,512]{2,1,0:T(8,128)(2,1)}, bf16[8,256,512]{2,1,0:T(8,128)(2,1)S(1)}, u32[]{:S(2)}, u32[]{:S(2)}) collective-permute-start(bf16[8,256,512]{2,1,0:T(8,128)(2,1)} %refs_0_.3), channel_id=1, source_target_pairs={{0,1},{1,0},{2,3},{3,2},{4,5},{5,4},{6,7},{7,6},{8,9},{9,8},{10,11... | collective-permute-start | bytes 6291464 | tf_op jit(solution)/shard_map/ppermute | solution.py:545
  4.0 1.8 %payload.1 = bf16[32,16,640]{2,1,0:T(8,128)(2,1)} custom-call(bf16[8,2,512]{2,1,0:T(2,128)(2,1)} %query_lat.1, bf16[8,2,64]{2,1,0:T(2,128)(2,1)} %query_rope.1, bf16[8,112]{1,0:T(8,128)(2,1)} %tokens.1), custom_call_target="tpu_custom_call" | custom-call | tf_op jit(solution)/shard_map/payload/pallas_call | solution.py:97
  5.7 9.5 %all-to-all-start = ((bf16[32,16,640]{2,1,0:T(8,128)(2,1)}), bf16[32,16,640]{2,1,0:T(8,128)(2,1)S(1)}, u32[]{:S(2)}, u32[]{:S(2)}) async-start(bf16[32,16,640]{2,1,0:T(8,128)(2,1)} %payload.1), calls=%async_computation | async-start | bytes 1310720 | tf_op jit(solution)/shard_map/all_to_all | solution.py:542
  15.6 1.2 %collective-permute-done.after.refs_5_ = bf16[8,64,256]{2,1,0:T(8,128)(2,1)S(1)} collective-permute-done((bf16[8,64,256]{2,1,0:T(8,128)(2,1)S(1)}, bf16[8,64,256]{2,1,0:T(8,128)(2,1)S(1)}, u32[]{:S(2)}, u32[]{:S(2)}) %collective-permute-start) | collective-permute-done | bytes 262176 | tf_op jit(solution)/shard_map/ppermute | solution.py:546
  16.9 5.9 %split.1 = (bf16[256,3584]{1,0:T(8,128)(2,1)}, bf16[256,3584]{1,0:T(8,128)(2,1)}) custom-call(bf16[8,64,256]{2,1,0:T(8,128)(2,1)S(1)} %collective-permute-done.after.refs_5_, bf16[256,7168]{1,0:T(8,128)(2,1)} %project.1), custom_call_target="tpu_custom_call" | custom-call | bytes 8388608 | tf_op jit(solution)/shard_map/split/pallas_call | solution.py:504
  23.0 1.6 %fetch.3 = (bf16[8,256,512]{2,1,0:T(8,128)(2,1)S(1)}, bf16[8,64,256]{2,1,0:T(8,128)(2,1)S(1)}) custom-call(bf16[8,64,256]{2,1,0:T(8,128)(2,1)S(1)} %collective-permute-done.after.refs_5_, bf16[8,256,512]{2,1,0:T(8,128)(2,1)} %refs_0_.3, bf16[8,64,256]{2,1,0:T(8,128)(2,1)} %refs_1_.3), custom_call_target="tpu_custom_call" | custom-call | bytes 2359296 | tf_op jit(solution)/shard_map/fetch/pallas_call | solution.py:53
  24.7 1.3 %copy-done = bf16[8,256,512]{2,1,0:T(8,128)(2,1)} copy-done((bf16[8,256,512]{2,1,0:T(8,128)(2,1)}, bf16[8,256,512]{2,1,0:T(8,128)(2,1)S(1)}, u32[]{:S(2)}) %copy-start) | copy-done | bytes 2097176
  26.0 6.7 %all-to-all-done.refs_1_ = bf16[32,16,640]{2,1,0:T(8,128)(2,1)S(1)} async-done(((bf16[32,16,640]{2,1,0:T(8,128)(2,1)}), bf16[32,16,640]{2,1,0:T(8,128)(2,1)S(1)}, u32[]{:S(2)}, u32[]{:S(2)}) %all-to-all-start) | async-done | bytes 655392 | tf_op jit(solution)/shard_map/all_to_all | solution.py:542
  32.7 1.6 %copy-done.1 = bf16[8,256,512]{2,1,0:T(8,128)(2,1)S(1)} copy-done((bf16[8,256,512]{2,1,0:T(8,128)(2,1)S(1)}, bf16[8,256,512]{2,1,0:T(8,128)(2,1)}, u32[]{:S(2)}) %copy-start.1) | copy-done | bytes 2097176
  34.3 6.2 %attention.1 = (bf16[32,72,128]{2,1,0:T(8,128)(2,1)}, bf16[4,3584]{1,0:T(4,128)(2,1)S(1)}, bf16[4,3584]{1,0:T(4,128)(2,1)S(1)}, bf16[4,3584]{1,0:T(4,128)(2,1)S(...) custom-call(s32[8]{0:T(128)} %refs_0_.4, bf16[32,16,640]{2,1,0:T(8,128)(2,1)S(1)} %all-to-all-done.refs_1_, ...), custom_call_target="tpu_custom_call" | custom-call | flops 570425344 | bytes 6291456 | tf_op jit(solution)/shard_map/attention/pallas_call | solution.py:268
  40.5 7.5 %all-to-all-start.1 = ((bf16[32,72,128]{2,1,0:T(8,128)(2,1)}), bf16[32,72,128]{2,1,0:T(8,128)(2,1)S(1)}, u32[]{:S(2)}, u32[]{:S(2)}) async-start(bf16[32,72,128]{2,1,0:T(8,128)(2,1)} %get-tuple-element.25.after), calls=%async_computation.1 | async-start | bytes 1179648 | tf_op jit(solution)/shard_map/all_to_all | solution.py:564
  48.0 1.3 %collective-permute-start.2 = (bf16[4,3584]{1,0:T(4,128)(2,1)S(1)}, bf16[4,3584]{1,0:T(4,128)(2,1)S(1)}, u32[]{:S(2)}, u32[]{:S(2)}) collective-permute-start(bf16[4,3584]{1,0:T(4,128)(2,1)S(1)} %get-tuple-element.28), channel_id=1, source_target_pairs={{0,64},{64,128},{128,192},{192,0},{1,65},{65,129},{129,193},{193,1... | collective-permute-start | bytes 86024 | tf_op jit(solution)/shard_map/ppermute | solution.py:538
  49.3 2.5 %collective-permute-start.3 = (bf16[4,3584]{1,0:T(4,128)(2,1)S(1)}, bf16[4,3584]{1,0:T(4,128)(2,1)S(1)}, u32[]{:S(2)}, u32[]{:S(2)}) collective-permute-start(bf16[4,3584]{1,0:T(4,128)(2,1)S(1)} %get-tuple-element.29), channel_id=1, source_target_pairs={{0,128},{64,192},{128,0},{192,64},{1,129},{65,193},{129,1},{193,65... | collective-permute-start | bytes 86024 | tf_op jit(solution)/shard_map/ppermute | solution.py:538
  51.8 1.1 %collective-permute-start.4 = (bf16[4,3584]{1,0:T(4,128)(2,1)S(1)}, bf16[4,3584]{1,0:T(4,128)(2,1)S(1)}, u32[]{:S(2)}, u32[]{:S(2)}) collective-permute-start(bf16[4,3584]{1,0:T(4,128)(2,1)S(1)} %get-tuple-element.30), channel_id=1, source_target_pairs={{0,192},{64,0},{128,64},{192,128},{1,193},{65,1},{129,65},{193,129... | collective-permute-start | bytes 86024 | tf_op jit(solution)/shard_map/ppermute | solution.py:538
  52.9 2.6 %fetch.4 = (bf16[7168,128]{1,0:T(8,128)(2,1)S(1)}, bf16[7168,128]{1,0:T(8,128)(2,1)S(1)}, bf16[128,7168]{1,0:T(8,128)(2,1)S(1)}) custom-call(bf16[32,72,128]{2,1,0:T(8,128)(2,1)} %get-tuple-element.25.after, bf16[7168,128]{1,0:T(8,128)(2,1)} %refs_0_.5, bf16[7168,128]{1,0:T(8,128)(2,1)} %refs_1_.4, bf16[128,7168]{1,0:T(8,128)(2,1)} %refs_2_.1), custom_call_target="tpu_custom_call" | custom-call | bytes 5505024 | tf_op jit(solution)/shard_map/fetch/pallas_call | solution.py:53
  55.6 2.2 %collective-permute-start.5 = (bf16[16,3584]{1,0:T(8,128)(2,1)S(1)}, bf16[16,3584]{1,0:T(8,128)(2,1)S(1)}, u32[]{:S(2)}, u32[]{:S(2)}) collective-permute-start(bf16[16,3584]{1,0:T(8,128)(2,1)S(1)} %stack.1.own), channel_id=1, source_target_pairs={{0,1},{1,0},{2,3},{3,2},{4,5},{5,4},{6,7},{7,6},{8,9},{9,8},{10,11... | collective-permute-start | bytes 344072 | tf_op jit(solution)/shard_map/ppermute | solution.py:569
  58.7 1.7 %experts.1 = (f32[16,3584]{1,0:T(8,128)S(1)}, bf16[16,3584]{1,0:T(8,128)(2,1)S(1)}) custom-call(bf16[16,3584]{1,0:T(8,128)(2,1)S(1)} %stack.1.own, bf16[16,3584]{1,0:T(8,128)(2,1)S(1)} %collective-permute-done.5.far, bf16[7168,128]{1,0:T(8,128)(2,1)S(1)} %get-tuple-element.26.after.gate, bf16[7168,128]{1,0:T(8,128)(2,1)S(1)} %get-tuple-element.31.up, ...), custom_call_target="tpu_custom_call" | custom-call | flops 88080384 | bytes 6291456 | tf_op jit(solution)/shard_map/experts/pallas_call | solution.py:364
  60.8 1.0 %collective-permute-done.6.taken = bf16[16,3584]{1,0:T(8,128)(2,1)S(1)} collective-permute-done((bf16[16,3584]{1,0:T(8,128)(2,1)S(1)}, bf16[16,3584]{1,0:T(8,128)(2,1)S(1)}, u32[]{:S(2)}, u32[]{:S(2)}) %collective-permute-start.6) | collective-permute-done | bytes 114720 | tf_op jit(solution)/shard_map/ppermute | solution.py:571
  61.8 1.1 %collective-permute-start.10 = (bf16[4,3584]{1,0:T(4,128)(2,1)S(1)}, bf16[4,3584]{1,0:T(4,128)(2,1)S(1)}, u32[]{:S(2)}, u32[]{:S(2)}) collective-permute-start(bf16[4,3584]{1,0:T(4,128)(2,1)S(1)} %get-tuple-element.42), channel_id=1, source_target_pairs={{0,128},{64,192},{128,0},{192,64},{1,129},{65,193},{129,1},{193,65... | collective-permute-start | bytes 86024 | tf_op jit(solution)/shard_map/ppermute | solution.py:538
  62.9 1.7 %collective-permute-start.11 = (bf16[4,3584]{1,0:T(4,128)(2,1)S(1)}, bf16[4,3584]{1,0:T(4,128)(2,1)S(1)}, u32[]{:S(2)}, u32[]{:S(2)}) collective-permute-start(bf16[4,3584]{1,0:T(4,128)(2,1)S(1)} %get-tuple-element.43), channel_id=1, source_target_pairs={{0,64},{64,128},{128,192},{192,0},{1,65},{65,129},{129,193},{193,1... | collective-permute-start | bytes 86024 | tf_op jit(solution)/shard_map/ppermute | solution.py:538
  65.6 1.5 %fetch.5 = (bf16[256,3584]{1,0:T(8,128)(2,1)S(1)}, bf16[2,512,128]{2,1,0:T(8,128)(2,1)S(1)}) custom-call(bf16[4,3584]{1,0:T(4,128)(2,1)S(1)} %get-tuple-element.35.after.back_0, bf16[256,3584]{1,0:T(8,128)(2,1)} %get-tuple-element.36.refs_0_, bf16[2,512,128]{2,1,0:T(8,128)(2,1)} %refs_1_.5), custom_call_target="tpu_custom_call" | custom-call | bytes 2097152 | tf_op jit(solution)/shard_map/fetch/pallas_call | solution.py:53
  67.6 1.2 %collective-permute-start.7 = (bf16[8,256]{1,0:T(8,128)(2,1)S(1)}, bf16[8,256]{1,0:T(8,128)(2,1)S(1)}, u32[]{:S(2)}, u32[]{:S(2)}) collective-permute-start(bf16[8,256]{1,0:T(8,128)(2,1)S(1)} %merge.1.values), channel_id=1, source_target_pairs={{0,1},{1,0},{2,3},{3,2},{4,5},{5,4},{6,7},{7,6},{8,9},{9,8},{10,11... | collective-permute-start | bytes 12296 | tf_op jit(solution)/shard_map/ppermute | solution.py:576
  69.6 2.2 %finish.1 = bf16[32,16,112]{2,1,0:T(8,128)(2,1)S(1)} custom-call(bf16[8,256]{1,0:T(8,128)(2,1)S(1)} %merge.1.values, bf16[8,256]{1,0:T(8,128)(2,1)S(1)} %collective-permute-done.7.values_far, bf16[256,3584]{1,0:T(8,128)(2,1)S(1)} %get-tuple-element.38.project, bf16[256,3584]{1,0:T(8,128)(2,1)} %collective-permute-done.8.project_far, ...), custom_call_target="tpu_custom_call" | custom-call | tf_op jit(solution)/shard_map/finish/pallas_call | solution.py:470
  71.9 18.5 %all_to_all.15 = bf16[32,16,112]{2,1,0:T(8,128)(2,1)S(1)} all-to-all(bf16[32,16,112]{2,1,0:T(8,128)(2,1)S(1)} %finish.1), channel_id=1, replica_groups=mesh['x'=4,'y'=4,'z'=8,'c'=2] {'y','z'}, dimensions={0} | all-to-all | bytes 229376 | tf_op jit(solution)/shard_map/all_to_all | solution.py:578
  (24 shorter events, 5.0 us)
Async XLA Ops:
  0.6 14.6 %copy-start.2 = (bf16[8,64,256]{2,1,0:T(8,128)(2,1)S(1)}, bf16[8,64,256]{2,1,0:T(8,128)(2,1)}, u32[]{:S(2)}) copy-start(bf16[8,64,256]{2,1,0:T(8,128)(2,1)} %refs_1_.3) | copy-start | bytes 786436
  0.6 32.1 %collective-permute-start.1 = (bf16[8,256,512]{2,1,0:T(8,128)(2,1)}, bf16[8,256,512]{2,1,0:T(8,128)(2,1)S(1)}, u32[]{:S(2)}, u32[]{:S(2)}) collective-permute-start(bf16[8,256,512]{2,1,0:T(8,128)(2,1)} %refs_0_.3), channel_id=1, source_target_pairs={{0,1},{1,0},{2,3},{3,2},{4,5},{5,4},{6,7},{7,6},{8,9},{9,8},{10,11... | collective-permute-start | bytes 6291464 | tf_op jit(solution)/shard_map/ppermute | solution.py:545
  5.7 27.0 %all-to-all-start = ((bf16[32,16,640]{2,1,0:T(8,128)(2,1)}), bf16[32,16,640]{2,1,0:T(8,128)(2,1)S(1)}, u32[]{:S(2)}, u32[]{:S(2)}) async-start(bf16[32,16,640]{2,1,0:T(8,128)(2,1)} %payload.1), calls=%async_computation | async-start | bytes 1310720 | tf_op jit(solution)/shard_map/all_to_all | solution.py:542
  15.2 1.6 %collective-permute-start = (bf16[8,64,256]{2,1,0:T(8,128)(2,1)S(1)}, bf16[8,64,256]{2,1,0:T(8,128)(2,1)S(1)}, u32[]{:S(2)}, u32[]{:S(2)}) collective-permute-start(bf16[8,64,256]{2,1,0:T(8,128)(2,1)S(1)} %copy-done.2), channel_id=1, source_target_pairs={{0,1},{1,0},{2,3},{3,2},{4,5},{5,4},{6,7},{7,6},{8,9},{9,8},{10,11... | collective-permute-start | bytes 786440 | tf_op jit(solution)/shard_map/ppermute | solution.py:546
  22.7 46.1 %collective-permute-start.8 = (bf16[256,3584]{1,0:T(8,128)(2,1)}, bf16[256,3584]{1,0:T(8,128)(2,1)}, u32[]{:S(2)}, u32[]{:S(2)}) collective-permute-start(bf16[256,3584]{1,0:T(8,128)(2,1)} %get-tuple-element.39), channel_id=1, source_target_pairs={{0,1},{1,0},{2,3},{3,2},{4,5},{5,4},{6,7},{7,6},{8,9},{9,8},{10,11... | collective-permute-start | bytes 5505032 | tf_op jit(solution)/shard_map/ppermute | solution.py:548
  24.7 1.3 %copy-start = (bf16[8,256,512]{2,1,0:T(8,128)(2,1)}, bf16[8,256,512]{2,1,0:T(8,128)(2,1)S(1)}, u32[]{:S(2)}) copy-start(bf16[8,256,512]{2,1,0:T(8,128)(2,1)S(1)} %get-tuple-element.23.refs_2_) | copy-start | bytes 6291460
  32.7 1.6 %copy-start.1 = (bf16[8,256,512]{2,1,0:T(8,128)(2,1)S(1)}, bf16[8,256,512]{2,1,0:T(8,128)(2,1)}, u32[]{:S(2)}) copy-start(bf16[8,256,512]{2,1,0:T(8,128)(2,1)} %copy-done) | copy-start | bytes 6291460
  40.5 26.6 %all-to-all-start.1 = ((bf16[32,72,128]{2,1,0:T(8,128)(2,1)}), bf16[32,72,128]{2,1,0:T(8,128)(2,1)S(1)}, u32[]{:S(2)}, u32[]{:S(2)}) async-start(bf16[32,72,128]{2,1,0:T(8,128)(2,1)} %get-tuple-element.25.after), calls=%async_computation.1 | async-start | bytes 1179648 | tf_op jit(solution)/shard_map/all_to_all | solution.py:564
  48.0 7.5 %collective-permute-start.2 = (bf16[4,3584]{1,0:T(4,128)(2,1)S(1)}, bf16[4,3584]{1,0:T(4,128)(2,1)S(1)}, u32[]{:S(2)}, u32[]{:S(2)}) collective-permute-start(bf16[4,3584]{1,0:T(4,128)(2,1)S(1)} %get-tuple-element.28), channel_id=1, source_target_pairs={{0,64},{64,128},{128,192},{192,0},{1,65},{65,129},{129,193},{193,1... | collective-permute-start | bytes 86024 | tf_op jit(solution)/shard_map/ppermute | solution.py:538
  49.3 6.3 %collective-permute-start.3 = (bf16[4,3584]{1,0:T(4,128)(2,1)S(1)}, bf16[4,3584]{1,0:T(4,128)(2,1)S(1)}, u32[]{:S(2)}, u32[]{:S(2)}) collective-permute-start(bf16[4,3584]{1,0:T(4,128)(2,1)S(1)} %get-tuple-element.29), channel_id=1, source_target_pairs={{0,128},{64,192},{128,0},{192,64},{1,129},{65,193},{129,1},{193,65... | collective-permute-start | bytes 86024 | tf_op jit(solution)/shard_map/ppermute | solution.py:538
  51.8 3.8 %collective-permute-start.4 = (bf16[4,3584]{1,0:T(4,128)(2,1)S(1)}, bf16[4,3584]{1,0:T(4,128)(2,1)S(1)}, u32[]{:S(2)}, u32[]{:S(2)}) collective-permute-start(bf16[4,3584]{1,0:T(4,128)(2,1)S(1)} %get-tuple-element.30), channel_id=1, source_target_pairs={{0,192},{64,0},{128,64},{192,128},{1,193},{65,1},{129,65},{193,129... | collective-permute-start | bytes 86024 | tf_op jit(solution)/shard_map/ppermute | solution.py:538
  55.6 3.1 %collective-permute-start.5 = (bf16[16,3584]{1,0:T(8,128)(2,1)S(1)}, bf16[16,3584]{1,0:T(8,128)(2,1)S(1)}, u32[]{:S(2)}, u32[]{:S(2)}) collective-permute-start(bf16[16,3584]{1,0:T(8,128)(2,1)S(1)} %stack.1.own), channel_id=1, source_target_pairs={{0,1},{1,0},{2,3},{3,2},{4,5},{5,4},{6,7},{7,6},{8,9},{9,8},{10,11... | collective-permute-start | bytes 344072 | tf_op jit(solution)/shard_map/ppermute | solution.py:569
  60.4 1.4 %collective-permute-start.6 = (bf16[16,3584]{1,0:T(8,128)(2,1)S(1)}, bf16[16,3584]{1,0:T(8,128)(2,1)S(1)}, u32[]{:S(2)}, u32[]{:S(2)}) collective-permute-start(bf16[16,3584]{1,0:T(8,128)(2,1)S(1)} %get-tuple-element.34), channel_id=1, source_target_pairs={{0,1},{1,0},{2,3},{3,2},{4,5},{5,4},{6,7},{7,6},{8,9},{9,8},{10,11... | collective-permute-start | bytes 344072 | tf_op jit(solution)/shard_map/ppermute | solution.py:571
  61.8 7.0 %collective-permute-start.10 = (bf16[4,3584]{1,0:T(4,128)(2,1)S(1)}, bf16[4,3584]{1,0:T(4,128)(2,1)S(1)}, u32[]{:S(2)}, u32[]{:S(2)}) collective-permute-start(bf16[4,3584]{1,0:T(4,128)(2,1)S(1)} %get-tuple-element.42), channel_id=1, source_target_pairs={{0,128},{64,192},{128,0},{192,64},{1,129},{65,193},{129,1},{193,65... | collective-permute-start | bytes 86024 | tf_op jit(solution)/shard_map/ppermute | solution.py:538
  62.9 5.9 %collective-permute-start.11 = (bf16[4,3584]{1,0:T(4,128)(2,1)S(1)}, bf16[4,3584]{1,0:T(4,128)(2,1)S(1)}, u32[]{:S(2)}, u32[]{:S(2)}) collective-permute-start(bf16[4,3584]{1,0:T(4,128)(2,1)S(1)} %get-tuple-element.43), channel_id=1, source_target_pairs={{0,64},{64,128},{128,192},{192,0},{1,65},{65,129},{129,193},{193,1... | collective-permute-start | bytes 86024 | tf_op jit(solution)/shard_map/ppermute | solution.py:538
  64.6 4.2 %collective-permute-start.9 = (bf16[4,3584]{1,0:T(4,128)(2,1)S(1)}, bf16[4,3584]{1,0:T(4,128)(2,1)S(1)}, u32[]{:S(2)}, u32[]{:S(2)}) collective-permute-start(bf16[4,3584]{1,0:T(4,128)(2,1)S(1)} %get-tuple-element.41), channel_id=1, source_target_pairs={{0,192},{64,0},{128,64},{192,128},{1,193},{65,1},{129,65},{193,129... | collective-permute-start | bytes 86024 | tf_op jit(solution)/shard_map/ppermute | solution.py:538
  67.6 2.0 %collective-permute-start.7 = (bf16[8,256]{1,0:T(8,128)(2,1)S(1)}, bf16[8,256]{1,0:T(8,128)(2,1)S(1)}, u32[]{:S(2)}, u32[]{:S(2)}) collective-permute-start(bf16[8,256]{1,0:T(8,128)(2,1)S(1)} %merge.1.values), channel_id=1, source_target_pairs={{0,1},{1,0},{2,3},{3,2},{4,5},{5,4},{6,7},{7,6},{8,9},{9,8},{10,11... | collective-permute-start | bytes 12296 | tf_op jit(solution)/shard_map/ppermute | solution.py:576

commit v6 on v5

--- a/solution.py
+++ b/solution.py
@@ -113,6 +113,9 @@
 def attention_kernel(
     lengths,
     query,
+    query_one,
+    query_two,
+    query_three,
     lat_own,
     lat_far,
     rope_own,
@@ -130,6 +133,8 @@
     stat_rows,
     token_rows,
     lengths_in,
+    lat_in,
+    rope_in,
     ids_in,
     route_in,
     sems,
@@ -137,14 +142,25 @@
     scale,
     units,
 ):
-    peers, chunk, width = query.shape
+    ring, chunk, width = query.shape
+    peers = 4 * ring
     requests, positions, latent = lat_own.shape
     small = [
         pltpu.make_async_copy(lengths, lengths_in, sems.at[0]),
         pltpu.make_async_copy(ids, ids_in, sems.at[1]),
         pltpu.make_async_copy(route, route_in, sems.at[2]),
     ]
-    for copy in small:
+    large = [
+        pltpu.make_async_copy(rope_own, rope_in, sems.at[3]),
+    ] + [
+        pltpu.make_async_copy(
+            lat_own.at[pl.ds(half_of, requests // 2)],
+            lat_in.at[pl.ds(half_of, requests // 2)],
+            sems.at[4 + half_of // (requests // 2)],
+        )
+        for half_of in range(0, requests, requests // 2)
+    ]
+    for copy in small + large:
         copy.start()
     rope = rope_own.shape[1]
     tiles = latent // LANES
@@ -154,9 +170,12 @@
     core = lax.axis_index("c")
     rows = peers * heads
 
-    for tile in range(tiles + 1):
-        piece = query[:, :, tile * LANES : (tile + 1) * LANES].astype(F32)
-        query_rows[tile] = piece.reshape(peers * chunk, LANES)
+    row = lax.axis_index("y")
+    for step, source in enumerate((query, query_one, query_two, query_three)):
+        begin = pl.multiple_of(lax.rem(row + 4 - step, 4) * (ring * chunk), ring * chunk)
+        for tile in range(tiles + 1):
+            piece = source[:, :, tile * LANES : (tile + 1) * LANES].astype(F32)
+            query_rows[tile, pl.ds(begin, ring * chunk), :] = piece.reshape(ring * chunk, LANES)
 
     half = token_rows.shape[1] // (peers * heads)
     for peer in range(peers):
@@ -204,41 +223,55 @@
     base_own = shard * positions
     base_far = (shard + 1 - 2 * core) * positions
     place = lax.broadcasted_iota(jnp.int32, (rows, positions), 1)
+    queries = []
     for request in range(requests):
-        mine = jnp.concatenate(
-            [
-                jnp.concatenate(
-                    [
-                        query_rows[tile, pl.ds(requests * head + request, peers, stride=chunk), :]
-                        for tile in range(tiles + 1)
-                    ],
-                    axis=1,
-                )
-                for head in range(heads)
-            ],
-            axis=0,
-        ).astype(BF16)
-        length = lengths_in[request]
-        parts = []
-        for lat, rot, base in ((lat_own, rope_own, base_own), (lat_far, rope_far, base_far)):
-            score = (
-                lax.dot_general(
-                    mine[:, :latent],
-                    lat[request],
-                    (((1,), (1,)), ((), ())),
-                    preferred_element_type=F32,
-                )
-                + jnp.dot(
-                    mine[:, latent : latent + rope], rot[request], preferred_element_type=F32
-                )
-            ) * scale
-            usable = place < length - base
-            parts.append((jnp.where(usable, score, -1e30), usable, lat))
+        queries.append(
+            jnp.concatenate(
+                [
+                    jnp.concatenate(
+                        [
+                            query_rows[
+                                tile, pl.ds(requests * head + request, peers, stride=chunk), :
+                            ]
+                            for tile in range(tiles + 1)
+                        ],
+                        axis=1,
+                    )
+                    for head in range(heads)
+                ],
+                axis=0,
+            ).astype(BF16)
+        )
+
+    def scores(request, lat, rot, base):
+        mine = queries[request]
+        score = (
+            lax.dot_general(
+                mine[:, :latent],
+                lat[request],
+                (((1,), (1,)), ((), ())),
+                preferred_element_type=F32,
+            )
+            + jnp.dot(mine[:, latent : latent + rope], rot[request], preferred_element_type=F32)
+        ) * scale
+        usable = place < lengths_in[request] - base
+        return jnp.where(usable, score, -1e30), usable
+
+    for request in range(requests):
+        if request == 0:
+            large[0].wait()
+            large[1].wait()
+        if request == requests // 2:
+            large[2].wait()
+        parts = [
+            scores(request, lat_in, rope_in, base_own),
+            scores(request, lat_far, rope_far, base_far),
+        ]
         top = jnp.max(jnp.maximum(parts[0][0], parts[1][0]), axis=1, keepdims=True)
-        weights = [jnp.where(usable, jnp.exp(score - top), 0.0) for score, usable, _ in parts]
+        weights = [jnp.where(usable, jnp.exp(score - top), 0.0) for score, usable in parts]
         total = jnp.sum(weights[0] + weights[1], axis=1, keepdims=True)
         weighted = jnp.dot(
-            weights[0].astype(BF16), lat_own[request], preferred_element_type=F32
+            weights[0].astype(BF16), lat_in[request], preferred_element_type=F32
         ) + jnp.dot(weights[1].astype(BF16), lat_far[request], preferred_element_type=F32)
         partial = weighted * (1.0 / jnp.maximum(total, 1.0))
         for index, term in enumerate(three_terms(top) + three_terms(total)):
@@ -260,17 +293,17 @@
 
 
 def attention(lengths, query, lat_own, lat_far, rope_own, rope_far, ids, route, scale, span, units):
-    peers, chunk, width = query.shape
+    peers, chunk, width = 4 * query[0].shape[0], *query[0].shape[1:]
     requests, positions, latent = lat_own.shape
     rope = rope_own.shape[1]
     tiles = latent // LANES
-    lengths, ids, route = pinned(lengths, ids, route)
+    lengths, lat_own, rope_own, ids, route = pinned(lengths, lat_own, rope_own, ids, route)
     return pl.pallas_call(
         lambda *refs: attention_kernel(*refs, scale=scale, units=units),
         out_shape=[jax.ShapeDtypeStruct((peers, tiles * chunk + ROWS, LANES), BF16)]
         + [jax.ShapeDtypeStruct((CAP, peers * span), BF16)] * 4
         + [jax.ShapeDtypeStruct((ROWS, LANES), F32)],
-        in_specs=[HBM] + [VMEM] * 5 + [HBM] * 2,
+        in_specs=[HBM] + [VMEM] * 4 + [HBM, VMEM, HBM, VMEM, HBM, HBM],
         out_specs=[VMEM] * 6,
         scratch_shapes=[
             pltpu.VMEM((width // LANES, peers * chunk, LANES), F32),
@@ -278,9 +311,11 @@
             pltpu.VMEM((peers * ROWS, LANES), F32),
             pltpu.VMEM((requests, peers * span), F32),
             pltpu.SMEM(lengths.shape, jnp.int32),
+            pltpu.VMEM(lat_own.shape, BF16),
+            pltpu.VMEM(rope_own.shape, BF16),
             pltpu.VMEM(ids.shape, jnp.int32),
             pltpu.VMEM(route.shape, F32),
-            pltpu.SemaphoreType.DMA((3,)),
+            pltpu.SemaphoreType.DMA((6,)),
         ],
         compiler_params=params(24),
         cost_estimate=pl.CostEstimate(
@@ -289,7 +324,7 @@
             transcendentals=peers * chunk * 2 * positions,
         ),
         name="attention",
-    )(lengths, query, lat_own, lat_far, rope_own, rope_far, ids, route)
+    )(lengths, *query, lat_own, lat_far, rope_own, rope_far, ids, route)
 
 
 def stack_kernel(after, *refs):
@@ -310,7 +345,7 @@
     )(after, *values)
 
 
-def experts_kernel(own, far, gate, up, down, keep, send):
+def experts_kernel(own, far, gate, up, down, *outs):
     depth, units = gate.shape
     width = down.shape[1]
     span = 112
@@ -343,29 +378,22 @@
             )
     gate_proj, up_proj = total[:, :units], total[:, units:]
     hidden = (gate_proj * jax.nn.sigmoid(gate_proj) * up_proj).astype(BF16)
-    pair = 2 * span
-    step = 8 * span
+    step = 1024
     for start in range(0, width, step):
-        result = jnp.dot(hidden, down[:, start : start + step], preferred_element_type=F32)
-        evens, odds = [], []
-        for inner in range(0, step, pair):
-            evens.append(result[:, inner : inner + span])
-            odds.append(result[:, inner + span : inner + pair])
-        even, odd = jnp.concatenate(evens, axis=1), jnp.concatenate(odds, axis=1)
-        here = slice(start // 2, (start + step) // 2)
-        keep[:, here] = jnp.where(core == 1, odd, even)
-        send[:, here] = jnp.where(core == 1, even, odd).astype(BF16)
+        here = slice(start, start + step)
+        result = jnp.dot(hidden, down[:, here], preferred_element_type=F32).astype(BF16)
+        for block, out in enumerate(outs):
+            out[:, here] = result[CAP * block : CAP * (block + 1)]
 
 
 def experts(own, far, gate, up, down):
     depth, units = gate.shape
     width = down.shape[1]
-    shape = (own.shape[0], width // 2)
     return pl.pallas_call(
         experts_kernel,
-        out_shape=[jax.ShapeDtypeStruct(shape, F32), jax.ShapeDtypeStruct(shape, BF16)],
+        out_shape=[jax.ShapeDtypeStruct((CAP, width), BF16)] * 4,
         in_specs=[VMEM] * 5,
-        out_specs=[VMEM] * 2,
+        out_specs=[VMEM] * 4,
         compiler_params=params(16),
         cost_estimate=pl.CostEstimate(
             flops=2 * 16 * 3 * depth * units, bytes_accessed=6 * 2**20, transcendentals=0
@@ -374,26 +402,20 @@
     )(own, far, gate, up, down)
 
 
-def pair_kernel(keep, taken, *outs):
-    total = (keep[...] + taken[...].astype(F32)).astype(BF16)
-    for block, out in enumerate(outs):
-        out[...] = total[CAP * block : CAP * (block + 1)]
-
-
-def pair(keep, taken):
-    width = keep.shape[1]
-    return pl.pallas_call(
-        pair_kernel,
-        out_shape=[jax.ShapeDtypeStruct((CAP, width), BF16)] * 4,
-        in_specs=[VMEM] * 2,
-        out_specs=[VMEM] * 4,
-        compiler_params=params(8),
-        name="pair",
-    )(keep, taken)
-
-
-def merge_kernel(after, got, value, out):
+def merge_kernel(after, got, value, project, out, value_in, project_in, sems):
     del after
+    copy = pltpu.make_async_copy(value, value_in, sems.at[0])
+    copy.start()
+    step = project.shape[1] // 4
+    moves = []
+    for index in range(4):
+        columns = pl.ds(index * step, step)
+        moves.append(
+            pltpu.make_async_copy(
+                project.at[:, columns], project_in.at[:, columns], sems.at[index + 1]
+            )
+        )
+        moves[index].start()
     peers, height, _ = got.shape
     heads = value.shape[0]
     chunk = ROWS * heads
@@ -421,95 +443,89 @@
         columns.append(jnp.sum(piece * share, axis=0) / denominator)
     merged = jnp.concatenate(columns, axis=1)
     values = []
+    copy.wait()
     for head in range(heads):
         rows = merged[ROWS * head : ROWS * (head + 1)].astype(BF16)
-        values.append(jnp.dot(rows, value[head], preferred_element_type=F32))
-    out[...] = jnp.concatenate(values, axis=1).astype(BF16)
-
-
-def merge(after, got, value):
-    heads, latent, width = value.shape
+        values.append(jnp.dot(rows, value_in[head], preferred_element_type=F32))
+    head_values = jnp.concatenate(values, axis=1).astype(BF16)
+    for index, move in enumerate(moves):
+        here = slice(index * step, (index + 1) * step)
+        move.wait()
+        out[:, here] = jnp.dot(head_values, project_in[:, here], preferred_element_type=F32)
+
+
+def merge(after, got, value, project):
+    depth, width = project.shape
     return pl.pallas_call(
         merge_kernel,
-        out_shape=jax.ShapeDtypeStruct((ROWS, heads * width), BF16),
-        in_specs=[ANY] + [VMEM] * 2,
+        out_shape=jax.ShapeDtypeStruct((ROWS, width), F32),
+        in_specs=[ANY, VMEM] + [HBM] * 2,
         out_specs=VMEM,
+        scratch_shapes=[
+            pltpu.VMEM(value.shape, BF16),
+            pltpu.VMEM(project.shape, BF16),
+            pltpu.SemaphoreType.DMA((5,)),
+        ],
         compiler_params=params(16),
         cost_estimate=pl.CostEstimate(
-            flops=2 * ROWS * heads * latent * width, bytes_accessed=2**20, transcendentals=0
+            flops=2 * ROWS * depth * width, bytes_accessed=4 * 2**20, transcendentals=0
         ),
         name="merge",
-    )(after, got, value)
-
-
-def finish_kernel(
-    values, values_far, project, project_far, mix, back_0, back_1, back_2, back_3, out
-):
-    peers, _, span = out.shape
+    )(after, got, *pinned(value, project))
+
+
+def finish_kernel(attended, mix, back_0, back_1, back_2, back_3, keep, send):
+    peers, _, span = keep.shape
+    core = lax.axis_index("c")
     back = jnp.concatenate(
         [ref[...].astype(F32) for ref in (back_0, back_1, back_2, back_3)], axis=0
     ).astype(BF16)
     mixing = mix[...][:, : 4 * CAP]
     high = mixing.astype(BF16)
     low = (mixing - high.astype(F32)).astype(BF16)
-    step = 8 * span
-    for start in range(0, peers * span, step):
-        here = slice(start, start + step)
-        routed = jnp.dot(high, back[:, here], preferred_element_type=F32) + jnp.dot(
-            low, back[:, here], preferred_element_type=F32
-        )
-        attended = jnp.dot(
-            values[...], project[:, here], preferred_element_type=F32
-        ) + jnp.dot(values_far[...], project_far[:, here], preferred_element_type=F32)
-        both = jnp.concatenate([attended, routed], axis=0)
-        for inner in range(8):
-            out[start // span + inner] = both[:, inner * span : (inner + 1) * span].astype(BF16)
-
-
-def finish(values, values_far, project, project_far, mix, back, peers, span):
+    step = 16 * span
+    for parity in range(2):
+
+        @pl.when(core == parity)
+        def _():
+            outs = (keep, send) if parity == 0 else (send, keep)
+            for start in range(0, 2 * peers * span, step):
+                here = slice(start, start + step)
+                routed = jnp.dot(high, back[:, here], preferred_element_type=F32) + jnp.dot(
+                    low, back[:, here], preferred_element_type=F32
+                )
+                both = jnp.concatenate([attended[:, here], routed], axis=0)
+                for inner in range(16):
+                    piece = both[:, inner * span : (inner + 1) * span]
+                    outs[inner % 2][(start // span + inner) // 2] = piece.astype(BF16)
+
+
+def finish(attended, mix, back, peers):
+    rows, width = attended.shape
+    shape = (peers, 2 * rows, width // (2 * peers))
     return pl.pallas_call(
         finish_kernel,
-        out_shape=jax.ShapeDtypeStruct((peers, 2 * ROWS, span), BF16),
-        in_specs=[VMEM] * 9,
-        out_specs=VMEM,
+        out_shape=[jax.ShapeDtypeStruct(shape, BF16)] * 2,
+        in_specs=[VMEM] * 6,
+        out_specs=[VMEM] * 2,
         compiler_params=params(16),
         name="finish",
-    )(values, values_far, project, project_far, mix, *back)
-
-
-def split_kernel(after, project, mine, theirs):
-    del after
-    span = 112
-    step = 8 * span
-    core = lax.axis_index("c")
-
-    @pl.loop(0, project.shape[0] // 32)
-    def _(block):
-        rows = pl.ds(pl.multiple_of(block * 32, 32), 32)
-        for start in range(0, project.shape[1], 2 * step):
-            piece = project[rows, start : start + 2 * step].astype(F32)
-            even = jnp.concatenate(
-                [piece[:, 2 * i * span : (2 * i + 1) * span] for i in range(8)], axis=1
-            )
-            odd = jnp.concatenate(
-                [piece[:, (2 * i + 1) * span : (2 * i + 2) * span] for i in range(8)], axis=1
-            )
-            here = slice(start // 2, start // 2 + step)
-            mine[rows, here] = jnp.where(core == 1, odd, even).astype(BF16)
-            theirs[rows, here] = jnp.where(core == 1, even, odd).astype(BF16)
-
-
-def split(after, project):
-    depth, width = project.shape
-    return pl.pallas_call(
-        split_kernel,
-        out_shape=[pltpu.HBM((depth, width // 2), BF16)] * 2,
-        in_specs=[ANY, VMEM],
-        out_specs=[VMEM] * 2,
-        compiler_params=params(20),
-        cost_estimate=pl.CostEstimate(flops=0, bytes_accessed=8 * 2**20, transcendentals=0),
-        name="split",
-    )(after, *pinned(project))
+    )(attended, mix, *back)
+
+
+def pair_kernel(keep, taken, out):
+    out[...] = (keep[...].astype(F32) + taken[...].astype(F32)).astype(BF16)
+
+
+def pair(keep, taken):
+    return pl.pallas_call(
+        pair_kernel,
+        out_shape=jax.ShapeDtypeStruct(taken.shape, BF16),
+        in_specs=[VMEM] * 2,
+        out_specs=VMEM,
+        compiler_params=params(8),
+        name="pair",
+    )(keep, taken)
 
 
 def shards(
@@ -539,21 +555,22 @@
             value, "x", [(i, (i + shift) % group_count) for i in range(group_count)]
         )
 
-    query = lax.all_to_all(
-        payload(query_lat, query_rope, moe_tokens, peers), plane, 0, 0, tiled=True
-    )
+    column, depth = lax.axis_size("y"), lax.axis_size("z")
+    sent = payload(query_lat, query_rope, moe_tokens, depth)
+    near_query = lax.all_to_all(sent, "z", 0, 0, tiled=True)
+    query = [near_query] + [
+        lax.ppermute(near_query, "y", [(i, (i + d) % column) for i in range(column)])
+        for d in range(1, column)
+    ]
+    rope_far = lax.ppermute(cache_rope, "c", swap)
     lat_far = lax.ppermute(cache_lat, "c", swap)
-    rope_far = lax.ppermute(cache_rope, "c", swap)
-    project, theirs = split(rope_far, w_out)
-    project_far = lax.ppermute(theirs, "c", swap)
-    lat_own, rope_own = fetch(rope_far, cache_lat, cache_rope)
     scale = (w_value.shape[2] + query_rope.shape[2]) ** (-0.5)
     part, *send, mix = attention(
         lengths,
         query,
-        lat_own,
+        cache_lat,
         lat_far,
-        rope_own,
+        cache_rope,
         rope_far,
         expert_ids,
         route_weights,
@@ -567,14 +584,12 @@
     gate, up, down = fetch(part, w_gate, w_up, w_down)
     own = stack(gate, *near)
     far = lax.ppermute(own, "c", swap)
-    keep, give = experts(own, far, gate, up, down)
-    routed = pair(keep, lax.ppermute(give, "c", swap))
+    routed = experts(own, far, gate, up, down)
     back = [routed[0]] + [along_x(routed[d], -d) for d in range(1, group_count)]
 
-    project, value = fetch(routed[0], project, w_value)
-    values = merge(routed[0], got, value)
-    values_far = lax.ppermute(values, "c", swap)
-    terms = finish(values, values_far, project, project_far, mix, back, peers, span)
+    attended = merge(routed[0], got, w_value, w_out)
+    keep, give = finish(attended, mix, back, peers)
+    terms = pair(keep, lax.ppermute(give, "c", swap))
     arrived = lax.all_to_all(terms, plane, 0, 0, tiled=True)
     summed = jnp.sum(arrived.astype(F32), axis=0).astype(BF16)
     return (summed[:requests], summed[requests:])

time: 91.5 us -> 85.5 us (0.934)
  Pallas kernels: 24 us -> 15.4 us
  waiting for transfers between devices: 10.7 us -> 15.8 us
  local copies, waits for them, and re-layouts: 3.52 us -> 0.59 us
  starting transfers between devices: 33.4 us -> 34.9 us
  blocking collectives: 18.5 us -> 17.4 us
    pallas_call x5 -> x4, Pallas kernels: 10.3 us -> 4.27 us  [the longest x1 2.4 us: merge(): pl.pallas_call(merge_kernel, out_shape=jax.ShapeDtypeStruct((ROWS, width)...]
    ppermute x3 -> x4, starting transfers between devices: 1.94 us -> 7.71 us  [the longest x3 4.99 us: shards(): lax.ppermute(near_query, 'y', [(i, (i + d) % column) for i in range(colum...]
    ppermute x3 -> x4, waiting for transfers between devices: 1.77 us -> 5.85 us  [the longest x3 4.86 us: shards(): lax.ppermute(near_query, 'y', [(i, (i + d) % column) for i in range(colum...]
    pallas_call x3 -> x1, Pallas kernels: 5.76 us -> 2.63 us  [fetch(): pl.pallas_call(fetch_kernel, out_shape=[pltpu.VMEM(value.shape, value.dty...]
    all_to_all x1, starting transfers between devices: 9.48 us -> 6.46 us  [shards(): near_query = lax.all_to_all(sent, 'z', 0, 0, tiled=True)]
    unnamed x6 -> x0, local copies, waits for them, and re-layouts: 2.93 us -> none
    all_to_all x1, starting transfers between devices: 7.51 us -> 5.29 us  [shards(): got = lax.all_to_all(part, plane, 0, 0, tiled=True)]
    all_to_all x1, waiting for transfers between devices: 6.73 us -> 8.92 us  [shards(): near_query = lax.all_to_all(sent, 'z', 0, 0, tiled=True)]
  transfers between devices with their start and end apart: 14 -> 15, of which waited for: 5 -> 6; matrix products, arithmetic and copies ran while one was open for 0% -> 0% of each run, Pallas kernels for 24% -> 9%
where the time goes in v6:
time: 85.5 us; the launch traced here: 84.9 us
  starting transfers between devices  34.9 us (41%)
  blocking collectives  17.4 us (20%)
  waiting for transfers between devices  15.8 us (18%)
  Pallas kernels  15.4 us (18%)
    all_to_all x1, blocking collectives, shards(): arrived = lax.all_to_all(terms, plane, 0, 0, tiled=True)  17.4 us
    all_to_all x1, waiting for transfers between devices, shards(): near_query = lax.all_to_all(sent, 'z', 0, 0, tiled=True)  8.92 us
    ppermute x6, starting transfers between devices, along_x(): lax.ppermute(value, 'x', [(i, (i + shift) % group_count) for i in range(g...  8.65 us
    pallas_call x1, Pallas kernels, attention(): pl.pallas_call(lambda *refs: attention_kernel(*refs, scale=scale, units=u...  6.96 us
    all_to_all x1, starting transfers between devices, shards(): near_query = lax.all_to_all(sent, 'z', 0, 0, tiled=True)  6.46 us
    all_to_all x1, starting transfers between devices, shards(): got = lax.all_to_all(part, plane, 0, 0, tiled=True)  5.29 us
    ppermute x3, starting transfers between devices, shards(): lax.ppermute(near_query, 'y', [(i, (i + d) % column) for i in range(colum...  4.99 us
    ppermute x3, waiting for transfers between devices, shards(): lax.ppermute(near_query, 'y', [(i, (i + d) % column) for i in range(colum...  4.86 us
  transfers between devices with their start and end apart: 15, of which 6 were waited for; matrix products, arithmetic and copies ran while one was open for 0% of the time, Pallas kernels for 9%

profile of v6, /device:TPU:1, one launch (start us, length us, event | category | flops | bytes accessed | tf_op | source)
XLA Modules:
  0.0 84.9 jit_solution(18303756244267981040)
XLA Ops:
  0.6 3.3 %collective-permute-start.3 = (bf16[8,256,512]{2,1,0:T(8,128)(2,1)}, bf16[8,256,512]{2,1,0:T(8,128)(2,1)S(1)}, u32[]{:S(2)}, u32[]{:S(2)}) collective-permute-start(bf16[8,256,512]{2,1,0:T(8,128)(2,1)} %refs_5_.1), channel_id=1, source_target_pairs={{0,1},{1,0},{2,3},{3,2},{4,5},{5,4},{6,7},{7,6},{8,9},{9,8},{10,11... | collective-permute-start | bytes 6291464 | tf_op jit(solution)/shard_map/ppermute | solution.py:566
  4.0 1.5 %payload.1 = bf16[8,16,640]{2,1,0:T(8,128)(2,1)} custom-call(bf16[8,2,512]{2,1,0:T(2,128)(2,1)} %query_lat.1, bf16[8,2,64]{2,1,0:T(2,128)(2,1)} %query_rope.1, bf16[8,112]{1,0:T(8,128)(2,1)} %tokens.1), custom_call_target="tpu_custom_call" | custom-call | tf_op jit(solution)/shard_map/payload/pallas_call | solution.py:97
  5.4 6.5 %all-to-all-start = ((bf16[8,16,640]{2,1,0:T(8,128)(2,1)}), bf16[8,16,640]{2,1,0:T(8,128)(2,1)S(1)}, u32[]{:S(2)}, u32[]{:S(2)}) async-start(bf16[8,16,640]{2,1,0:T(8,128)(2,1)} %payload.1), calls=%async_computation | async-start | bytes 327680 | tf_op jit(solution)/shard_map/all_to_all | solution.py:560
  12.2 8.9 %all-to-all-done.refs_1_ = bf16[8,16,640]{2,1,0:T(8,128)(2,1)S(1)} async-done(((bf16[8,16,640]{2,1,0:T(8,128)(2,1)}), bf16[8,16,640]{2,1,0:T(8,128)(2,1)S(1)}, u32[]{:S(2)}, u32[]{:S(2)}) %all-to-all-start) | async-done | bytes 163872 | tf_op jit(solution)/shard_map/all_to_all | solution.py:560
  21.1 1.3 %collective-permute-start = (bf16[8,16,640]{2,1,0:T(8,128)(2,1)S(1)}, bf16[8,16,640]{2,1,0:T(8,128)(2,1)S(1)}, u32[]{:S(2)}, u32[]{:S(2)}) collective-permute-start(bf16[8,16,640]{2,1,0:T(8,128)(2,1)S(1)} %all-to-all-done.refs_1_), channel_id=1, source_target_pairs={{0,16},{16,32},{32,48},{48,0},{1,17},{17,33},{33,49},{49,1},{2,18}... | collective-permute-start | bytes 491528 | tf_op jit(solution)/shard_map/ppermute | solution.py:562
  22.4 2.6 %collective-permute-start.1 = (bf16[8,16,640]{2,1,0:T(8,128)(2,1)S(1)}, bf16[8,16,640]{2,1,0:T(8,128)(2,1)S(1)}, u32[]{:S(2)}, u32[]{:S(2)}) collective-permute-start(bf16[8,16,640]{2,1,0:T(8,128)(2,1)S(1)} %all-to-all-done.refs_1_), channel_id=1, source_target_pairs={{0,32},{16,48},{32,0},{48,16},{1,33},{17,49},{33,1},{49,17},{2,34}... | collective-permute-start | bytes 491528 | tf_op jit(solution)/shard_map/ppermute | solution.py:562
  25.0 1.1 %collective-permute-start.2 = (bf16[8,16,640]{2,1,0:T(8,128)(2,1)S(1)}, bf16[8,16,640]{2,1,0:T(8,128)(2,1)S(1)}, u32[]{:S(2)}, u32[]{:S(2)}) collective-permute-start(bf16[8,16,640]{2,1,0:T(8,128)(2,1)S(1)} %all-to-all-done.refs_1_), channel_id=1, source_target_pairs={{0,48},{16,0},{32,16},{48,32},{1,49},{17,1},{33,17},{49,33},{2,50}... | collective-permute-start | bytes 491528 | tf_op jit(solution)/shard_map/ppermute | solution.py:562
  26.6 4.4 %collective-permute-done.1.refs_3_ = bf16[8,16,640]{2,1,0:T(8,128)(2,1)S(1)} collective-permute-done((bf16[8,16,640]{2,1,0:T(8,128)(2,1)S(1)}, bf16[8,16,640]{2,1,0:T(8,128)(2,1)S(1)}, u32[]{:S(2)}, u32[]{:S(2)}) %collective-permute-start.1) | collective-permute-done | bytes 163872 | tf_op jit(solution)/shard_map/ppermute | solution.py:562
  31.0 7.0 %attention.1 = (bf16[32,72,128]{2,1,0:T(8,128)(2,1)}, bf16[4,3584]{1,0:T(4,128)(2,1)S(1)}, bf16[4,3584]{1,0:T(4,128)(2,1)S(1)}, bf16[4,3584]{1,0:T(4,128)(2,1)S(...) custom-call(s32[8]{0:T(128)} %refs_0_.2, bf16[8,16,640]{2,1,0:T(8,128)(2,1)S(1)} %all-to-all-done.refs_1_, ...), custom_call_target="tpu_custom_call" | custom-call | flops 570425344 | bytes 6291456 | tf_op jit(solution)/shard_map/attention/pallas_call | solution.py:301
  37.9 5.3 %all-to-all-start.1 = ((bf16[32,72,128]{2,1,0:T(8,128)(2,1)}), bf16[32,72,128]{2,1,0:T(8,128)(2,1)S(1)}, u32[]{:S(2)}, u32[]{:S(2)}) async-start(bf16[32,72,128]{2,1,0:T(8,128)(2,1)} %get-tuple-element.17.after), calls=%async_computation.1 | async-start | bytes 1179648 | tf_op jit(solution)/shard_map/all_to_all | solution.py:581
  43.2 1.3 %collective-permute-start.5 = (bf16[4,3584]{1,0:T(4,128)(2,1)S(1)}, bf16[4,3584]{1,0:T(4,128)(2,1)S(1)}, u32[]{:S(2)}, u32[]{:S(2)}) collective-permute-start(bf16[4,3584]{1,0:T(4,128)(2,1)S(1)} %get-tuple-element.20), channel_id=1, source_target_pairs={{0,64},{64,128},{128,192},{192,0},{1,65},{65,129},{129,193},{193,1... | collective-permute-start | bytes 86024 | tf_op jit(solution)/shard_map/ppermute | solution.py:554
  44.5 2.5 %collective-permute-start.6 = (bf16[4,3584]{1,0:T(4,128)(2,1)S(1)}, bf16[4,3584]{1,0:T(4,128)(2,1)S(1)}, u32[]{:S(2)}, u32[]{:S(2)}) collective-permute-start(bf16[4,3584]{1,0:T(4,128)(2,1)S(1)} %get-tuple-element.21), channel_id=1, source_target_pairs={{0,128},{64,192},{128,0},{192,64},{1,129},{65,193},{129,1},{193,65... | collective-permute-start | bytes 86024 | tf_op jit(solution)/shard_map/ppermute | solution.py:554
  47.0 1.2 %collective-permute-start.7 = (bf16[4,3584]{1,0:T(4,128)(2,1)S(1)}, bf16[4,3584]{1,0:T(4,128)(2,1)S(1)}, u32[]{:S(2)}, u32[]{:S(2)}) collective-permute-start(bf16[4,3584]{1,0:T(4,128)(2,1)S(1)} %get-tuple-element.22), channel_id=1, source_target_pairs={{0,192},{64,0},{128,64},{192,128},{1,193},{65,1},{129,65},{193,129... | collective-permute-start | bytes 86024 | tf_op jit(solution)/shard_map/ppermute | solution.py:554
  48.1 2.6 %fetch.1 = (bf16[7168,128]{1,0:T(8,128)(2,1)S(1)}, bf16[7168,128]{1,0:T(8,128)(2,1)S(1)}, bf16[128,7168]{1,0:T(8,128)(2,1)S(1)}) custom-call(bf16[32,72,128]{2,1,0:T(8,128)(2,1)} %get-tuple-element.17.after, bf16[7168,128]{1,0:T(8,128)(2,1)} %refs_0_.3, bf16[7168,128]{1,0:T(8,128)(2,1)} %refs_1_.1, bf16[128,7168]{1,0:T(8,128)(2,1)} %refs_2_.1), custom_call_target="tpu_custom_call" | custom-call | bytes 5505024 | tf_op jit(solution)/shard_map/fetch/pallas_call | solution.py:53
  50.8 3.1 %collective-permute-start.8 = (bf16[16,3584]{1,0:T(8,128)(2,1)S(1)}, bf16[16,3584]{1,0:T(8,128)(2,1)S(1)}, u32[]{:S(2)}, u32[]{:S(2)}) collective-permute-start(bf16[16,3584]{1,0:T(8,128)(2,1)S(1)} %stack.1.own), channel_id=1, source_target_pairs={{0,1},{1,0},{2,3},{3,2},{4,5},{5,4},{6,7},{7,6},{8,9},{9,8},{10,11... | collective-permute-start | bytes 344072 | tf_op jit(solution)/shard_map/ppermute | solution.py:586
  54.0 1.0 %collective-permute-done.8.far = bf16[16,3584]{1,0:T(8,128)(2,1)S(1)} collective-permute-done((bf16[16,3584]{1,0:T(8,128)(2,1)S(1)}, bf16[16,3584]{1,0:T(8,128)(2,1)S(1)}, u32[]{:S(2)}, u32[]{:S(2)}) %collective-permute-start.8) | collective-permute-done | bytes 114720 | tf_op jit(solution)/shard_map/ppermute | solution.py:586
  54.9 1.4 %experts.1 = (bf16[4,7168]{1,0:T(4,128)(2,1)S(1)}, bf16[4,7168]{1,0:T(4,128)(2,1)S(1)}, bf16[4,7168]{1,0:T(4,128)(2,1)S(1)}, bf16[4,7168]{1,0:T(4,128)(2,1)S(1)}) custom-call(bf16[16,3584]{1,0:T(8,128)(2,1)S(1)} %stack.1.own, bf16[16,3584]{1,0:T(8,128)(2,1)S(1)} %collective-permute-done.8.far, bf16[7168,128]{1,0:T(8,128)(2,1)S(1)} %get-tuple-element.18.after.gate, ...), custom_call_target="tpu_custom_call" | custom-call | flops 88080384 | bytes 6291456 | tf_op jit(solution)/shard_map/experts/pallas_call | solution.py:392
  56.3 1.1 %collective-permute-start.10 = (bf16[4,7168]{1,0:T(4,128)(2,1)S(1)}, bf16[4,7168]{1,0:T(4,128)(2,1)S(1)}, u32[]{:S(2)}, u32[]{:S(2)}) collective-permute-start(bf16[4,7168]{1,0:T(4,128)(2,1)S(1)} %get-tuple-element.28), channel_id=1, source_target_pairs={{0,128},{64,192},{128,0},{192,64},{1,129},{65,193},{129,1},{193,65... | collective-permute-start | bytes 172040 | tf_op jit(solution)/shard_map/ppermute | solution.py:554
  57.4 1.7 %collective-permute-start.11 = (bf16[4,7168]{1,0:T(4,128)(2,1)S(1)}, bf16[4,7168]{1,0:T(4,128)(2,1)S(1)}, u32[]{:S(2)}, u32[]{:S(2)}) collective-permute-start(bf16[4,7168]{1,0:T(4,128)(2,1)S(1)} %get-tuple-element.29), channel_id=1, source_target_pairs={{0,64},{64,128},{128,192},{192,0},{1,65},{65,129},{129,193},{193,1... | collective-permute-start | bytes 172040 | tf_op jit(solution)/shard_map/ppermute | solution.py:554
  59.1 1.0 %collective-permute-start.9 = (bf16[4,7168]{1,0:T(4,128)(2,1)S(1)}, bf16[4,7168]{1,0:T(4,128)(2,1)S(1)}, u32[]{:S(2)}, u32[]{:S(2)}) collective-permute-start(bf16[4,7168]{1,0:T(4,128)(2,1)S(1)} %get-tuple-element.27), channel_id=1, source_target_pairs={{0,192},{64,0},{128,64},{192,128},{1,193},{65,1},{129,65},{193,129... | collective-permute-start | bytes 172040 | tf_op jit(solution)/shard_map/ppermute | solution.py:554
  60.1 2.4 %merge.1.attended = f32[8,7168]{1,0:T(8,128)S(1)} custom-call(bf16[4,7168]{1,0:T(4,128)(2,1)S(1)} %get-tuple-element.25.after.back_0, bf16[32,72,128]{2,1,0:T(8,128)(2,1)S(1)} %all-to-all-done.1.got, bf16[2,512,128]{2,1,0:T(8,128)(2,1)} %value.1, bf16[256,7168]{1,0:T(8,128)(2,1)} %project.1), custom_call_target="tpu_custom_call" | custom-call | flops 29360128 | bytes 4194304 | tf_op jit(solution)/shard_map/merge/pallas_call | solution.py:459
  63.0 2.7 %collective-permute-start.12 = (bf16[32,16,112]{2,1,0:T(8,128)(2,1)S(1)}, bf16[32,16,112]{2,1,0:T(8,128)(2,1)S(1)}, u32[]{:S(2)}, u32[]{:S(2)}) collective-permute-start(bf16[32,16,112]{2,1,0:T(8,128)(2,1)S(1)} %get-tuple-element.31), channel_id=1, source_target_pairs={{0,1},{1,0},{2,3},{3,2},{4,5},{5,4},{6,7},{7,6},{8,9},{9,8},{10,11... | collective-permute-start | bytes 344072 | tf_op jit(solution)/shard_map/ppermute | solution.py:592
  65.8 1.0 %collective-permute-done.12.taken = bf16[32,16,112]{2,1,0:T(8,128)(2,1)S(1)} collective-permute-done((bf16[32,16,112]{2,1,0:T(8,128)(2,1)S(1)}, bf16[32,16,112]{2,1,0:T(8,128)(2,1)S(1)}, u32[]{:S(2)}, u32[]{:S(2)}) %collective-permute-start.12) | collective-permute-done | bytes 114720 | tf_op jit(solution)/shard_map/ppermute | solution.py:592
  66.8 17.4 %all_to_all.15 = bf16[32,16,112]{2,1,0:T(8,128)(2,1)S(1)} all-to-all(bf16[32,16,112]{2,1,0:T(8,128)(2,1)S(1)} %pair.1), channel_id=1, replica_groups=mesh['x'=4,'y'=4,'z'=8,'c'=2] {'y','z'}, dimensions={0} | all-to-all | bytes 229376 | tf_op jit(solution)/shard_map/all_to_all | solution.py:593
  (17 shorter events, 2.0 us)
Async XLA Ops:
  0.6 30.4 %collective-permute-start.3 = (bf16[8,256,512]{2,1,0:T(8,128)(2,1)}, bf16[8,256,512]{2,1,0:T(8,128)(2,1)S(1)}, u32[]{:S(2)}, u32[]{:S(2)}) collective-permute-start(bf16[8,256,512]{2,1,0:T(8,128)(2,1)} %refs_5_.1), channel_id=1, source_target_pairs={{0,1},{1,0},{2,3},{3,2},{4,5},{5,4},{6,7},{7,6},{8,9},{9,8},{10,11... | collective-permute-start | bytes 6291464 | tf_op jit(solution)/shard_map/ppermute | solution.py:566
  5.4 15.7 %all-to-all-start = ((bf16[8,16,640]{2,1,0:T(8,128)(2,1)}), bf16[8,16,640]{2,1,0:T(8,128)(2,1)S(1)}, u32[]{:S(2)}, u32[]{:S(2)}) async-start(bf16[8,16,640]{2,1,0:T(8,128)(2,1)} %payload.1), calls=%async_computation | async-start | bytes 327680 | tf_op jit(solution)/shard_map/all_to_all | solution.py:560
  11.9 14.2 %collective-permute-start.4 = (bf16[8,64,256]{2,1,0:T(8,128)(2,1)}, bf16[8,64,256]{2,1,0:T(8,128)(2,1)S(1)}, u32[]{:S(2)}, u32[]{:S(2)}) collective-permute-start(bf16[8,64,256]{2,1,0:T(8,128)(2,1)} %refs_7_.1), channel_id=1, source_target_pairs={{0,1},{1,0},{2,3},{3,2},{4,5},{5,4},{6,7},{7,6},{8,9},{9,8},{10,11... | collective-permute-start | bytes 786440 | tf_op jit(solution)/shard_map/ppermute | solution.py:565
  21.1 5.4 %collective-permute-start = (bf16[8,16,640]{2,1,0:T(8,128)(2,1)S(1)}, bf16[8,16,640]{2,1,0:T(8,128)(2,1)S(1)}, u32[]{:S(2)}, u32[]{:S(2)}) collective-permute-start(bf16[8,16,640]{2,1,0:T(8,128)(2,1)S(1)} %all-to-all-done.refs_1_), channel_id=1, source_target_pairs={{0,16},{16,32},{32,48},{48,0},{1,17},{17,33},{33,49},{49,1},{2,18}... | collective-permute-start | bytes 491528 | tf_op jit(solution)/shard_map/ppermute | solution.py:562
  22.4 8.6 %collective-permute-start.1 = (bf16[8,16,640]{2,1,0:T(8,128)(2,1)S(1)}, bf16[8,16,640]{2,1,0:T(8,128)(2,1)S(1)}, u32[]{:S(2)}, u32[]{:S(2)}) collective-permute-start(bf16[8,16,640]{2,1,0:T(8,128)(2,1)S(1)} %all-to-all-done.refs_1_), channel_id=1, source_target_pairs={{0,32},{16,48},{32,0},{48,16},{1,33},{17,49},{33,1},{49,17},{2,34}... | collective-permute-start | bytes 491528 | tf_op jit(solution)/shard_map/ppermute | solution.py:562
  25.0 5.9 %collective-permute-start.2 = (bf16[8,16,640]{2,1,0:T(8,128)(2,1)S(1)}, bf16[8,16,640]{2,1,0:T(8,128)(2,1)S(1)}, u32[]{:S(2)}, u32[]{:S(2)}) collective-permute-start(bf16[8,16,640]{2,1,0:T(8,128)(2,1)S(1)} %all-to-all-done.refs_1_), channel_id=1, source_target_pairs={{0,48},{16,0},{32,16},{48,32},{1,49},{17,1},{33,17},{49,33},{2,50}... | collective-permute-start | bytes 491528 | tf_op jit(solution)/shard_map/ppermute | solution.py:562
  37.9 22.2 %all-to-all-start.1 = ((bf16[32,72,128]{2,1,0:T(8,128)(2,1)}), bf16[32,72,128]{2,1,0:T(8,128)(2,1)S(1)}, u32[]{:S(2)}, u32[]{:S(2)}) async-start(bf16[32,72,128]{2,1,0:T(8,128)(2,1)} %get-tuple-element.17.after), calls=%async_computation.1 | async-start | bytes 1179648 | tf_op jit(solution)/shard_map/all_to_all | solution.py:581
  43.2 7.5 %collective-permute-start.5 = (bf16[4,3584]{1,0:T(4,128)(2,1)S(1)}, bf16[4,3584]{1,0:T(4,128)(2,1)S(1)}, u32[]{:S(2)}, u32[]{:S(2)}) collective-permute-start(bf16[4,3584]{1,0:T(4,128)(2,1)S(1)} %get-tuple-element.20), channel_id=1, source_target_pairs={{0,64},{64,128},{128,192},{192,0},{1,65},{65,129},{129,193},{193,1... | collective-permute-start | bytes 86024 | tf_op jit(solution)/shard_map/ppermute | solution.py:554
  44.5 6.3 %collective-permute-start.6 = (bf16[4,3584]{1,0:T(4,128)(2,1)S(1)}, bf16[4,3584]{1,0:T(4,128)(2,1)S(1)}, u32[]{:S(2)}, u32[]{:S(2)}) collective-permute-start(bf16[4,3584]{1,0:T(4,128)(2,1)S(1)} %get-tuple-element.21), channel_id=1, source_target_pairs={{0,128},{64,192},{128,0},{192,64},{1,129},{65,193},{129,1},{193,65... | collective-permute-start | bytes 86024 | tf_op jit(solution)/shard_map/ppermute | solution.py:554
  47.0 3.8 %collective-permute-start.7 = (bf16[4,3584]{1,0:T(4,128)(2,1)S(1)}, bf16[4,3584]{1,0:T(4,128)(2,1)S(1)}, u32[]{:S(2)}, u32[]{:S(2)}) collective-permute-start(bf16[4,3584]{1,0:T(4,128)(2,1)S(1)} %get-tuple-element.22), channel_id=1, source_target_pairs={{0,192},{64,0},{128,64},{192,128},{1,193},{65,1},{129,65},{193,129... | collective-permute-start | bytes 86024 | tf_op jit(solution)/shard_map/ppermute | solution.py:554
  50.8 4.1 %collective-permute-start.8 = (bf16[16,3584]{1,0:T(8,128)(2,1)S(1)}, bf16[16,3584]{1,0:T(8,128)(2,1)S(1)}, u32[]{:S(2)}, u32[]{:S(2)}) collective-permute-start(bf16[16,3584]{1,0:T(8,128)(2,1)S(1)} %stack.1.own), channel_id=1, source_target_pairs={{0,1},{1,0},{2,3},{3,2},{4,5},{5,4},{6,7},{7,6},{8,9},{9,8},{10,11... | collective-permute-start | bytes 344072 | tf_op jit(solution)/shard_map/ppermute | solution.py:586
  56.3 6.2 %collective-permute-start.10 = (bf16[4,7168]{1,0:T(4,128)(2,1)S(1)}, bf16[4,7168]{1,0:T(4,128)(2,1)S(1)}, u32[]{:S(2)}, u32[]{:S(2)}) collective-permute-start(bf16[4,7168]{1,0:T(4,128)(2,1)S(1)} %get-tuple-element.28), channel_id=1, source_target_pairs={{0,128},{64,192},{128,0},{192,64},{1,129},{65,193},{129,1},{193,65... | collective-permute-start | bytes 172040 | tf_op jit(solution)/shard_map/ppermute | solution.py:554
  57.4 5.2 %collective-permute-start.11 = (bf16[4,7168]{1,0:T(4,128)(2,1)S(1)}, bf16[4,7168]{1,0:T(4,128)(2,1)S(1)}, u32[]{:S(2)}, u32[]{:S(2)}) collective-permute-start(bf16[4,7168]{1,0:T(4,128)(2,1)S(1)} %get-tuple-element.29), channel_id=1, source_target_pairs={{0,64},{64,128},{128,192},{192,0},{1,65},{65,129},{129,193},{193,1... | collective-permute-start | bytes 172040 | tf_op jit(solution)/shard_map/ppermute | solution.py:554
  59.1 3.5 %collective-permute-start.9 = (bf16[4,7168]{1,0:T(4,128)(2,1)S(1)}, bf16[4,7168]{1,0:T(4,128)(2,1)S(1)}, u32[]{:S(2)}, u32[]{:S(2)}) collective-permute-start(bf16[4,7168]{1,0:T(4,128)(2,1)S(1)} %get-tuple-element.27), channel_id=1, source_target_pairs={{0,192},{64,0},{128,64},{192,128},{1,193},{65,1},{129,65},{193,129... | collective-permute-start | bytes 172040 | tf_op jit(solution)/shard_map/ppermute | solution.py:554
  63.0 3.7 %collective-permute-start.12 = (bf16[32,16,112]{2,1,0:T(8,128)(2,1)S(1)}, bf16[32,16,112]{2,1,0:T(8,128)(2,1)S(1)}, u32[]{:S(2)}, u32[]{:S(2)}) collective-permute-start(bf16[32,16,112]{2,1,0:T(8,128)(2,1)S(1)} %get-tuple-element.31), channel_id=1, source_target_pairs={{0,1},{1,0},{2,3},{3,2},{4,5},{5,4},{6,7},{7,6},{8,9},{9,8},{10,11... | collective-permute-start | bytes 344072 | tf_op jit(solution)/shard_map/ppermute | solution.py:592

commit v7 on v6

--- a/solution.py
+++ b/solution.py
@@ -562,8 +562,12 @@
         lax.ppermute(near_query, "y", [(i, (i + d) % column) for i in range(column)])
         for d in range(1, column)
     ]
-    rope_far = lax.ppermute(cache_rope, "c", swap)
-    lat_far = lax.ppermute(cache_lat, "c", swap)
+    later_lat, later_rope, near_query = lax.optimization_barrier(
+        (cache_lat, cache_rope, near_query)
+    )
+    query[0] = near_query
+    lat_far = lax.ppermute(later_lat, "c", swap)
+    rope_far = lax.ppermute(later_rope, "c", swap)
     scale = (w_value.shape[2] + query_rope.shape[2]) ** (-0.5)
     part, *send, mix = attention(
         lengths,

time: 85.5 us -> 84.9 us (level)
  blocking collectives: 17.4 us -> 33.6 us
  starting transfers between devices: 34.9 us -> 26.3 us
  waiting for transfers between devices: 15.8 us -> 8.28 us
    all_to_all x0 -> x1, blocking collectives: none -> 17 us  [shards(): near_query = lax.all_to_all(sent, 'z', 0, 0, tiled=True)]
    all_to_all x1 -> x0, waiting for transfers between devices: 8.92 us -> none  [shards(): near_query = lax.all_to_all(sent, 'z', 0, 0, tiled=True)]
    all_to_all x1 -> x0, starting transfers between devices: 6.46 us -> none  [shards(): near_query = lax.all_to_all(sent, 'z', 0, 0, tiled=True)]
    all_to_all x1, starting transfers between devices: 5.29 us -> 3.91 us  [shards(): got = lax.all_to_all(part, plane, 0, 0, tiled=True)]
    ppermute x3, waiting for transfers between devices: 4.86 us -> 6.23 us  [shards(): lax.ppermute(near_query, 'y', [(i, (i + d) % column) for i in range(colum...]
    ppermute x2, starting transfers between devices: 3.62 us -> 2.58 us  [the longest x1 2.58 us: shards(): lat_far = lax.ppermute(later_lat, 'c', swap)]
  transfers between devices with their start and end apart: 15 -> 14, of which waited for: 6 -> 5; matrix products, arithmetic and copies ran while one was open for 0% -> 0% of each run, Pallas kernels for 9% -> 8%
where the time goes in v7:
time: 84.9 us; the launch traced here: 84.3 us
  blocking collectives  33.6 us (40%)
  starting transfers between devices  26.3 us (31%)
  Pallas kernels  14.7 us (17%)
  waiting for transfers between devices  8.28 us (10%)
    all_to_all x1, blocking collectives, shards(): near_query = lax.all_to_all(sent, 'z', 0, 0, tiled=True)  17 us
    all_to_all x1, blocking collectives, shards(): arrived = lax.all_to_all(terms, plane, 0, 0, tiled=True)  16.7 us
    ppermute x6, starting transfers between devices, along_x(): lax.ppermute(value, 'x', [(i, (i + shift) % group_count) for i in range(g...  8.64 us
    pallas_call x1, Pallas kernels, attention(): pl.pallas_call(lambda *refs: attention_kernel(*refs, scale=scale, units=u...  6.98 us
    ppermute x3, waiting for transfers between devices, shards(): lax.ppermute(near_query, 'y', [(i, (i + d) % column) for i in range(colum...  6.23 us
    ppermute x3, starting transfers between devices, shards(): lax.ppermute(near_query, 'y', [(i, (i + d) % column) for i in range(colum...  4.99 us
    all_to_all x1, starting transfers between devices, shards(): got = lax.all_to_all(part, plane, 0, 0, tiled=True)  3.91 us
    ppermute x1, starting transfers between devices, shards(): terms = pair(keep, lax.ppermute(give, 'c', swap))  3.52 us
  transfers between devices with their start and end apart: 14, of which 5 were waited for; matrix products, arithmetic and copies ran while one was open for 0% of the time, Pallas kernels for 8%

profile of v7, /device:TPU:1, one launch (start us, length us, event | category | flops | bytes accessed | tf_op | source)
XLA Modules:
  0.0 84.3 jit_solution(15645288693351311973)
XLA Ops:
  0.6 0.8 payload.1
  1.5 17.0 %all_to_all.15.refs_1_ = bf16[8,16,640]{2,1,0:T(8,128)(2,1)S(1)} all-to-all(bf16[8,16,640]{2,1,0:T(8,128)(2,1)S(1)} %payload.1), channel_id=1, replica_groups=mesh['x'=4,'y'=4,'z'=8,'c'=2] {'z'}, dimensions={0} | all-to-all | bytes 327680 | tf_op jit(solution)/shard_map/all_to_all | solution.py:560
  18.4 2.6 %collective-permute-start.3 = (bf16[8,256,512]{2,1,0:T(8,128)(2,1)}, bf16[8,256,512]{2,1,0:T(8,128)(2,1)S(1)}, u32[]{:S(2)}, u32[]{:S(2)}) collective-permute-start(bf16[8,256,512]{2,1,0:T(8,128)(2,1)} %refs_5_.1), channel_id=1, source_target_pairs={{0,1},{1,0},{2,3},{3,2},{4,5},{5,4},{6,7},{7,6},{8,9},{9,8},{10,11... | collective-permute-start | bytes 6291464 | tf_op jit(solution)/shard_map/ppermute | solution.py:569
  21.0 1.3 %collective-permute-start = (bf16[8,16,640]{2,1,0:T(8,128)(2,1)S(1)}, bf16[8,16,640]{2,1,0:T(8,128)(2,1)S(1)}, u32[]{:S(2)}, u32[]{:S(2)}) collective-permute-start(bf16[8,16,640]{2,1,0:T(8,128)(2,1)S(1)} %all_to_all.15.refs_1_), channel_id=1, source_target_pairs={{0,16},{16,32},{32,48},{48,0},{1,17},{17,33},{33,49},{49,1},{2,18}... | collective-permute-start | bytes 491528 | tf_op jit(solution)/shard_map/ppermute | solution.py:562
  22.3 2.6 %collective-permute-start.1 = (bf16[8,16,640]{2,1,0:T(8,128)(2,1)S(1)}, bf16[8,16,640]{2,1,0:T(8,128)(2,1)S(1)}, u32[]{:S(2)}, u32[]{:S(2)}) collective-permute-start(bf16[8,16,640]{2,1,0:T(8,128)(2,1)S(1)} %all_to_all.15.refs_1_), channel_id=1, source_target_pairs={{0,32},{16,48},{32,0},{48,16},{1,33},{17,49},{33,1},{49,17},{2,34}... | collective-permute-start | bytes 491528 | tf_op jit(solution)/shard_map/ppermute | solution.py:562
  24.9 1.1 %collective-permute-start.2 = (bf16[8,16,640]{2,1,0:T(8,128)(2,1)S(1)}, bf16[8,16,640]{2,1,0:T(8,128)(2,1)S(1)}, u32[]{:S(2)}, u32[]{:S(2)}) collective-permute-start(bf16[8,16,640]{2,1,0:T(8,128)(2,1)S(1)} %all_to_all.15.refs_1_), channel_id=1, source_target_pairs={{0,48},{16,0},{32,16},{48,32},{1,49},{17,1},{33,17},{49,33},{2,50}... | collective-permute-start | bytes 491528 | tf_op jit(solution)/shard_map/ppermute | solution.py:562
  26.0 1.6 %collective-permute-done.refs_2_ = bf16[8,16,640]{2,1,0:T(8,128)(2,1)S(1)} collective-permute-done((bf16[8,16,640]{2,1,0:T(8,128)(2,1)S(1)}, bf16[8,16,640]{2,1,0:T(8,128)(2,1)S(1)}, u32[]{:S(2)}, u32[]{:S(2)}) %collective-permute-start) | collective-permute-done | bytes 163872 | tf_op jit(solution)/shard_map/ppermute | solution.py:562
  27.6 4.6 %collective-permute-done.1.refs_3_ = bf16[8,16,640]{2,1,0:T(8,128)(2,1)S(1)} collective-permute-done((bf16[8,16,640]{2,1,0:T(8,128)(2,1)S(1)}, bf16[8,16,640]{2,1,0:T(8,128)(2,1)S(1)}, u32[]{:S(2)}, u32[]{:S(2)}) %collective-permute-start.1) | collective-permute-done | bytes 163872 | tf_op jit(solution)/shard_map/ppermute | solution.py:562
  32.2 7.0 %attention.1 = (bf16[32,72,128]{2,1,0:T(8,128)(2,1)}, bf16[4,3584]{1,0:T(4,128)(2,1)S(1)}, bf16[4,3584]{1,0:T(4,128)(2,1)S(1)}, bf16[4,3584]{1,0:T(4,128)(2,1)S(...) custom-call(s32[8]{0:T(128)} %refs_0_.2, bf16[8,16,640]{2,1,0:T(8,128)(2,1)S(1)} %all_to_all.15.refs_1_, ...), custom_call_target="tpu_custom_call" | custom-call | flops 570425344 | bytes 6291456 | tf_op jit(solution)/shard_map/attention/pallas_call | solution.py:301
  39.2 3.9 %all-to-all-start.1 = ((bf16[32,72,128]{2,1,0:T(8,128)(2,1)}), bf16[32,72,128]{2,1,0:T(8,128)(2,1)S(1)}, u32[]{:S(2)}, u32[]{:S(2)}) async-start(bf16[32,72,128]{2,1,0:T(8,128)(2,1)} %get-tuple-element.23.after), calls=%async_computation.1 | async-start | bytes 1179648 | tf_op jit(solution)/shard_map/all_to_all | solution.py:585
  43.1 1.3 %collective-permute-start.5 = (bf16[4,3584]{1,0:T(4,128)(2,1)S(1)}, bf16[4,3584]{1,0:T(4,128)(2,1)S(1)}, u32[]{:S(2)}, u32[]{:S(2)}) collective-permute-start(bf16[4,3584]{1,0:T(4,128)(2,1)S(1)} %get-tuple-element.26), channel_id=1, source_target_pairs={{0,64},{64,128},{128,192},{192,0},{1,65},{65,129},{129,193},{193,1... | collective-permute-start | bytes 86024 | tf_op jit(solution)/shard_map/ppermute | solution.py:554
  44.4 2.4 %collective-permute-start.6 = (bf16[4,3584]{1,0:T(4,128)(2,1)S(1)}, bf16[4,3584]{1,0:T(4,128)(2,1)S(1)}, u32[]{:S(2)}, u32[]{:S(2)}) collective-permute-start(bf16[4,3584]{1,0:T(4,128)(2,1)S(1)} %get-tuple-element.27), channel_id=1, source_target_pairs={{0,128},{64,192},{128,0},{192,64},{1,129},{65,193},{129,1},{193,65... | collective-permute-start | bytes 86024 | tf_op jit(solution)/shard_map/ppermute | solution.py:554
  46.9 1.2 %collective-permute-start.7 = (bf16[4,3584]{1,0:T(4,128)(2,1)S(1)}, bf16[4,3584]{1,0:T(4,128)(2,1)S(1)}, u32[]{:S(2)}, u32[]{:S(2)}) collective-permute-start(bf16[4,3584]{1,0:T(4,128)(2,1)S(1)} %get-tuple-element.28), channel_id=1, source_target_pairs={{0,192},{64,0},{128,64},{192,128},{1,193},{65,1},{129,65},{193,129... | collective-permute-start | bytes 86024 | tf_op jit(solution)/shard_map/ppermute | solution.py:554
  48.0 2.6 %fetch.1 = (bf16[7168,128]{1,0:T(8,128)(2,1)S(1)}, bf16[7168,128]{1,0:T(8,128)(2,1)S(1)}, bf16[128,7168]{1,0:T(8,128)(2,1)S(1)}) custom-call(bf16[32,72,128]{2,1,0:T(8,128)(2,1)} %get-tuple-element.23.after, bf16[7168,128]{1,0:T(8,128)(2,1)} %refs_0_.3, bf16[7168,128]{1,0:T(8,128)(2,1)} %refs_1_.1, bf16[128,7168]{1,0:T(8,128)(2,1)} %refs_2_.1), custom_call_target="tpu_custom_call" | custom-call | bytes 5505024 | tf_op jit(solution)/shard_map/fetch/pallas_call | solution.py:53
  50.7 2.6 %collective-permute-start.8 = (bf16[16,3584]{1,0:T(8,128)(2,1)S(1)}, bf16[16,3584]{1,0:T(8,128)(2,1)S(1)}, u32[]{:S(2)}, u32[]{:S(2)}) collective-permute-start(bf16[16,3584]{1,0:T(8,128)(2,1)S(1)} %stack.1.own), channel_id=1, source_target_pairs={{0,1},{1,0},{2,3},{3,2},{4,5},{5,4},{6,7},{7,6},{8,9},{9,8},{10,11... | collective-permute-start | bytes 344072 | tf_op jit(solution)/shard_map/ppermute | solution.py:590
  53.4 1.0 %collective-permute-done.8.far = bf16[16,3584]{1,0:T(8,128)(2,1)S(1)} collective-permute-done((bf16[16,3584]{1,0:T(8,128)(2,1)S(1)}, bf16[16,3584]{1,0:T(8,128)(2,1)S(1)}, u32[]{:S(2)}, u32[]{:S(2)}) %collective-permute-start.8) | collective-permute-done | bytes 114720 | tf_op jit(solution)/shard_map/ppermute | solution.py:590
  54.3 1.4 %experts.1 = (bf16[4,7168]{1,0:T(4,128)(2,1)S(1)}, bf16[4,7168]{1,0:T(4,128)(2,1)S(1)}, bf16[4,7168]{1,0:T(4,128)(2,1)S(1)}, bf16[4,7168]{1,0:T(4,128)(2,1)S(1)}) custom-call(bf16[16,3584]{1,0:T(8,128)(2,1)S(1)} %stack.1.own, bf16[16,3584]{1,0:T(8,128)(2,1)S(1)} %collective-permute-done.8.far, bf16[7168,128]{1,0:T(8,128)(2,1)S(1)} %get-tuple-element.24.after.gate, ...), custom_call_target="tpu_custom_call" | custom-call | flops 88080384 | bytes 6291456 | tf_op jit(solution)/shard_map/experts/pallas_call | solution.py:392
  55.7 1.1 %collective-permute-start.10 = (bf16[4,7168]{1,0:T(4,128)(2,1)S(1)}, bf16[4,7168]{1,0:T(4,128)(2,1)S(1)}, u32[]{:S(2)}, u32[]{:S(2)}) collective-permute-start(bf16[4,7168]{1,0:T(4,128)(2,1)S(1)} %get-tuple-element.34), channel_id=1, source_target_pairs={{0,128},{64,192},{128,0},{192,64},{1,129},{65,193},{129,1},{193,65... | collective-permute-start | bytes 172040 | tf_op jit(solution)/shard_map/ppermute | solution.py:554
  56.8 1.7 %collective-permute-start.11 = (bf16[4,7168]{1,0:T(4,128)(2,1)S(1)}, bf16[4,7168]{1,0:T(4,128)(2,1)S(1)}, u32[]{:S(2)}, u32[]{:S(2)}) collective-permute-start(bf16[4,7168]{1,0:T(4,128)(2,1)S(1)} %get-tuple-element.35), channel_id=1, source_target_pairs={{0,64},{64,128},{128,192},{192,0},{1,65},{65,129},{129,193},{193,1... | collective-permute-start | bytes 172040 | tf_op jit(solution)/shard_map/ppermute | solution.py:554
  58.5 1.0 %collective-permute-start.9 = (bf16[4,7168]{1,0:T(4,128)(2,1)S(1)}, bf16[4,7168]{1,0:T(4,128)(2,1)S(1)}, u32[]{:S(2)}, u32[]{:S(2)}) collective-permute-start(bf16[4,7168]{1,0:T(4,128)(2,1)S(1)} %get-tuple-element.33), channel_id=1, source_target_pairs={{0,192},{64,0},{128,64},{192,128},{1,193},{65,1},{129,65},{193,129... | collective-permute-start | bytes 172040 | tf_op jit(solution)/shard_map/ppermute | solution.py:554
  59.5 2.4 %merge.1.attended = f32[8,7168]{1,0:T(8,128)S(1)} custom-call(bf16[4,7168]{1,0:T(4,128)(2,1)S(1)} %get-tuple-element.31.after.back_0, bf16[32,72,128]{2,1,0:T(8,128)(2,1)S(1)} %all-to-all-done.1.got, bf16[2,512,128]{2,1,0:T(8,128)(2,1)} %value.1, bf16[256,7168]{1,0:T(8,128)(2,1)} %project.1), custom_call_target="tpu_custom_call" | custom-call | flops 29360128 | bytes 4194304 | tf_op jit(solution)/shard_map/merge/pallas_call | solution.py:459
  62.4 3.5 %collective-permute-start.12 = (bf16[32,16,112]{2,1,0:T(8,128)(2,1)S(1)}, bf16[32,16,112]{2,1,0:T(8,128)(2,1)S(1)}, u32[]{:S(2)}, u32[]{:S(2)}) collective-permute-start(bf16[32,16,112]{2,1,0:T(8,128)(2,1)S(1)} %get-tuple-element.37), channel_id=1, source_target_pairs={{0,1},{1,0},{2,3},{3,2},{4,5},{5,4},{6,7},{7,6},{8,9},{9,8},{10,11... | collective-permute-start | bytes 344072 | tf_op jit(solution)/shard_map/ppermute | solution.py:596
  65.9 1.0 %collective-permute-done.12.taken = bf16[32,16,112]{2,1,0:T(8,128)(2,1)S(1)} collective-permute-done((bf16[32,16,112]{2,1,0:T(8,128)(2,1)S(1)}, bf16[32,16,112]{2,1,0:T(8,128)(2,1)S(1)}, u32[]{:S(2)}, u32[]{:S(2)}) %collective-permute-start.12) | collective-permute-done | bytes 114720 | tf_op jit(solution)/shard_map/ppermute | solution.py:596
  67.0 16.7 %all_to_all.16 = bf16[32,16,112]{2,1,0:T(8,128)(2,1)S(1)} all-to-all(bf16[32,16,112]{2,1,0:T(8,128)(2,1)S(1)} %pair.1), channel_id=1, replica_groups=mesh['x'=4,'y'=4,'z'=8,'c'=2] {'y','z'}, dimensions={0} | all-to-all | bytes 229376 | tf_op jit(solution)/shard_map/all_to_all | solution.py:597
  (16 shorter events, 1.2 us)
Async XLA Ops:
  18.4 13.8 %collective-permute-start.3 = (bf16[8,256,512]{2,1,0:T(8,128)(2,1)}, bf16[8,256,512]{2,1,0:T(8,128)(2,1)S(1)}, u32[]{:S(2)}, u32[]{:S(2)}) collective-permute-start(bf16[8,256,512]{2,1,0:T(8,128)(2,1)} %refs_5_.1), channel_id=1, source_target_pairs={{0,1},{1,0},{2,3},{3,2},{4,5},{5,4},{6,7},{7,6},{8,9},{9,8},{10,11... | collective-permute-start | bytes 6291464 | tf_op jit(solution)/shard_map/ppermute | solution.py:569
  21.0 11.2 %collective-permute-start.4 = (bf16[8,64,256]{2,1,0:T(8,128)(2,1)}, bf16[8,64,256]{2,1,0:T(8,128)(2,1)S(1)}, u32[]{:S(2)}, u32[]{:S(2)}) collective-permute-start(bf16[8,64,256]{2,1,0:T(8,128)(2,1)} %refs_7_.1), channel_id=1, source_target_pairs={{0,1},{1,0},{2,3},{3,2},{4,5},{5,4},{6,7},{7,6},{8,9},{9,8},{10,11... | collective-permute-start | bytes 786440 | tf_op jit(solution)/shard_map/ppermute | solution.py:570
  21.0 6.6 %collective-permute-start = (bf16[8,16,640]{2,1,0:T(8,128)(2,1)S(1)}, bf16[8,16,640]{2,1,0:T(8,128)(2,1)S(1)}, u32[]{:S(2)}, u32[]{:S(2)}) collective-permute-start(bf16[8,16,640]{2,1,0:T(8,128)(2,1)S(1)} %all_to_all.15.refs_1_), channel_id=1, source_target_pairs={{0,16},{16,32},{32,48},{48,0},{1,17},{17,33},{33,49},{49,1},{2,18}... | collective-permute-start | bytes 491528 | tf_op jit(solution)/shard_map/ppermute | solution.py:562
  22.3 9.9 %collective-permute-start.1 = (bf16[8,16,640]{2,1,0:T(8,128)(2,1)S(1)}, bf16[8,16,640]{2,1,0:T(8,128)(2,1)S(1)}, u32[]{:S(2)}, u32[]{:S(2)}) collective-permute-start(bf16[8,16,640]{2,1,0:T(8,128)(2,1)S(1)} %all_to_all.15.refs_1_), channel_id=1, source_target_pairs={{0,32},{16,48},{32,0},{48,16},{1,33},{17,49},{33,1},{49,17},{2,34}... | collective-permute-start | bytes 491528 | tf_op jit(solution)/shard_map/ppermute | solution.py:562
  24.9 7.3 %collective-permute-start.2 = (bf16[8,16,640]{2,1,0:T(8,128)(2,1)S(1)}, bf16[8,16,640]{2,1,0:T(8,128)(2,1)S(1)}, u32[]{:S(2)}, u32[]{:S(2)}) collective-permute-start(bf16[8,16,640]{2,1,0:T(8,128)(2,1)S(1)} %all_to_all.15.refs_1_), channel_id=1, source_target_pairs={{0,48},{16,0},{32,16},{48,32},{1,49},{17,1},{33,17},{49,33},{2,50}... | collective-permute-start | bytes 491528 | tf_op jit(solution)/shard_map/ppermute | solution.py:562
  39.2 20.3 %all-to-all-start.1 = ((bf16[32,72,128]{2,1,0:T(8,128)(2,1)}), bf16[32,72,128]{2,1,0:T(8,128)(2,1)S(1)}, u32[]{:S(2)}, u32[]{:S(2)}) async-start(bf16[32,72,128]{2,1,0:T(8,128)(2,1)} %get-tuple-element.23.after), calls=%async_computation.1 | async-start | bytes 1179648 | tf_op jit(solution)/shard_map/all_to_all | solution.py:585
  43.1 7.5 %collective-permute-start.5 = (bf16[4,3584]{1,0:T(4,128)(2,1)S(1)}, bf16[4,3584]{1,0:T(4,128)(2,1)S(1)}, u32[]{:S(2)}, u32[]{:S(2)}) collective-permute-start(bf16[4,3584]{1,0:T(4,128)(2,1)S(1)} %get-tuple-element.26), channel_id=1, source_target_pairs={{0,64},{64,128},{128,192},{192,0},{1,65},{65,129},{129,193},{193,1... | collective-permute-start | bytes 86024 | tf_op jit(solution)/shard_map/ppermute | solution.py:554
  44.4 6.3 %collective-permute-start.6 = (bf16[4,3584]{1,0:T(4,128)(2,1)S(1)}, bf16[4,3584]{1,0:T(4,128)(2,1)S(1)}, u32[]{:S(2)}, u32[]{:S(2)}) collective-permute-start(bf16[4,3584]{1,0:T(4,128)(2,1)S(1)} %get-tuple-element.27), channel_id=1, source_target_pairs={{0,128},{64,192},{128,0},{192,64},{1,129},{65,193},{129,1},{193,65... | collective-permute-start | bytes 86024 | tf_op jit(solution)/shard_map/ppermute | solution.py:554
  46.9 3.8 %collective-permute-start.7 = (bf16[4,3584]{1,0:T(4,128)(2,1)S(1)}, bf16[4,3584]{1,0:T(4,128)(2,1)S(1)}, u32[]{:S(2)}, u32[]{:S(2)}) collective-permute-start(bf16[4,3584]{1,0:T(4,128)(2,1)S(1)} %get-tuple-element.28), channel_id=1, source_target_pairs={{0,192},{64,0},{128,64},{192,128},{1,193},{65,1},{129,65},{193,129... | collective-permute-start | bytes 86024 | tf_op jit(solution)/shard_map/ppermute | solution.py:554
  50.7 3.6 %collective-permute-start.8 = (bf16[16,3584]{1,0:T(8,128)(2,1)S(1)}, bf16[16,3584]{1,0:T(8,128)(2,1)S(1)}, u32[]{:S(2)}, u32[]{:S(2)}) collective-permute-start(bf16[16,3584]{1,0:T(8,128)(2,1)S(1)} %stack.1.own), channel_id=1, source_target_pairs={{0,1},{1,0},{2,3},{3,2},{4,5},{5,4},{6,7},{7,6},{8,9},{9,8},{10,11... | collective-permute-start | bytes 344072 | tf_op jit(solution)/shard_map/ppermute | solution.py:590
  55.7 6.2 %collective-permute-start.10 = (bf16[4,7168]{1,0:T(4,128)(2,1)S(1)}, bf16[4,7168]{1,0:T(4,128)(2,1)S(1)}, u32[]{:S(2)}, u32[]{:S(2)}) collective-permute-start(bf16[4,7168]{1,0:T(4,128)(2,1)S(1)} %get-tuple-element.34), channel_id=1, source_target_pairs={{0,128},{64,192},{128,0},{192,64},{1,129},{65,193},{129,1},{193,65... | collective-permute-start | bytes 172040 | tf_op jit(solution)/shard_map/ppermute | solution.py:554
  56.8 5.2 %collective-permute-start.11 = (bf16[4,7168]{1,0:T(4,128)(2,1)S(1)}, bf16[4,7168]{1,0:T(4,128)(2,1)S(1)}, u32[]{:S(2)}, u32[]{:S(2)}) collective-permute-start(bf16[4,7168]{1,0:T(4,128)(2,1)S(1)} %get-tuple-element.35), channel_id=1, source_target_pairs={{0,64},{64,128},{128,192},{192,0},{1,65},{65,129},{129,193},{193,1... | collective-permute-start | bytes 172040 | tf_op jit(solution)/shard_map/ppermute | solution.py:554
  58.5 3.5 %collective-permute-start.9 = (bf16[4,7168]{1,0:T(4,128)(2,1)S(1)}, bf16[4,7168]{1,0:T(4,128)(2,1)S(1)}, u32[]{:S(2)}, u32[]{:S(2)}) collective-permute-start(bf16[4,7168]{1,0:T(4,128)(2,1)S(1)} %get-tuple-element.33), channel_id=1, source_target_pairs={{0,192},{64,0},{128,64},{192,128},{1,193},{65,1},{129,65},{193,129... | collective-permute-start | bytes 172040 | tf_op jit(solution)/shard_map/ppermute | solution.py:554
  62.4 4.5 %collective-permute-start.12 = (bf16[32,16,112]{2,1,0:T(8,128)(2,1)S(1)}, bf16[32,16,112]{2,1,0:T(8,128)(2,1)S(1)}, u32[]{:S(2)}, u32[]{:S(2)}) collective-permute-start(bf16[32,16,112]{2,1,0:T(8,128)(2,1)S(1)} %get-tuple-element.37), channel_id=1, source_target_pairs={{0,1},{1,0},{2,3},{3,2},{4,5},{5,4},{6,7},{7,6},{8,9},{9,8},{10,11... | collective-permute-start | bytes 344072 | tf_op jit(solution)/shard_map/ppermute | solution.py:596

commit v8 on v7

--- a/solution.py
+++ b/solution.py
@@ -284,12 +284,12 @@
 
     for tile in range(tiles):
         out[:, tile * chunk : (tile + 1) * chunk, :] = (
-            out_rows[tile].reshape(peers, chunk, LANES).astype(BF16)
+            out_rows[tile, : peers * chunk].reshape(peers, chunk, LANES).astype(BF16)
         )
     stat_rows[...] = jnp.zeros_like(stat_rows)
     for head in range(heads):
         stat_rows[pl.ds(head, peers, stride=ROWS), :] = stats[peers * head : peers * (head + 1)]
-    out[:, tiles * chunk :, :] = stat_rows[...].reshape(peers, ROWS, LANES).astype(BF16)
+    out[:, tiles * chunk :, :] = stat_rows[: peers * ROWS].reshape(peers, ROWS, LANES).astype(BF16)
 
 
 def attention(lengths, query, lat_own, lat_far, rope_own, rope_far, ids, route, scale, span, units):
@@ -306,9 +306,9 @@
         in_specs=[HBM] + [VMEM] * 4 + [HBM, VMEM, HBM, VMEM, HBM, HBM],
         out_specs=[VMEM] * 6,
         scratch_shapes=[
-            pltpu.VMEM((width // LANES, peers * chunk, LANES), F32),
-            pltpu.VMEM((tiles, peers * chunk, LANES), F32),
-            pltpu.VMEM((peers * ROWS, LANES), F32),
+            pltpu.VMEM((width // LANES, (peers + 1) * chunk, LANES), F32),
+            pltpu.VMEM((tiles, (peers + 1) * chunk, LANES), F32),
+            pltpu.VMEM(((peers + 1) * ROWS, LANES), F32),
             pltpu.VMEM((requests, peers * span), F32),
             pltpu.SMEM(lengths.shape, jnp.int32),
             pltpu.VMEM(lat_own.shape, BF16),

time: 84.9 us -> 84.9 us (level)
  no operation moved by 1% of the time
where the time goes in v8:
time: 84.9 us; the launch traced here: 84.3 us
  blocking collectives  33.6 us (40%)
  starting transfers between devices  26.2 us (31%)
  Pallas kernels  14.8 us (17%)
  waiting for transfers between devices  8.29 us (10%)
    all_to_all x1, blocking collectives, shards(): near_query = lax.all_to_all(sent, 'z', 0, 0, tiled=True)  17 us
    all_to_all x1, blocking collectives, shards(): arrived = lax.all_to_all(terms, plane, 0, 0, tiled=True)  16.7 us
    ppermute x6, starting transfers between devices, along_x(): lax.ppermute(value, 'x', [(i, (i + shift) % group_count) for i in range(g...  8.64 us
    pallas_call x1, Pallas kernels, attention(): pl.pallas_call(lambda *refs: attention_kernel(*refs, scale=scale, units=u...  7.01 us
    ppermute x3, waiting for transfers between devices, shards(): lax.ppermute(near_query, 'y', [(i, (i + d) % column) for i in range(colum...  6.23 us
    ppermute x3, starting transfers between devices, shards(): lax.ppermute(near_query, 'y', [(i, (i + d) % column) for i in range(colum...  4.99 us
    all_to_all x1, starting transfers between devices, shards(): got = lax.all_to_all(part, plane, 0, 0, tiled=True)  3.91 us
    ppermute x1, starting transfers between devices, shards(): terms = pair(keep, lax.ppermute(give, 'c', swap))  3.51 us
  transfers between devices with their start and end apart: 14, of which 5 were waited for; matrix products, arithmetic and copies ran while one was open for 0% of the time, Pallas kernels for 8%

profile of v8, /device:TPU:1, one launch (start us, length us, event | category | flops | bytes accessed | tf_op | source)
XLA Modules:
  0.0 84.3 jit_solution(2352800879003149055)
XLA Ops:
  0.6 0.8 payload.1
  1.5 17.0 %all_to_all.15.refs_1_ = bf16[8,16,640]{2,1,0:T(8,128)(2,1)S(1)} all-to-all(bf16[8,16,640]{2,1,0:T(8,128)(2,1)S(1)} %payload.1), channel_id=1, replica_groups=mesh['x'=4,'y'=4,'z'=8,'c'=2] {'z'}, dimensions={0} | all-to-all | bytes 327680 | tf_op jit(solution)/shard_map/all_to_all | solution.py:560
  18.4 2.6 %collective-permute-start.3 = (bf16[8,256,512]{2,1,0:T(8,128)(2,1)}, bf16[8,256,512]{2,1,0:T(8,128)(2,1)S(1)}, u32[]{:S(2)}, u32[]{:S(2)}) collective-permute-start(bf16[8,256,512]{2,1,0:T(8,128)(2,1)} %refs_5_.1), channel_id=1, source_target_pairs={{0,1},{1,0},{2,3},{3,2},{4,5},{5,4},{6,7},{7,6},{8,9},{9,8},{10,11... | collective-permute-start | bytes 6291464 | tf_op jit(solution)/shard_map/ppermute | solution.py:569
  21.0 1.3 %collective-permute-start = (bf16[8,16,640]{2,1,0:T(8,128)(2,1)S(1)}, bf16[8,16,640]{2,1,0:T(8,128)(2,1)S(1)}, u32[]{:S(2)}, u32[]{:S(2)}) collective-permute-start(bf16[8,16,640]{2,1,0:T(8,128)(2,1)S(1)} %all_to_all.15.refs_1_), channel_id=1, source_target_pairs={{0,16},{16,32},{32,48},{48,0},{1,17},{17,33},{33,49},{49,1},{2,18}... | collective-permute-start | bytes 491528 | tf_op jit(solution)/shard_map/ppermute | solution.py:562
  22.3 2.6 %collective-permute-start.1 = (bf16[8,16,640]{2,1,0:T(8,128)(2,1)S(1)}, bf16[8,16,640]{2,1,0:T(8,128)(2,1)S(1)}, u32[]{:S(2)}, u32[]{:S(2)}) collective-permute-start(bf16[8,16,640]{2,1,0:T(8,128)(2,1)S(1)} %all_to_all.15.refs_1_), channel_id=1, source_target_pairs={{0,32},{16,48},{32,0},{48,16},{1,33},{17,49},{33,1},{49,17},{2,34}... | collective-permute-start | bytes 491528 | tf_op jit(solution)/shard_map/ppermute | solution.py:562
  24.9 1.1 %collective-permute-start.2 = (bf16[8,16,640]{2,1,0:T(8,128)(2,1)S(1)}, bf16[8,16,640]{2,1,0:T(8,128)(2,1)S(1)}, u32[]{:S(2)}, u32[]{:S(2)}) collective-permute-start(bf16[8,16,640]{2,1,0:T(8,128)(2,1)S(1)} %all_to_all.15.refs_1_), channel_id=1, source_target_pairs={{0,48},{16,0},{32,16},{48,32},{1,49},{17,1},{33,17},{49,33},{2,50}... | collective-permute-start | bytes 491528 | tf_op jit(solution)/shard_map/ppermute | solution.py:562
  26.0 1.6 %collective-permute-done.refs_2_ = bf16[8,16,640]{2,1,0:T(8,128)(2,1)S(1)} collective-permute-done((bf16[8,16,640]{2,1,0:T(8,128)(2,1)S(1)}, bf16[8,16,640]{2,1,0:T(8,128)(2,1)S(1)}, u32[]{:S(2)}, u32[]{:S(2)}) %collective-permute-start) | collective-permute-done | bytes 163872 | tf_op jit(solution)/shard_map/ppermute | solution.py:562
  27.6 4.6 %collective-permute-done.1.refs_3_ = bf16[8,16,640]{2,1,0:T(8,128)(2,1)S(1)} collective-permute-done((bf16[8,16,640]{2,1,0:T(8,128)(2,1)S(1)}, bf16[8,16,640]{2,1,0:T(8,128)(2,1)S(1)}, u32[]{:S(2)}, u32[]{:S(2)}) %collective-permute-start.1) | collective-permute-done | bytes 163872 | tf_op jit(solution)/shard_map/ppermute | solution.py:562
  32.2 7.0 %attention.1 = (bf16[32,72,128]{2,1,0:T(8,128)(2,1)}, bf16[4,3584]{1,0:T(4,128)(2,1)S(1)}, bf16[4,3584]{1,0:T(4,128)(2,1)S(1)}, bf16[4,3584]{1,0:T(4,128)(2,1)S(...) custom-call(s32[8]{0:T(128)} %refs_0_.2, bf16[8,16,640]{2,1,0:T(8,128)(2,1)S(1)} %all_to_all.15.refs_1_, ...), custom_call_target="tpu_custom_call" | custom-call | flops 570425344 | bytes 6291456 | tf_op jit(solution)/shard_map/attention/pallas_call | solution.py:301
  39.2 3.9 %all-to-all-start.1 = ((bf16[32,72,128]{2,1,0:T(8,128)(2,1)}), bf16[32,72,128]{2,1,0:T(8,128)(2,1)S(1)}, u32[]{:S(2)}, u32[]{:S(2)}) async-start(bf16[32,72,128]{2,1,0:T(8,128)(2,1)} %get-tuple-element.23.after), calls=%async_computation.1 | async-start | bytes 1179648 | tf_op jit(solution)/shard_map/all_to_all | solution.py:585
  43.2 1.3 %collective-permute-start.5 = (bf16[4,3584]{1,0:T(4,128)(2,1)S(1)}, bf16[4,3584]{1,0:T(4,128)(2,1)S(1)}, u32[]{:S(2)}, u32[]{:S(2)}) collective-permute-start(bf16[4,3584]{1,0:T(4,128)(2,1)S(1)} %get-tuple-element.26), channel_id=1, source_target_pairs={{0,64},{64,128},{128,192},{192,0},{1,65},{65,129},{129,193},{193,1... | collective-permute-start | bytes 86024 | tf_op jit(solution)/shard_map/ppermute | solution.py:554
  44.5 2.5 %collective-permute-start.6 = (bf16[4,3584]{1,0:T(4,128)(2,1)S(1)}, bf16[4,3584]{1,0:T(4,128)(2,1)S(1)}, u32[]{:S(2)}, u32[]{:S(2)}) collective-permute-start(bf16[4,3584]{1,0:T(4,128)(2,1)S(1)} %get-tuple-element.27), channel_id=1, source_target_pairs={{0,128},{64,192},{128,0},{192,64},{1,129},{65,193},{129,1},{193,65... | collective-permute-start | bytes 86024 | tf_op jit(solution)/shard_map/ppermute | solution.py:554
  46.9 1.1 %collective-permute-start.7 = (bf16[4,3584]{1,0:T(4,128)(2,1)S(1)}, bf16[4,3584]{1,0:T(4,128)(2,1)S(1)}, u32[]{:S(2)}, u32[]{:S(2)}) collective-permute-start(bf16[4,3584]{1,0:T(4,128)(2,1)S(1)} %get-tuple-element.28), channel_id=1, source_target_pairs={{0,192},{64,0},{128,64},{192,128},{1,193},{65,1},{129,65},{193,129... | collective-permute-start | bytes 86024 | tf_op jit(solution)/shard_map/ppermute | solution.py:554
  48.1 2.6 %fetch.1 = (bf16[7168,128]{1,0:T(8,128)(2,1)S(1)}, bf16[7168,128]{1,0:T(8,128)(2,1)S(1)}, bf16[128,7168]{1,0:T(8,128)(2,1)S(1)}) custom-call(bf16[32,72,128]{2,1,0:T(8,128)(2,1)} %get-tuple-element.23.after, bf16[7168,128]{1,0:T(8,128)(2,1)} %refs_0_.3, bf16[7168,128]{1,0:T(8,128)(2,1)} %refs_1_.1, bf16[128,7168]{1,0:T(8,128)(2,1)} %refs_2_.1), custom_call_target="tpu_custom_call" | custom-call | bytes 5505024 | tf_op jit(solution)/shard_map/fetch/pallas_call | solution.py:53
  50.8 2.6 %collective-permute-start.8 = (bf16[16,3584]{1,0:T(8,128)(2,1)S(1)}, bf16[16,3584]{1,0:T(8,128)(2,1)S(1)}, u32[]{:S(2)}, u32[]{:S(2)}) collective-permute-start(bf16[16,3584]{1,0:T(8,128)(2,1)S(1)} %stack.1.own), channel_id=1, source_target_pairs={{0,1},{1,0},{2,3},{3,2},{4,5},{5,4},{6,7},{7,6},{8,9},{9,8},{10,11... | collective-permute-start | bytes 344072 | tf_op jit(solution)/shard_map/ppermute | solution.py:590
  53.4 1.0 %collective-permute-done.8.far = bf16[16,3584]{1,0:T(8,128)(2,1)S(1)} collective-permute-done((bf16[16,3584]{1,0:T(8,128)(2,1)S(1)}, bf16[16,3584]{1,0:T(8,128)(2,1)S(1)}, u32[]{:S(2)}, u32[]{:S(2)}) %collective-permute-start.8) | collective-permute-done | bytes 114720 | tf_op jit(solution)/shard_map/ppermute | solution.py:590
  54.4 1.4 %experts.1 = (bf16[4,7168]{1,0:T(4,128)(2,1)S(1)}, bf16[4,7168]{1,0:T(4,128)(2,1)S(1)}, bf16[4,7168]{1,0:T(4,128)(2,1)S(1)}, bf16[4,7168]{1,0:T(4,128)(2,1)S(1)}) custom-call(bf16[16,3584]{1,0:T(8,128)(2,1)S(1)} %stack.1.own, bf16[16,3584]{1,0:T(8,128)(2,1)S(1)} %collective-permute-done.8.far, bf16[7168,128]{1,0:T(8,128)(2,1)S(1)} %get-tuple-element.24.after.gate, ...), custom_call_target="tpu_custom_call" | custom-call | flops 88080384 | bytes 6291456 | tf_op jit(solution)/shard_map/experts/pallas_call | solution.py:392
  55.8 1.1 %collective-permute-start.10 = (bf16[4,7168]{1,0:T(4,128)(2,1)S(1)}, bf16[4,7168]{1,0:T(4,128)(2,1)S(1)}, u32[]{:S(2)}, u32[]{:S(2)}) collective-permute-start(bf16[4,7168]{1,0:T(4,128)(2,1)S(1)} %get-tuple-element.34), channel_id=1, source_target_pairs={{0,128},{64,192},{128,0},{192,64},{1,129},{65,193},{129,1},{193,65... | collective-permute-start | bytes 172040 | tf_op jit(solution)/shard_map/ppermute | solution.py:554
  56.8 1.7 %collective-permute-start.11 = (bf16[4,7168]{1,0:T(4,128)(2,1)S(1)}, bf16[4,7168]{1,0:T(4,128)(2,1)S(1)}, u32[]{:S(2)}, u32[]{:S(2)}) collective-permute-start(bf16[4,7168]{1,0:T(4,128)(2,1)S(1)} %get-tuple-element.35), channel_id=1, source_target_pairs={{0,64},{64,128},{128,192},{192,0},{1,65},{65,129},{129,193},{193,1... | collective-permute-start | bytes 172040 | tf_op jit(solution)/shard_map/ppermute | solution.py:554
  58.5 1.0 %collective-permute-start.9 = (bf16[4,7168]{1,0:T(4,128)(2,1)S(1)}, bf16[4,7168]{1,0:T(4,128)(2,1)S(1)}, u32[]{:S(2)}, u32[]{:S(2)}) collective-permute-start(bf16[4,7168]{1,0:T(4,128)(2,1)S(1)} %get-tuple-element.33), channel_id=1, source_target_pairs={{0,192},{64,0},{128,64},{192,128},{1,193},{65,1},{129,65},{193,129... | collective-permute-start | bytes 172040 | tf_op jit(solution)/shard_map/ppermute | solution.py:554
  59.5 2.4 %merge.1.attended = f32[8,7168]{1,0:T(8,128)S(1)} custom-call(bf16[4,7168]{1,0:T(4,128)(2,1)S(1)} %get-tuple-element.31.after.back_0, bf16[32,72,128]{2,1,0:T(8,128)(2,1)S(1)} %all-to-all-done.1.got, bf16[2,512,128]{2,1,0:T(8,128)(2,1)} %value.1, bf16[256,7168]{1,0:T(8,128)(2,1)} %project.1), custom_call_target="tpu_custom_call" | custom-call | flops 29360128 | bytes 4194304 | tf_op jit(solution)/shard_map/merge/pallas_call | solution.py:459
  62.5 3.5 %collective-permute-start.12 = (bf16[32,16,112]{2,1,0:T(8,128)(2,1)S(1)}, bf16[32,16,112]{2,1,0:T(8,128)(2,1)S(1)}, u32[]{:S(2)}, u32[]{:S(2)}) collective-permute-start(bf16[32,16,112]{2,1,0:T(8,128)(2,1)S(1)} %get-tuple-element.37), channel_id=1, source_target_pairs={{0,1},{1,0},{2,3},{3,2},{4,5},{5,4},{6,7},{7,6},{8,9},{9,8},{10,11... | collective-permute-start | bytes 344072 | tf_op jit(solution)/shard_map/ppermute | solution.py:596
  66.0 1.0 %collective-permute-done.12.taken = bf16[32,16,112]{2,1,0:T(8,128)(2,1)S(1)} collective-permute-done((bf16[32,16,112]{2,1,0:T(8,128)(2,1)S(1)}, bf16[32,16,112]{2,1,0:T(8,128)(2,1)S(1)}, u32[]{:S(2)}, u32[]{:S(2)}) %collective-permute-start.12) | collective-permute-done | bytes 114720 | tf_op jit(solution)/shard_map/ppermute | solution.py:596
  67.0 16.7 %all_to_all.16 = bf16[32,16,112]{2,1,0:T(8,128)(2,1)S(1)} all-to-all(bf16[32,16,112]{2,1,0:T(8,128)(2,1)S(1)} %pair.1), channel_id=1, replica_groups=mesh['x'=4,'y'=4,'z'=8,'c'=2] {'y','z'}, dimensions={0} | all-to-all | bytes 229376 | tf_op jit(solution)/shard_map/all_to_all | solution.py:597
  (16 shorter events, 1.2 us)
Async XLA Ops:
  18.4 13.8 %collective-permute-start.3 = (bf16[8,256,512]{2,1,0:T(8,128)(2,1)}, bf16[8,256,512]{2,1,0:T(8,128)(2,1)S(1)}, u32[]{:S(2)}, u32[]{:S(2)}) collective-permute-start(bf16[8,256,512]{2,1,0:T(8,128)(2,1)} %refs_5_.1), channel_id=1, source_target_pairs={{0,1},{1,0},{2,3},{3,2},{4,5},{5,4},{6,7},{7,6},{8,9},{9,8},{10,11... | collective-permute-start | bytes 6291464 | tf_op jit(solution)/shard_map/ppermute | solution.py:569
  21.0 11.2 %collective-permute-start.4 = (bf16[8,64,256]{2,1,0:T(8,128)(2,1)}, bf16[8,64,256]{2,1,0:T(8,128)(2,1)S(1)}, u32[]{:S(2)}, u32[]{:S(2)}) collective-permute-start(bf16[8,64,256]{2,1,0:T(8,128)(2,1)} %refs_7_.1), channel_id=1, source_target_pairs={{0,1},{1,0},{2,3},{3,2},{4,5},{5,4},{6,7},{7,6},{8,9},{9,8},{10,11... | collective-permute-start | bytes 786440 | tf_op jit(solution)/shard_map/ppermute | solution.py:570
  21.0 6.6 %collective-permute-start = (bf16[8,16,640]{2,1,0:T(8,128)(2,1)S(1)}, bf16[8,16,640]{2,1,0:T(8,128)(2,1)S(1)}, u32[]{:S(2)}, u32[]{:S(2)}) collective-permute-start(bf16[8,16,640]{2,1,0:T(8,128)(2,1)S(1)} %all_to_all.15.refs_1_), channel_id=1, source_target_pairs={{0,16},{16,32},{32,48},{48,0},{1,17},{17,33},{33,49},{49,1},{2,18}... | collective-permute-start | bytes 491528 | tf_op jit(solution)/shard_map/ppermute | solution.py:562
  22.3 9.9 %collective-permute-start.1 = (bf16[8,16,640]{2,1,0:T(8,128)(2,1)S(1)}, bf16[8,16,640]{2,1,0:T(8,128)(2,1)S(1)}, u32[]{:S(2)}, u32[]{:S(2)}) collective-permute-start(bf16[8,16,640]{2,1,0:T(8,128)(2,1)S(1)} %all_to_all.15.refs_1_), channel_id=1, source_target_pairs={{0,32},{16,48},{32,0},{48,16},{1,33},{17,49},{33,1},{49,17},{2,34}... | collective-permute-start | bytes 491528 | tf_op jit(solution)/shard_map/ppermute | solution.py:562
  24.9 7.3 %collective-permute-start.2 = (bf16[8,16,640]{2,1,0:T(8,128)(2,1)S(1)}, bf16[8,16,640]{2,1,0:T(8,128)(2,1)S(1)}, u32[]{:S(2)}, u32[]{:S(2)}) collective-permute-start(bf16[8,16,640]{2,1,0:T(8,128)(2,1)S(1)} %all_to_all.15.refs_1_), channel_id=1, source_target_pairs={{0,48},{16,0},{32,16},{48,32},{1,49},{17,1},{33,17},{49,33},{2,50}... | collective-permute-start | bytes 491528 | tf_op jit(solution)/shard_map/ppermute | solution.py:562
  39.2 20.3 %all-to-all-start.1 = ((bf16[32,72,128]{2,1,0:T(8,128)(2,1)}), bf16[32,72,128]{2,1,0:T(8,128)(2,1)S(1)}, u32[]{:S(2)}, u32[]{:S(2)}) async-start(bf16[32,72,128]{2,1,0:T(8,128)(2,1)} %get-tuple-element.23.after), calls=%async_computation.1 | async-start | bytes 1179648 | tf_op jit(solution)/shard_map/all_to_all | solution.py:585
  43.2 7.5 %collective-permute-start.5 = (bf16[4,3584]{1,0:T(4,128)(2,1)S(1)}, bf16[4,3584]{1,0:T(4,128)(2,1)S(1)}, u32[]{:S(2)}, u32[]{:S(2)}) collective-permute-start(bf16[4,3584]{1,0:T(4,128)(2,1)S(1)} %get-tuple-element.26), channel_id=1, source_target_pairs={{0,64},{64,128},{128,192},{192,0},{1,65},{65,129},{129,193},{193,1... | collective-permute-start | bytes 86024 | tf_op jit(solution)/shard_map/ppermute | solution.py:554
  44.5 6.3 %collective-permute-start.6 = (bf16[4,3584]{1,0:T(4,128)(2,1)S(1)}, bf16[4,3584]{1,0:T(4,128)(2,1)S(1)}, u32[]{:S(2)}, u32[]{:S(2)}) collective-permute-start(bf16[4,3584]{1,0:T(4,128)(2,1)S(1)} %get-tuple-element.27), channel_id=1, source_target_pairs={{0,128},{64,192},{128,0},{192,64},{1,129},{65,193},{129,1},{193,65... | collective-permute-start | bytes 86024 | tf_op jit(solution)/shard_map/ppermute | solution.py:554
  46.9 3.8 %collective-permute-start.7 = (bf16[4,3584]{1,0:T(4,128)(2,1)S(1)}, bf16[4,3584]{1,0:T(4,128)(2,1)S(1)}, u32[]{:S(2)}, u32[]{:S(2)}) collective-permute-start(bf16[4,3584]{1,0:T(4,128)(2,1)S(1)} %get-tuple-element.28), channel_id=1, source_target_pairs={{0,192},{64,0},{128,64},{192,128},{1,193},{65,1},{129,65},{193,129... | collective-permute-start | bytes 86024 | tf_op jit(solution)/shard_map/ppermute | solution.py:554
  50.8 3.6 %collective-permute-start.8 = (bf16[16,3584]{1,0:T(8,128)(2,1)S(1)}, bf16[16,3584]{1,0:T(8,128)(2,1)S(1)}, u32[]{:S(2)}, u32[]{:S(2)}) collective-permute-start(bf16[16,3584]{1,0:T(8,128)(2,1)S(1)} %stack.1.own), channel_id=1, source_target_pairs={{0,1},{1,0},{2,3},{3,2},{4,5},{5,4},{6,7},{7,6},{8,9},{9,8},{10,11... | collective-permute-start | bytes 344072 | tf_op jit(solution)/shard_map/ppermute | solution.py:590
  55.8 6.2 %collective-permute-start.10 = (bf16[4,7168]{1,0:T(4,128)(2,1)S(1)}, bf16[4,7168]{1,0:T(4,128)(2,1)S(1)}, u32[]{:S(2)}, u32[]{:S(2)}) collective-permute-start(bf16[4,7168]{1,0:T(4,128)(2,1)S(1)} %get-tuple-element.34), channel_id=1, source_target_pairs={{0,128},{64,192},{128,0},{192,64},{1,129},{65,193},{129,1},{193,65... | collective-permute-start | bytes 172040 | tf_op jit(solution)/shard_map/ppermute | solution.py:554
  56.8 5.2 %collective-permute-start.11 = (bf16[4,7168]{1,0:T(4,128)(2,1)S(1)}, bf16[4,7168]{1,0:T(4,128)(2,1)S(1)}, u32[]{:S(2)}, u32[]{:S(2)}) collective-permute-start(bf16[4,7168]{1,0:T(4,128)(2,1)S(1)} %get-tuple-element.35), channel_id=1, source_target_pairs={{0,64},{64,128},{128,192},{192,0},{1,65},{65,129},{129,193},{193,1... | collective-permute-start | bytes 172040 | tf_op jit(solution)/shard_map/ppermute | solution.py:554
  58.5 3.5 %collective-permute-start.9 = (bf16[4,7168]{1,0:T(4,128)(2,1)S(1)}, bf16[4,7168]{1,0:T(4,128)(2,1)S(1)}, u32[]{:S(2)}, u32[]{:S(2)}) collective-permute-start(bf16[4,7168]{1,0:T(4,128)(2,1)S(1)} %get-tuple-element.33), channel_id=1, source_target_pairs={{0,192},{64,0},{128,64},{192,128},{1,193},{65,1},{129,65},{193,129... | collective-permute-start | bytes 172040 | tf_op jit(solution)/shard_map/ppermute | solution.py:554
  62.5 4.5 %collective-permute-start.12 = (bf16[32,16,112]{2,1,0:T(8,128)(2,1)S(1)}, bf16[32,16,112]{2,1,0:T(8,128)(2,1)S(1)}, u32[]{:S(2)}, u32[]{:S(2)}) collective-permute-start(bf16[32,16,112]{2,1,0:T(8,128)(2,1)S(1)} %get-tuple-element.37), channel_id=1, source_target_pairs={{0,1},{1,0},{2,3},{3,2},{4,5},{5,4},{6,7},{7,6},{8,9},{9,8},{10,11... | collective-permute-start | bytes 344072 | tf_op jit(solution)/shard_map/ppermute | solution.py:596
